TPU v7x, 32 devices: a whole 2x2x4 slice. The times are simulated.
32 devices in a mesh: dp: 8 (over z, core), ctx: 4 (over y, x).
Axes of the slice: x: 2, y: 2, z: 4, core: 2. Of those that a mesh axis runs over, the one named last changes fastest.
Arguments:
- layer_input: bfloat16 [8192, 1536], P(('dp', 'ctx')), may hold values from -6 to 6
- cotangent: bfloat16 [8192, 1536], P(('dp', 'ctx')), may hold values from -6 to 6
- doc_lengths: int32 [8, 5], P('dp'), may hold values from 1 to 512, 1024 in all within a row
- attention_gain: bfloat16 [1536], P(('dp', 'ctx')), may hold values from 0.5 to 1.5
- query_weight: bfloat16 [1536, 1536], P(('dp', 'ctx')), may hold values from -0.15625 to 0.15625
- key_weight: bfloat16 [1536, 256], P(('dp', 'ctx')), may hold values from -0.15625 to 0.15625
- value_weight: bfloat16 [1536, 256], P(('dp', 'ctx')), may hold values from -0.15625 to 0.15625
- query_bias: bfloat16 [1536], P(('dp', 'ctx')), may hold values from -3 to 3
- key_bias: bfloat16 [256], P(('dp', 'ctx')), may hold values from -3 to 3
- value_bias: bfloat16 [256], P(('dp', 'ctx')), may hold values from -3 to 3
- output_weight: bfloat16 [1536, 1536], P(('dp', 'ctx')), may hold values from -0.625 to 0.625
- feedforward_gain: bfloat16 [1536], P(('dp', 'ctx')), may hold values from 0.5 to 1.5
- gate_weight: bfloat16 [1536, 8960], P(('dp', 'ctx')), may hold values from -0.15625 to 0.15625
- up_weight: bfloat16 [1536, 8960], P(('dp', 'ctx')), may hold values from -0.15625 to 0.15625
- down_weight: bfloat16 [8960, 1536], P(('dp', 'ctx')), may hold values from -0.0625 to 0.0625
Outputs:
- layer_output: bfloat16 [8192, 1536], P(('dp', 'ctx'))
- input_grad: float32 [8192, 1536], P(('dp', 'ctx'))
- attention_gain_grad: float32 [1536], P(('dp', 'ctx'))
- query_weight_grad: float32 [1536, 1536], P(('dp', 'ctx'))
- key_weight_grad: float32 [1536, 256], P(('dp', 'ctx'))
- value_weight_grad: float32 [1536, 256], P(('dp', 'ctx'))
- query_bias_grad: float32 [1536], P(('dp', 'ctx'))
- key_bias_grad: float32 [256], P(('dp', 'ctx'))
- value_bias_grad: float32 [256], P(('dp', 'ctx'))
- output_weight_grad: float32 [1536, 1536], P(('dp', 'ctx'))
- feedforward_gain_grad: float32 [1536], P(('dp', 'ctx'))
- gate_weight_grad: float32 [1536, 8960], P(('dp', 'ctx'))
- up_weight_grad: float32 [1536, 8960], P(('dp', 'ctx'))
- down_weight_grad: float32 [8960, 1536], P(('dp', 'ctx'))
Inputs may be any that keep to these rules, and one draw needn't show every extreme that they name: `doc_lengths`: each row sums to 1024; its last entry counts padding tokens at the row's end; each row's largest entry is exactly 512.
All inputs are finite; a program needn't handle non-finite values.
Results may differ from a plain program's by a relative error of at most 0.024.
Values may be sent and summed in bfloat16 or wider, within the bound.
No kernel may reach another device: no remote copies, remote signals or barrier semaphores. Data moves between devices by JAX's collectives and lax.ppermute only.
A program may use at most 384 MiB of HBM per device.

v0:
```python
import jax
import jax.numpy as jnp
from jax import lax
from jax.sharding import PartitionSpec as P

D = 1536
HEADS = 12
KV_HEADS = 2
HEAD = 128
DOCS = 5


EPS = 1e-06


def turn(values, cosine, sine):
    half = values.shape[-1] // 2
    first = values[..., :half]
    second = values[..., half:]
    cosine = cosine[:, None, :]
    sine = sine[:, None, :]
    return jnp.concatenate(
        [first * cosine - second * sine, second * cosine + first * sine], axis=-1
    )


def unturn(grads, cosine, sine):
    half = grads.shape[-1] // 2
    first = grads[..., :half]
    second = grads[..., half:]
    cosine = cosine[:, None, :]
    sine = sine[:, None, :]
    return jnp.concatenate(
        [first * cosine + second * sine, second * cosine - first * sine], axis=-1
    )


def score_block(query_rot, key_all, allowed):
    tokens = query_rot.shape[0]
    grouped = query_rot.reshape(tokens, KV_HEADS, HEADS // KV_HEADS, HEAD)
    keyed = key_all.reshape(key_all.shape[0], KV_HEADS, HEAD)
    scores = jnp.einsum(
        "tkgd,skd->kgts", grouped, keyed, preferred_element_type=jnp.float32
    ) * HEAD ** (-0.5)
    return jnp.where(allowed[None, None], scores, -1e30)


def norm_back(grad_normed, hidden, inverse, gain):
    scaled = grad_normed * gain
    grad_gain = jnp.sum(grad_normed * hidden * inverse, axis=0)
    grad_hidden = inverse * scaled - hidden * inverse**3 * jnp.mean(
        scaled * hidden, axis=1, keepdims=True
    )
    return (grad_gain, grad_hidden)


def own_columns(matrix, outer, inner, which):
    width = matrix.shape[1] // (outer * inner)
    split = matrix.reshape(matrix.shape[0], outer, inner, width)
    picked = lax.dynamic_slice_in_dim(split, which, 1, 2)
    return picked.reshape(matrix.shape[0], outer * width)


def per_device(
    layer_input,
    cotangent,
    doc_lengths,
    attention_gain,
    query_weight,
    key_weight,
    value_weight,
    query_bias,
    key_bias,
    value_bias,
    output_weight,
    feedforward_gain,
    gate_weight,
    up_weight,
    down_weight,
):
    tokens = layer_input.shape[0]
    n_dp = lax.axis_size("dp")
    n_ctx = lax.axis_size("ctx")
    which = lax.axis_index("ctx")
    whole = tokens * n_ctx
    places = jnp.arange(whole, dtype=jnp.int32)
    lengths = doc_lengths[0]
    ends = jnp.cumsum(lengths)
    starts = ends - lengths
    segment = jnp.sum((places[:, None] >= ends[None, :]).astype(jnp.int32), axis=1)
    chosen = (segment[:, None] == jnp.arange(DOCS, dtype=jnp.int32)[None, :]).astype(jnp.int32)
    offsets = places - jnp.sum(chosen * starts[None, :], axis=1)
    padded = segment == DOCS - 1
    first_row = which * tokens
    mine = lax.dynamic_slice_in_dim(places, first_row, tokens)
    my_segment = lax.dynamic_slice_in_dim(segment, first_row, tokens)
    my_offsets = lax.dynamic_slice_in_dim(offsets, first_row, tokens)
    allowed = (places[None, :] <= mine[:, None]) & (segment[None, :] == my_segment[:, None])
    allowed = allowed & (jnp.logical_not(padded)[None, :] | (places[None, :] == mine[:, None]))
    freqs = 10000.0 ** (-jnp.arange(0, HEAD // 2, dtype=jnp.float32) * 2.0 / HEAD)
    angles = my_offsets.astype(jnp.float32)[:, None] * freqs[None, :]
    cosine = jnp.cos(angles)
    sine = jnp.sin(angles)
    kv_width = KV_HEADS * HEAD
    gain_a, weight_q, weight_k, weight_v, bias_q, bias_k, bias_v, weight_o = (
        lax.all_gather(attention_gain, ("dp", "ctx"), axis=0, tiled=True),
        lax.all_gather(query_weight, ("dp", "ctx"), axis=0, tiled=True),
        lax.all_gather(key_weight, ("dp", "ctx"), axis=0, tiled=True),
        lax.all_gather(value_weight, ("dp", "ctx"), axis=0, tiled=True),
        lax.all_gather(query_bias, ("dp", "ctx"), axis=0, tiled=True),
        lax.all_gather(key_bias, ("dp", "ctx"), axis=0, tiled=True),
        lax.all_gather(value_bias, ("dp", "ctx"), axis=0, tiled=True),
        lax.all_gather(output_weight, ("dp", "ctx"), axis=0, tiled=True),
    )
    hidden = layer_input.astype(jnp.float32)
    inverse = lax.rsqrt(jnp.mean(hidden * hidden, axis=1, keepdims=True) + EPS)
    normed = (hidden * inverse * gain_a.astype(jnp.float32)).astype(jnp.bfloat16)
    queries = jnp.dot(normed, weight_q, preferred_element_type=jnp.float32) + bias_q.astype(
        jnp.float32
    )
    keys = jnp.dot(normed, weight_k, preferred_element_type=jnp.float32) + bias_k.astype(
        jnp.float32
    )
    values = jnp.dot(normed, weight_v, preferred_element_type=jnp.float32) + bias_v.astype(
        jnp.float32
    )
    query_rot = turn(queries.reshape(tokens, HEADS, HEAD), cosine, sine).astype(jnp.bfloat16)
    key_rot = (
        turn(keys.reshape(tokens, KV_HEADS, HEAD), cosine, sine)
        .astype(jnp.bfloat16)
        .reshape(tokens, kv_width)
    )
    value_low = values.astype(jnp.bfloat16)
    key_all, value_all = (
        lax.all_gather(key_rot, "ctx", axis=0, tiled=True),
        lax.all_gather(value_low, "ctx", axis=0, tiled=True),
    )
    scores = score_block(query_rot, key_all, allowed)
    top = jnp.max(scores, axis=-1, keepdims=True)
    weights = jnp.exp(scores - top)
    totals = jnp.sum(weights, axis=-1, keepdims=True)
    probs = weights / totals
    log_total = top + jnp.log(totals)
    value_heads = value_all.reshape(whole, KV_HEADS, HEAD)
    mixed = jnp.einsum(
        "kgts,skd->tkgd",
        probs.astype(jnp.bfloat16),
        value_heads,
        preferred_element_type=jnp.float32,
    )
    mixed_low = mixed.reshape(tokens, D).astype(jnp.bfloat16)
    middle = hidden + jnp.dot(mixed_low, weight_o, preferred_element_type=jnp.float32)
    gain_f, weight_g, weight_u, weight_d = (
        lax.all_gather(feedforward_gain, ("dp", "ctx"), axis=0, tiled=True),
        lax.all_gather(gate_weight, ("dp", "ctx"), axis=0, tiled=True),
        lax.all_gather(up_weight, ("dp", "ctx"), axis=0, tiled=True),
        lax.all_gather(down_weight, ("dp", "ctx"), axis=0, tiled=True),
    )
    inverse2 = lax.rsqrt(jnp.mean(middle * middle, axis=1, keepdims=True) + EPS)
    normed2 = (middle * inverse2 * gain_f.astype(jnp.float32)).astype(jnp.bfloat16)
    gate = jnp.dot(normed2, weight_g, preferred_element_type=jnp.float32)
    upward = jnp.dot(normed2, weight_u, preferred_element_type=jnp.float32)
    sigmoid_gate = jax.nn.sigmoid(gate)
    active = (gate * sigmoid_gate * upward).astype(jnp.bfloat16)
    layer_output = (middle + jnp.dot(active, weight_d, preferred_element_type=jnp.float32)).astype(
        jnp.bfloat16
    )
    gain_f, weight_g, weight_u, weight_d = (
        lax.all_gather(feedforward_gain, ("dp", "ctx"), axis=0, tiled=True),
        lax.all_gather(gate_weight, ("dp", "ctx"), axis=0, tiled=True),
        lax.all_gather(up_weight, ("dp", "ctx"), axis=0, tiled=True),
        lax.all_gather(down_weight, ("dp", "ctx"), axis=0, tiled=True),
    )
    grad_active = jnp.einsum("td,fd->tf", cotangent, weight_d, preferred_element_type=jnp.float32)
    grad_gate = (grad_active * upward * sigmoid_gate * (1.0 + gate * (1.0 - sigmoid_gate))).astype(
        jnp.bfloat16
    )
    grad_upward = (grad_active * gate * sigmoid_gate).astype(jnp.bfloat16)
    grad_normed2 = jnp.einsum("tf,df->td", grad_gate, weight_g, preferred_element_type=jnp.float32)
    grad_normed2 = grad_normed2 + jnp.einsum(
        "tf,df->td", grad_upward, weight_u, preferred_element_type=jnp.float32
    )
    grad_gain_f, grad_middle = norm_back(grad_normed2, middle, inverse2, gain_f.astype(jnp.float32))
    grad_middle = grad_middle + cotangent.astype(jnp.float32)
    normed_piece = lax.all_gather(normed2, "ctx", axis=0, tiled=True)
    cotangent_piece = lax.all_gather(cotangent, "ctx", axis=0, tiled=True)
    active_piece = lax.all_gather(active, "ctx", axis=0, tiled=True)
    gate_piece = lax.all_gather(grad_gate, "ctx", axis=0, tiled=True)
    upward_piece = lax.all_gather(grad_upward, "ctx", axis=0, tiled=True)
    normed_own = own_columns(normed_piece, n_dp, n_ctx, which)
    active_own = own_columns(active_piece, n_dp, n_ctx, which)
    part_gate = jnp.einsum("td,tf->df", normed_own, gate_piece, preferred_element_type=jnp.float32)
    part_up = jnp.einsum("td,tf->df", normed_own, upward_piece, preferred_element_type=jnp.float32)
    part_down = jnp.einsum(
        "tf,td->fd", active_own, cotangent_piece, preferred_element_type=jnp.float32
    )
    feed_grads = (
        lax.psum_scatter(
            part_gate.astype(jnp.bfloat16), "dp", scatter_dimension=0, tiled=True
        ).astype(jnp.float32),
        lax.psum_scatter(
            part_up.astype(jnp.bfloat16), "dp", scatter_dimension=0, tiled=True
        ).astype(jnp.float32),
        lax.psum_scatter(
            part_down.astype(jnp.bfloat16), "dp", scatter_dimension=0, tiled=True
        ).astype(jnp.float32),
    )
    gain_a, weight_q, weight_k, weight_v, bias_q, bias_k, bias_v, weight_o = (
        lax.all_gather(attention_gain, ("dp", "ctx"), axis=0, tiled=True),
        lax.all_gather(query_weight, ("dp", "ctx"), axis=0, tiled=True),
        lax.all_gather(key_weight, ("dp", "ctx"), axis=0, tiled=True),
        lax.all_gather(value_weight, ("dp", "ctx"), axis=0, tiled=True),
        lax.all_gather(query_bias, ("dp", "ctx"), axis=0, tiled=True),
        lax.all_gather(key_bias, ("dp", "ctx"), axis=0, tiled=True),
        lax.all_gather(value_bias, ("dp", "ctx"), axis=0, tiled=True),
        lax.all_gather(output_weight, ("dp", "ctx"), axis=0, tiled=True),
    )
    grad_attention = grad_middle.astype(jnp.bfloat16)
    grad_mixed = jnp.einsum(
        "te,de->td", grad_attention, weight_o, preferred_element_type=jnp.float32
    ).astype(jnp.bfloat16)
    grad_heads = grad_mixed.reshape(tokens, KV_HEADS, HEADS // KV_HEADS, HEAD)
    scores = score_block(query_rot, key_all, allowed)
    probs = jnp.exp(scores - log_total)
    grad_probs = jnp.einsum(
        "tkgd,skd->kgts", grad_heads, value_heads, preferred_element_type=jnp.float32
    )
    grad_scores = (
        probs * (grad_probs - jnp.sum(probs * grad_probs, axis=-1, keepdims=True))
    ).astype(jnp.bfloat16)
    grad_value_part = jnp.einsum(
        "kgts,tkgd->skd", probs.astype(jnp.bfloat16), grad_heads, preferred_element_type=jnp.float32
    )
    key_heads = key_all.reshape(whole, KV_HEADS, HEAD)
    grouped = query_rot.reshape(tokens, KV_HEADS, HEADS // KV_HEADS, HEAD)
    grad_query_rot = jnp.einsum(
        "kgts,skd->tkgd", grad_scores, key_heads, preferred_element_type=jnp.float32
    ) * HEAD ** (-0.5)
    grad_key_part = jnp.einsum(
        "kgts,tkgd->skd", grad_scores, grouped, preferred_element_type=jnp.float32
    ) * HEAD ** (-0.5)
    grad_key_rot, grad_value_sum = (
        lax.psum_scatter(
            grad_key_part.reshape(whole, kv_width), "ctx", scatter_dimension=0, tiled=True
        ),
        lax.psum_scatter(
            grad_value_part.reshape(whole, kv_width), "ctx", scatter_dimension=0, tiled=True
        ),
    )
    grad_keys = (
        unturn(grad_key_rot.reshape(tokens, KV_HEADS, HEAD), cosine, sine)
        .reshape(tokens, kv_width)
        .astype(jnp.bfloat16)
    )
    grad_values = grad_value_sum.astype(jnp.bfloat16)
    grad_queries = (
        unturn(grad_query_rot.reshape(tokens, HEADS, HEAD), cosine, sine)
        .reshape(tokens, D)
        .astype(jnp.bfloat16)
    )
    grad_query_bias = jnp.sum(grad_queries.astype(jnp.float32), axis=0)
    grad_key_bias = jnp.sum(grad_keys.astype(jnp.float32), axis=0)
    grad_value_bias = jnp.sum(grad_values.astype(jnp.float32), axis=0)
    grad_normed = jnp.einsum(
        "te,de->td", grad_queries, weight_q, preferred_element_type=jnp.float32
    )
    grad_normed = grad_normed + jnp.einsum(
        "te,de->td", grad_keys, weight_k, preferred_element_type=jnp.float32
    )
    grad_normed = grad_normed + jnp.einsum(
        "te,de->td", grad_values, weight_v, preferred_element_type=jnp.float32
    )
    grad_gain_a, grad_hidden = norm_back(grad_normed, hidden, inverse, gain_a.astype(jnp.float32))
    input_grad = grad_middle + grad_hidden
    normed_piece = lax.all_gather(normed, "ctx", axis=0, tiled=True)
    query_piece = lax.all_gather(grad_queries, "ctx", axis=0, tiled=True)
    key_piece = lax.all_gather(grad_keys, "ctx", axis=0, tiled=True)
    value_piece = lax.all_gather(grad_values, "ctx", axis=0, tiled=True)
    mixed_piece = lax.all_gather(mixed_low, "ctx", axis=0, tiled=True)
    attention_piece = lax.all_gather(grad_attention, "ctx", axis=0, tiled=True)
    normed_own = own_columns(normed_piece, n_dp, n_ctx, which)
    mixed_own = own_columns(mixed_piece, n_dp, n_ctx, which)
    part_query = jnp.einsum(
        "td,te->de", normed_own, query_piece, preferred_element_type=jnp.float32
    )
    part_key = jnp.einsum("td,te->de", normed_own, key_piece, preferred_element_type=jnp.float32)
    part_value = jnp.einsum(
        "td,te->de", normed_own, value_piece, preferred_element_type=jnp.float32
    )
    part_output = jnp.einsum(
        "td,te->de", mixed_own, attention_piece, preferred_element_type=jnp.float32
    )
    attend_grads = (
        lax.psum_scatter(
            part_query.astype(jnp.bfloat16), "dp", scatter_dimension=0, tiled=True
        ).astype(jnp.float32),
        lax.psum_scatter(
            part_key.astype(jnp.bfloat16), "dp", scatter_dimension=0, tiled=True
        ).astype(jnp.float32),
        lax.psum_scatter(
            part_value.astype(jnp.bfloat16), "dp", scatter_dimension=0, tiled=True
        ).astype(jnp.float32),
        lax.psum_scatter(
            part_output.astype(jnp.bfloat16), "dp", scatter_dimension=0, tiled=True
        ).astype(jnp.float32),
    )
    small = (
        lax.psum_scatter(grad_gain_a, ("dp", "ctx"), scatter_dimension=0, tiled=True),
        lax.psum_scatter(grad_query_bias, ("dp", "ctx"), scatter_dimension=0, tiled=True),
        lax.psum_scatter(grad_key_bias, ("dp", "ctx"), scatter_dimension=0, tiled=True),
        lax.psum_scatter(grad_value_bias, ("dp", "ctx"), scatter_dimension=0, tiled=True),
        lax.psum_scatter(grad_gain_f, ("dp", "ctx"), scatter_dimension=0, tiled=True),
    )
    return (
        layer_output,
        input_grad,
        small[0],
        attend_grads[0],
        attend_grads[1],
        attend_grads[2],
        small[1],
        small[2],
        small[3],
        attend_grads[3],
        small[4],
        feed_grads[0],
        feed_grads[1],
        feed_grads[2],
    )


def solution(mesh):
    placed = (
        P(("dp", "ctx"), None),
        P(("dp", "ctx"), None),
        P("dp", None),
        P(("dp", "ctx")),
        P(("dp", "ctx"), None),
        P(("dp", "ctx"), None),
        P(("dp", "ctx"), None),
        P(("dp", "ctx")),
        P(("dp", "ctx")),
        P(("dp", "ctx")),
        P(("dp", "ctx"), None),
        P(("dp", "ctx")),
        P(("dp", "ctx"), None),
        P(("dp", "ctx"), None),
        P(("dp", "ctx"), None),
    )
    return jax.shard_map(
        per_device,
        mesh=mesh,
        in_specs=placed,
        out_specs=(
            P(("dp", "ctx"), None),
            P(("dp", "ctx"), None),
            P(("dp", "ctx")),
            P(("dp", "ctx"), None),
            P(("dp", "ctx"), None),
            P(("dp", "ctx"), None),
            P(("dp", "ctx")),
            P(("dp", "ctx")),
            P(("dp", "ctx")),
            P(("dp", "ctx"), None),
            P(("dp", "ctx")),
            P(("dp", "ctx"), None),
            P(("dp", "ctx"), None),
            P(("dp", "ctx"), None),
        ),
        check_vma=False,
    )
```

profile of v0, /device:TPU:0, one launch (start us, length us, event | category | flops | bytes accessed | tf_op | source)
XLA Modules:
  0.0 1907.8 jit_solution(2553774672615718625)
XLA Ops:
  14.9 42.6 %all-reduce.11 = (bf16[1536]{0:T(1024)(128)(2,1)S(1)}, bf16[256]{0:T(256)(128)(2,1)S(1)}, bf16[1536]{0:T(1024)(128)(2,1)S(1)}, bf16[256]{0:T(256)(128)(2,1)S(1)}, bf16[1536]{0:T(1024)(128)(2,1)S(1)}) all-reduce(bf16[1536]{0:T(1024)(128)(2,1)S(1)} %dynamic-update-slice, ...), channel_id=1, replica_groups=mesh['dp'=8,'ctx'=4] {'dp','ctx'}, use_global_device_ids=true, to_apply=%add | all-reduce | flops 5120 | bytes 20480
  62.0 72.1 %all_gather.88 = bf16[1536,256]{1,0:T(8,128)(2,1)S(1)} all-gather(bf16[48,256]{1,0:T(8,128)(2,1)S(1)} %copy-done.24), channel_id=1, replica_groups=mesh['dp'=8,'ctx'=4] {'dp','ctx'}, dimensions={0}, use_global_device_ids=true | all-gather | bytes 811008 | tf_op jit(solution)/shard_map/all_gather | solution.py:108
  136.6 11.4 all_gather.90
  148.1 74.8 %all_gather.85 = bf16[1536,256]{1,0:T(8,128)(2,1)S(1)} all-gather(bf16[48,256]{1,0:T(8,128)(2,1)S(1)} %copy-done.25), channel_id=1, replica_groups=mesh['dp'=8,'ctx'=4] {'dp','ctx'}, dimensions={0}, use_global_device_ids=true | all-gather | bytes 811008 | tf_op jit(solution)/shard_map/all_gather | solution.py:109
  224.2 9.4 all_gather.87
  235.3 4.9 convolution_add_fusion.4
  254.1 4.2 fusion.20
  258.3 4.1 multiply_reduce_fusion.2
  262.6 60.8 %all-gather.19.cloned.1.call-done = bf16[1536,8960]{1,0:T(8,128)(2,1)} async-done(((bf16[48,8960]{1,0:T(8,128)(2,1)}), bf16[1536,8960]{1,0:T(8,128)(2,1)}) %all-gather.19.cloned.1.call-update) | async-done | bytes 27525136 | tf_op jit(solution)/shard_map/all_gather | solution.py:155
  323.4 15.3 fusion.38
  338.8 151.5 %all-gather.21.cloned.1.call-done = bf16[1536,8960]{1,0:T(8,128)(2,1)} async-done(((bf16[48,8960]{1,0:T(8,128)(2,1)}), bf16[1536,8960]{1,0:T(8,128)(2,1)}) %all-gather.21.cloned.1.call-update) | async-done | bytes 27525136 | tf_op jit(solution)/shard_map/all_gather | solution.py:156
  490.3 15.1 fusion.39
  505.4 151.8 %all-gather.23.cloned.1.call-done = bf16[8960,1536]{1,0:T(8,128)(2,1)} async-done(((bf16[280,1536]{1,0:T(8,128)(2,1)}), bf16[8960,1536]{1,0:T(8,128)(2,1)}) %all-gather.23.cloned.1.call-update) | async-done | bytes 27525136 | tf_op jit(solution)/shard_map/all_gather | solution.py:157
  657.2 21.6 %multiply_convert_fusion = (bf16[256,8960]{1,0:T(8,128)(2,1)}, bf16[256,8960]{1,0:T(8,128)(2,1)}, bf16[256,8960]{1,0:T(8,128)(2,1)}) fusion(f32[256,8960]{1,0:T(8,128)} %fusion.38, f32[256,8960]{1,0:T(8,128)} %fusion.39, bf16[256,1536]{1,0:T(8,128)(2,1)S(1)} %copy-done.12, bf16[8960,1536]{1,0:T(8,128)(2,1)} %all-gather.23.cloned.1.call-done), kind=kOutput, calls=%fused_computation.14 | convolution fusion | flops 7083130880 | bytes 60424192 | tf_op jit(solution)/shard_map/td,fd->tf/dot_general | solution.py:174
  678.8 15.3 fusion.40
  694.1 14.3 multiply_reduce_fusion
  710.4 4.9 convolution_convert_fusion.5
  716.7 8.9 fusion.5
  725.6 6.7 fusion
  732.3 6.8 fusion.2
  754.9 4.7 copy.90
  762.0 18.1 all_gather.101
  780.0 5.7 reduce-scatter.10.cloned.1.call-done
  788.0 18.7 all_gather.100
  807.9 26.7 %all-gather.27.cloned.1.call-done = bf16[1024,1536]{0,1:T(8,128)(2,1)} async-done(((bf16[256,1536]{0,1:T(8,128)(2,1)}), bf16[1024,1536]{0,1:T(8,128)(2,1)}) %all-gather.27.cloned.1.call-update) | async-done | bytes 3145744 | tf_op jit(solution)/shard_map/all_gather | solution.py:276
  834.5 4.3 convolution_convert_fusion.4
  838.9 41.7 %all-gather.29.cloned.1.call-done = bf16[1024,1536]{0,1:T(8,128)(2,1)} async-done(((bf16[256,1536]{0,1:T(8,128)(2,1)}), bf16[1024,1536]{0,1:T(8,128)(2,1)}) %all-gather.29.cloned.1.call-update) | async-done | bytes 3145744 | tf_op jit(solution)/shard_map/all_gather | solution.py:279
  881.9 44.6 %all-gather.31.cloned.1.call-done = bf16[1024,1536]{1,0:T(8,128)(2,1)} async-done(((bf16[256,1536]{1,0:T(8,128)(2,1)}), bf16[1024,1536]{1,0:T(8,128)(2,1)}) %all-gather.31.cloned.1.call-update) | async-done | bytes 3145744 | tf_op jit(solution)/shard_map/all_gather | solution.py:280
  926.5 4.3 convolution_convert_fusion.3
  930.9 41.3 %all-gather.33.cloned.1.call-done = bf16[1024,1536]{1,0:T(8,128)(2,1)} async-done(((bf16[256,1536]{1,0:T(8,128)(2,1)}), bf16[1024,1536]{1,0:T(8,128)(2,1)}) %all-gather.33.cloned.1.call-update) | async-done | bytes 3145744 | tf_op jit(solution)/shard_map/all_gather | solution.py:185
  972.2 4.7 copy.91
  978.1 167.6 %all-gather.35.cloned.1.call-done = bf16[1024,8960]{1,0:T(8,128)(2,1)} async-done(((bf16[256,8960]{1,0:T(8,128)(2,1)}), bf16[1024,8960]{1,0:T(8,128)(2,1)}) %all-gather.35.cloned.1.call-update) | async-done | bytes 18350096 | tf_op jit(solution)/shard_map/all_gather | solution.py:188
  1145.8 15.4 convolution_convert_fusion.1
  1161.2 157.9 %all-gather.37.cloned.1.call-done = bf16[1024,8960]{1,0:T(8,128)(2,1)} async-done(((bf16[256,8960]{1,0:T(8,128)(2,1)}), bf16[1024,8960]{1,0:T(8,128)(2,1)}) %all-gather.37.cloned.1.call-update) | async-done | bytes 18350096 | tf_op jit(solution)/shard_map/all_gather | solution.py:189
  1319.1 15.4 convolution_convert_fusion
  1334.8 157.7 %all-gather.39.cloned.1.call-done = bf16[1024,8960]{1,0:T(8,128)(2,1)} async-done(((bf16[256,8960]{1,0:T(8,128)(2,1)}), bf16[1024,8960]{1,0:T(8,128)(2,1)}) %all-gather.39.cloned.1.call-update) | async-done | bytes 18350096 | tf_op jit(solution)/shard_map/all_gather | solution.py:187
  1492.5 24.5 %copy.92 = bf16[1024,8960]{0,1:T(8,128)(2,1)} copy(bf16[1024,8960]{1,0:T(8,128)(2,1)} %all-gather.39.cloned.1.call-done) | data formatting | bytes 36700160 | tf_op jit(solution)/shard_map/all_gather | solution.py:187
  1517.0 5.2 constant_dynamic-slice_fusion.3
  1522.2 16.0 all-gather.41.cloned.1.call-done
  1538.2 12.1 convolution_convert_fusion.2
  1551.4 3.9 fusion.41
  1555.5 13.9 fusion.10
  1572.6 39.7 %all-reduce.10 = (f32[1536]{0:T(1024)S(1)}, f32[1536]{0:T(1024)S(1)}, f32[256]{0:T(256)S(1)}, f32[256]{0:T(256)S(1)}, f32[1536]{0:T(1024)S(1)}) all-reduce(f32[1536]{0:T(1024)S(1)} %get-tuple-element.16, f32[1536]{0:T(1024)S(1)} %bitcast.168, f32[256]{0:T(256)S(1)} %bitcast.169, ...), channel_id=4, replica_groups=mesh['dp'=8,'ctx'=4] {'dp','ctx'}, use_global_device_ids=true, to_apply=%region_13.14.clone | all-reduce | flops 5120 | bytes 40960
  1621.0 15.6 reduce-scatter.14.cloned.1.call-done
  1638.2 32.0 %reduce-scatter.20.cloned.1.call-done = bf16[48,1536]{1,0:T(8,128)(2,1)} async-done(((bf16[384,1536]{1,0:T(8,128)(2,1)}), bf16[48,1536]{1,0:T(8,128)(2,1)}) %reduce-scatter.20.cloned.1.call-update) | async-done | bytes 147472 | tf_op jit(solution)/shard_map/reduce_scatter | solution.py:303
  1671.9 74.3 %reduce-scatter.22.cloned.1.call-done = bf16[48,8960]{1,0:T(8,128)(2,1)} async-done(((bf16[384,8960]{1,0:T(8,128)(2,1)}), bf16[48,8960]{1,0:T(8,128)(2,1)}) %reduce-scatter.22.cloned.1.call-update) | async-done | bytes 860176 | tf_op jit(solution)/shard_map/reduce_scatter | solution.py:198
  1748.6 73.6 %reduce-scatter.24.cloned.1.call-done = bf16[48,8960]{1,0:T(8,128)(2,1)} async-done(((bf16[384,8960]{1,0:T(8,128)(2,1)}), bf16[48,8960]{1,0:T(8,128)(2,1)}) %reduce-scatter.24.cloned.1.call-update) | async-done | bytes 860176 | tf_op jit(solution)/shard_map/reduce_scatter | solution.py:201
  1824.7 73.6 %reduce-scatter.26.cloned.1.call-done = bf16[280,1536]{1,0:T(8,128)(2,1)} async-done(((bf16[2240,1536]{1,0:T(8,128)(2,1)}), bf16[280,1536]{1,0:T(8,128)(2,1)}) %reduce-scatter.26.cloned.1.call-update) | async-done | bytes 860176 | tf_op jit(solution)/shard_map/reduce_scatter | solution.py:204
  (193 shorter events, 82.9 us)
Async XLA Ops:
  7.2 54.8 %copy-start.24 = (bf16[48,256]{1,0:T(8,128)(2,1)S(1)}, bf16[48,256]{1,0:T(8,128)(2,1)}, u32[]{:S(2)}) copy-start(bf16[48,256]{1,0:T(8,128)(2,1)} %param.20) | copy-start | bytes 73732
  7.2 126.9 %copy-start.29 = (s32[1,5]{1,0:T(1,128)S(1)}, s32[1,5]{1,0:T(1,128)}, u32[]{:S(2)}) copy-start(s32[1,5]{1,0:T(1,128)} %param.17) | copy-start | bytes 64
  7.2 228.1 %all-gather.15.cloned.1.call-start = ((), (), s32[]{:S(2)}) async-start(), calls=%async_computation.9 | async-start | bytes 4866048 | tf_op jit(solution)/shard_map/all_gather | solution.py:107
  7.9 250.4 %all-gather.17.cloned.1.call-start = ((), (), s32[]{:S(2)}) async-start(), calls=%async_computation.10 | async-start | bytes 4866048 | tf_op jit(solution)/shard_map/all_gather | solution.py:113
  8.7 314.7 %all-gather.19.cloned.1.call-start = ((), (), s32[]{:S(2)}) async-start(), calls=%async_computation.11 | async-start | bytes 28385280 | tf_op jit(solution)/shard_map/all_gather | solution.py:155
  9.4 138.7 %copy-start.25 = (bf16[48,256]{1,0:T(8,128)(2,1)S(1)}, bf16[48,256]{1,0:T(8,128)(2,1)}, u32[]{:S(2)}) copy-start(bf16[48,256]{1,0:T(8,128)(2,1)} %param.21) | copy-start | bytes 73732
  9.4 480.9 %all-gather.21.cloned.1.call-start = ((), (), s32[]{:S(2)}) async-start(), calls=%async_computation.12 | async-start | bytes 28385280 | tf_op jit(solution)/shard_map/all_gather | solution.py:156
  10.0 647.2 %all-gather.23.cloned.1.call-start = ((), (), s32[]{:S(2)}) async-start(), calls=%async_computation.13 | async-start | bytes 28385280 | tf_op jit(solution)/shard_map/all_gather | solution.py:157
  10.6 744.3 %all-gather.25.cloned.1.call-start = ((), (), s32[]{:S(2)}) async-start(), calls=%async_computation.16 | async-start | bytes 3932160 | tf_op jit(solution)/shard_map/all_gather | solution.py:275
  59.6 75.0 %copy-start.26 = (f32[256]{0:T(256)}, f32[256]{0:T(256)S(1)}, u32[]{:S(2)}) copy-start(f32[256]{0:T(256)S(1)} %get-tuple-element.50) | copy-start | bytes 3076
  61.8 161.9 %copy-start.6 = (bf16[256,1536]{1,0:T(8,128)(2,1)S(1)}, bf16[256,1536]{1,0:T(8,128)(2,1)}, u32[]{:S(2)}) copy-start(bf16[256,1536]{1,0:T(8,128)(2,1)} %fusion.13) | copy-start | bytes 2359300
  61.9 699.0 %reduce-scatter.12.cloned.1.call-start = ((), (), s32[]{:S(2)}) async-start(), calls=%async_computation.15 | async-start | bytes 1310720 | tf_op jit(solution)/shard_map/reduce_scatter | solution.py:246
  134.1 106.1 %copy-start.7 = (bf16[1536,256]{1,0:T(8,128)(2,1)}, bf16[1536,256]{1,0:T(8,128)(2,1)S(1)}, u32[]{:S(2)}) copy-start(bf16[1536,256]{1,0:T(8,128)(2,1)S(1)} %all_gather.88) | copy-start | bytes 2359300
  136.5 107.2 %copy-start.18 = (f32[256,64]{0,1:T(8,128)}, f32[256,64]{0,1:T(8,128)S(1)}, u32[]{:S(2)}) copy-start(f32[256,64]{0,1:T(8,128)S(1)} %get-tuple-element.47) | copy-start | bytes 196612
  136.5 107.2 %copy-start.20 = (f32[256,64]{0,1:T(8,128)}, f32[256,64]{0,1:T(8,128)S(1)}, u32[]{:S(2)}) copy-start(f32[256,64]{0,1:T(8,128)S(1)} %get-tuple-element.48) | copy-start | bytes 196612
  148.0 98.5 %copy-start.10 = (bf16[1024,256]{0,1:T(8,128)(2,1)}, bf16[1024,256]{0,1:T(8,128)(2,1)S(1)}, u32[]{:S(2)}) copy-start(bf16[1024,256]{0,1:T(8,128)(2,1)S(1)} %all_gather.90) | copy-start | bytes 1572868
  249.5 4.5 copy-start
  249.5 4.5 copy-start.17
  254.1 4.2 copy-start.2
  262.6 60.8 %copy-start.14 = (bf16[256,1536]{1,0:T(8,128)(2,1)}, bf16[256,1536]{1,0:T(8,128)(2,1)S(1)}, u32[]{:S(2)}) copy-start(bf16[256,1536]{1,0:T(8,128)(2,1)S(1)} %multiply_convert_fusion.3) | copy-start | bytes 2359300
  338.8 318.4 %copy-start.12 = (bf16[256,1536]{1,0:T(8,128)(2,1)S(1)}, bf16[256,1536]{1,0:T(8,128)(2,1)}, u32[]{:S(2)}) copy-start(bf16[256,1536]{1,0:T(8,128)(2,1)} %param.16) | copy-start | bytes 2359300
  725.5 60.2 %reduce-scatter.10.cloned.1.call-start = ((), (), s32[]{:S(2)}) async-start(), calls=%async_computation.14 | async-start | bytes 1310720 | tf_op jit(solution)/shard_map/reduce_scatter | solution.py:243
  732.3 9.5 copy-start.5
  741.8 3.5 copy-start.11
  745.2 3.9 copy-start.19
  745.2 3.9 copy-start.21
  745.2 89.3 %all-gather.27.cloned.1.call-start = ((), (), s32[]{:S(2)}) async-start(), calls=%async_computation.17 | async-start | bytes 3932160 | tf_op jit(solution)/shard_map/all_gather | solution.py:276
  750.5 130.2 %all-gather.29.cloned.1.call-start = ((), (), s32[]{:S(2)}) async-start(), calls=%async_computation.21 | async-start | bytes 3932160 | tf_op jit(solution)/shard_map/all_gather | solution.py:279
  751.1 175.5 %all-gather.31.cloned.1.call-start = ((), (), s32[]{:S(2)}) async-start(), calls=%async_computation.22 | async-start | bytes 3932160 | tf_op jit(solution)/shard_map/all_gather | solution.py:280
  751.8 220.4 %all-gather.33.cloned.1.call-start = ((), (), s32[]{:S(2)}) async-start(), calls=%async_computation.24 | async-start | bytes 3932160 | tf_op jit(solution)/shard_map/all_gather | solution.py:185
  752.4 393.4 %all-gather.35.cloned.1.call-start = ((), (), s32[]{:S(2)}) async-start(), calls=%async_computation.25 | async-start | bytes 22937600 | tf_op jit(solution)/shard_map/all_gather | solution.py:188
  753.1 566.0 %all-gather.37.cloned.1.call-start = ((), (), s32[]{:S(2)}) async-start(), calls=%async_computation.27 | async-start | bytes 22937600 | tf_op jit(solution)/shard_map/all_gather | solution.py:189
  753.7 738.8 %all-gather.39.cloned.1.call-start = ((), (), s32[]{:S(2)}) async-start(), calls=%async_computation.29 | async-start | bytes 22937600 | tf_op jit(solution)/shard_map/all_gather | solution.py:187
  754.3 783.9 %all-gather.41.cloned.1.call-start = ((), (), s32[]{:S(2)}) async-start(), calls=%async_computation.30 | async-start | bytes 3932160 | tf_op jit(solution)/shard_map/all_gather | solution.py:186
  754.9 863.4 %reduce-scatter.18.cloned.1.call-start = ((), (), s32[]{:S(2)}) async-start(), calls=%async_computation.20 | async-start | bytes 221184 | tf_op jit(solution)/shard_map/reduce_scatter | solution.py:300
  787.8 831.8 %reduce-scatter.16.cloned.1.call-start = ((), (), s32[]{:S(2)}) async-start(), calls=%async_computation.19 | async-start | bytes 221184 | tf_op jit(solution)/shard_map/reduce_scatter | solution.py:297
  807.8 828.7 %reduce-scatter.14.cloned.1.call-start = ((), (), s32[]{:S(2)}) async-start(), calls=%async_computation.18 | async-start | bytes 1327104 | tf_op jit(solution)/shard_map/reduce_scatter | solution.py:294
  838.9 831.3 %reduce-scatter.20.cloned.1.call-start = ((), (), s32[]{:S(2)}) async-start(), calls=%async_computation.23 | async-start | bytes 1327104 | tf_op jit(solution)/shard_map/reduce_scatter | solution.py:303
  930.8 815.3 %reduce-scatter.22.cloned.1.call-start = ((), (), s32[]{:S(2)}) async-start(), calls=%async_computation.26 | async-start | bytes 7741440 | tf_op jit(solution)/shard_map/reduce_scatter | solution.py:198
  1161.2 661.1 %reduce-scatter.24.cloned.1.call-start = ((), (), s32[]{:S(2)}) async-start(), calls=%async_computation.28 | async-start | bytes 7741440 | tf_op jit(solution)/shard_map/reduce_scatter | solution.py:201
  1334.5 563.8 %reduce-scatter.26.cloned.1.call-start = ((), (), s32[]{:S(2)}) async-start(), calls=%async_computation.31 | async-start | bytes 7741440 | tf_op jit(solution)/shard_map/reduce_scatter | solution.py:204
  1550.3 5.1 slice-start
  1551.4 4.0 slice-start.1
  1555.4 14.0 copy-start.8
  1555.4 14.4 copy-start.23
  1555.4 14.4 copy-start.27
  1569.4 45.9 %copy-start.9 = (f32[256,1536]{1,0:T(8,128)S(1)}, f32[256,1536]{1,0:T(8,128)}, u32[]{:S(2)}) copy-start(f32[256,1536]{1,0:T(8,128)} %get-tuple-element.35) | copy-start | bytes 4718596
  1569.4 45.9 %copy-start.28 = (f32[256]{0:T(256)S(1)}, f32[256]{0:T(256)}, u32[]{:S(2)}) copy-start(f32[256]{0:T(256)} %get-tuple-element.49) | copy-start | bytes 3076
  (7 other events, 12.2 us)
Sparse Core Ops, SparseCore 0:
  10.9 67.7 all-gather.14
  81.6 66.5 all-gather.16
  151.1 172.2 all-gather.18
  326.2 164.0 all-gather.20
  493.1 164.0 all-gather.22
  659.5 42.1 all-gather.24
  725.7 26.0 reduce-scatter.11
  755.4 30.2 reduce-scatter.9
  787.5 46.9 all-gather.26
  836.8 43.8 all-gather.28
  882.5 43.9 all-gather.30
  928.2 43.9 all-gather.32
  974.1 171.6 all-gather.34
  1147.5 171.6 all-gather.36
  1320.9 171.6 all-gather.38
  1494.2 43.9 all-gather.40
  1540.9 30.3 reduce-scatter.17
  1574.0 28.4 reduce-scatter.15
  1605.4 31.1 reduce-scatter.13
  1639.3 30.9 reduce-scatter.19
  1672.5 73.5 reduce-scatter.21
  1748.5 73.7 reduce-scatter.23
  1824.6 73.7 reduce-scatter.25
where the time goes:
time: 1910 us
  waiting for transfers between devices  1300 us (68%)
  blocking collectives  287 us (15%)
  matrix products  201 us (11%)
  local copies, waits for them, and re-layouts  64.2 us (3%)
  other arithmetic  39.5 us (2%)
    all_gather x1, waiting for transfers between devices, per_device(): gate_piece = lax.all_gather(grad_gate, 'ctx', axis=0, tiled=True)  168 us
    all_gather x1, waiting for transfers between devices, per_device(): upward_piece = lax.all_gather(grad_upward, 'ctx', axis=0, tiled=True)  158 us
    all_gather x1, waiting for transfers between devices, per_device(): active_piece = lax.all_gather(active, 'ctx', axis=0, tiled=True)  158 us
    all_gather x1, waiting for transfers between devices, per_device(): lax.all_gather(down_weight, ('dp', 'ctx'), axis=0, tiled=True)  152 us
    all_gather x1, waiting for transfers between devices, per_device(): lax.all_gather(up_weight, ('dp', 'ctx'), axis=0, tiled=True)  152 us
    unnamed x2, blocking collectives  82.3 us
    all_gather x1, blocking collectives, per_device(): lax.all_gather(value_weight, ('dp', 'ctx'), axis=0, tiled=True)  74.8 us
    reduce_scatter x1, waiting for transfers between devices, per_device(): lax.psum_scatter(part_gate.astype(jnp.bfloat16), 'dp', scatter_dimension=...  74.3 us
  transfers between devices with their start and end apart: 23, of which 17 were waited for; matrix products, arithmetic and copies ran while one was open for 15% of the time, Pallas kernels for 0%

commit v1 on v0

v1 whole, which is shorter than its diff:
```python
import jax
import jax.numpy as jnp
from jax import lax
from jax.sharding import PartitionSpec as P

D = 1536
HEADS = 12
KV_HEADS = 2
HEAD = 128
DOCS = 5


EPS = 1e-06
F32 = jnp.float32
LOW = jnp.bfloat16


def turn(values, cosine, sine):
    half = values.shape[-1] // 2
    first = values[..., :half]
    second = values[..., half:]
    cosine = cosine[:, None, :]
    sine = sine[:, None, :]
    return jnp.concatenate(
        [first * cosine - second * sine, second * cosine + first * sine], axis=-1
    )


def unturn(grads, cosine, sine):
    half = grads.shape[-1] // 2
    first = grads[..., :half]
    second = grads[..., half:]
    cosine = cosine[:, None, :]
    sine = sine[:, None, :]
    return jnp.concatenate(
        [first * cosine + second * sine, second * cosine - first * sine], axis=-1
    )


def score_block(query_rot, key_all, allowed):
    tokens = query_rot.shape[0]
    grouped = query_rot.reshape(tokens, KV_HEADS, HEADS // KV_HEADS, HEAD)
    keyed = key_all.reshape(key_all.shape[0], KV_HEADS, HEAD)
    scores = jnp.einsum(
        "tkgd,skd->kgts", grouped, keyed, preferred_element_type=F32
    ) * HEAD ** (-0.5)
    return jnp.where(allowed[None, None], scores, -1e30)


def norm_back(grad_normed, hidden, inverse, gain):
    scaled = grad_normed * gain
    grad_gain = jnp.sum(grad_normed * hidden * inverse, axis=0)
    grad_hidden = inverse * scaled - hidden * inverse**3 * jnp.mean(
        scaled * hidden, axis=1, keepdims=True
    )
    return (grad_gain, grad_hidden)


class Line:
    def __init__(self, axis, size, stride):
        self.axis, self.size, self.stride = axis, size, stride
        total = lax.axis_size(axis)
        self.place = (lax.axis_index(axis) // stride) % size
        self.up = []
        for i in range(total):
            place = (i // stride) % size
            self.up.append((i, i + ((place + 1) % size - place) * stride))

    def shift(self, value):
        return lax.ppermute(value, self.axis, self.up)

    def ring(self, value):
        parts = [value]
        for _ in range(self.size - 1):
            parts.append(self.shift(parts[-1]))
        return parts

    def ordered(self, parts, dim):
        if self.size == 2:
            first = self.place == 0
            return jnp.stack(
                [jnp.where(first, parts[0], parts[1]), jnp.where(first, parts[1], parts[0])], dim
            )
        shape = parts[0].shape
        whole = jnp.zeros(shape[:dim] + (self.size,) + shape[dim:], parts[0].dtype)
        for step, part in enumerate(parts):
            whole = lax.dynamic_update_slice_in_dim(
                whole, jnp.expand_dims(part, dim), (self.place - step) % self.size, dim
            )
        return whole

    def gather(self, value, dim):
        return self.ordered(self.ring(value), dim)

    def pick(self, blocks, dim, step):
        return lax.dynamic_index_in_dim(blocks, (self.place - step) % self.size, dim, False)

    def scatter(self, blocks, dim, kind=LOW):
        total = self.pick(blocks, dim, 1)
        for step in range(2, self.size + 1):
            total = self.shift(total.astype(kind)).astype(F32)
            total = total + self.pick(blocks, dim, step).astype(F32)
        return total


def per_device(
    layer_input,
    cotangent,
    doc_lengths,
    attention_gain,
    query_weight,
    key_weight,
    value_weight,
    query_bias,
    key_bias,
    value_bias,
    output_weight,
    feedforward_gain,
    gate_weight,
    up_weight,
    down_weight,
):
    tokens = layer_input.shape[0]
    n_dp = lax.axis_size("dp")
    n_ctx = lax.axis_size("ctx")
    here = lax.axis_index("dp")
    which = lax.axis_index("ctx")
    chip = Line("dp", n_dp // 2, 2)
    core = Line("dp", 2, 1)
    outer = Line("ctx", n_ctx // 2, 2)
    inner = Line("ctx", 2, 1)
    rows = query_weight.shape[0]
    kv_width = KV_HEADS * HEAD

    def plane_gather(value, first, dim):
        if first:
            return outer.gather(inner.gather(value, dim), dim)
        return inner.gather(outer.gather(value, dim), dim + 1)

    def plane_scatter(blocks, first, dim, kind=LOW):
        if first:
            return outer.scatter(inner.scatter(blocks, dim + 1, kind), dim, kind)
        return inner.scatter(outer.scatter(blocks, dim, kind), dim, kind)

    def all_gather(value, first):
        gathered = plane_gather(chip.gather(value, 0), first, 1)
        return core.gather(gathered, 1)

    def all_scatter(blocks, first, kind=LOW):
        return chip.scatter(
            plane_scatter(core.scatter(blocks, 1, kind), first, 1, kind), 0, kind
        )

    def split_owners(array):
        return array.reshape((n_dp // 2, 2, n_ctx // 2, 2, -1) + array.shape[1:])

    vectors = jnp.concatenate(
        [attention_gain, feedforward_gain, query_bias, key_bias, value_bias]
    )[None]
    vectors = all_gather(vectors, True).reshape(n_dp * n_ctx, -1)
    cuts = [rows, 2 * rows, 3 * rows, 3 * rows + key_bias.shape[0]]
    gain_a, gain_f, bias_q, bias_k, bias_v = (
        part.reshape(-1).astype(F32) for part in jnp.split(vectors, cuts, axis=1)
    )
    mixed_weight = jnp.concatenate([query_weight, key_weight, value_weight], axis=1)
    half = mixed_weight.shape[1] // 2
    weight_in = [
        all_gather(mixed_weight[:, :half], True).reshape(D, half),
        all_gather(mixed_weight[:, half:], False).reshape(D, half),
    ]
    weight_o = jnp.concatenate(
        [
            all_gather(output_weight[:, : D // 2], True).reshape(D, D // 2),
            all_gather(output_weight[:, D // 2 :], False).reshape(D, D // 2),
        ],
        axis=1,
    )

    width = gate_weight.shape[1] // n_dp
    units = jnp.stack(
        [gate_weight.reshape(rows, n_dp, width), up_weight.reshape(rows, n_dp, width)]
    ).transpose(2, 0, 1, 3)

    def exchange(blocks):
        got = jnp.zeros(blocks.shape, blocks.dtype)
        own = lax.dynamic_index_in_dim(blocks, here, 0, True)
        got = lax.dynamic_update_slice_in_dim(got, own, here, 0)
        for step in range(1, n_dp):
            there = lax.dynamic_index_in_dim(blocks, (here + step) % n_dp, 0, True)
            arrived = lax.ppermute(there, "dp", [(i, (i + step) % n_dp) for i in range(n_dp)])
            got = lax.dynamic_update_slice_in_dim(got, arrived, (here - step) % n_dp, 0)
        return got

    units = exchange(units)
    weight_g = plane_gather(units[:, 0], True, 1).reshape(D, width)
    weight_u = plane_gather(units[:, 1], False, 1).reshape(D, width)
    weight_d = jnp.concatenate(
        [
            plane_gather(down_weight[:, : D // 2], True, 0).reshape(width, D // 2),
            plane_gather(down_weight[:, D // 2 :], False, 0).reshape(width, D // 2),
        ],
        axis=1,
    )

    def token_chunks(value):
        return [
            jnp.concatenate([part, core.shift(part)], axis=0) for part in chip.ring(value)
        ]

    upstream = token_chunks(cotangent)

    whole = tokens * n_ctx
    places = jnp.arange(whole, dtype=jnp.int32)
    lengths = doc_lengths[0]
    order = jnp.arange(DOCS, dtype=jnp.int32)
    ends = jnp.sum(jnp.where(order[None, :] <= order[:, None], lengths[None, :], 0), axis=1)
    starts = ends - lengths
    segment = jnp.sum((places[:, None] >= ends[None, :]).astype(jnp.int32), axis=1)
    chosen = (segment[:, None] == order[None, :]).astype(jnp.int32)
    offsets = places - jnp.sum(chosen * starts[None, :], axis=1)
    padded = segment == DOCS - 1
    first_row = which * tokens
    mine = lax.dynamic_slice_in_dim(places, first_row, tokens)
    my_segment = lax.dynamic_slice_in_dim(segment, first_row, tokens)
    my_offsets = lax.dynamic_slice_in_dim(offsets, first_row, tokens)
    allowed = (places[None, :] <= mine[:, None]) & (segment[None, :] == my_segment[:, None])
    allowed = allowed & (jnp.logical_not(padded)[None, :] | (places[None, :] == mine[:, None]))
    freqs = 10000.0 ** (-jnp.arange(0, HEAD // 2, dtype=F32) * 2.0 / HEAD)
    angles = my_offsets.astype(F32)[:, None] * freqs[None, :]
    cosine = jnp.cos(angles)
    sine = jnp.sin(angles)

    hidden = layer_input.astype(F32)
    inverse = lax.rsqrt(jnp.mean(hidden * hidden, axis=1, keepdims=True) + EPS)
    normed = (hidden * inverse * gain_a).astype(LOW)
    projected = jnp.concatenate(
        [jnp.dot(normed, part, preferred_element_type=F32) for part in weight_in], axis=1
    )
    queries = projected[:, :D] + bias_q
    keys = projected[:, D : D + kv_width] + bias_k
    values = projected[:, D + kv_width :] + bias_v
    query_rot = turn(queries.reshape(tokens, HEADS, HEAD), cosine, sine).astype(LOW)
    key_rot = (
        turn(keys.reshape(tokens, KV_HEADS, HEAD), cosine, sine)
        .astype(LOW)
        .reshape(tokens, kv_width)
    )
    value_low = values.astype(LOW)
    key_all = plane_gather(key_rot, True, 0).reshape(whole, kv_width)
    value_all = plane_gather(value_low, False, 0).reshape(whole, kv_width)
    scores = score_block(query_rot, key_all, allowed)
    top = jnp.max(scores, axis=-1, keepdims=True)
    weights = jnp.exp(scores - top)
    totals = jnp.sum(weights, axis=-1, keepdims=True)
    probs = weights / totals
    log_total = top + jnp.log(totals)
    value_heads = value_all.reshape(whole, KV_HEADS, HEAD)
    mixed = jnp.einsum(
        "kgts,skd->tkgd", probs.astype(LOW), value_heads, preferred_element_type=F32
    )
    mixed_low = mixed.reshape(tokens, D).astype(LOW)
    middle = hidden + jnp.dot(mixed_low, weight_o, preferred_element_type=F32)

    inverse2 = lax.rsqrt(jnp.mean(middle * middle, axis=1, keepdims=True) + EPS)
    normed2 = (middle * inverse2 * gain_f).astype(LOW)
    inputs = token_chunks(normed2)
    actives, grad_gates, grad_upwards, outs, grads = [], [], [], [], []
    for fed, back in zip(inputs, upstream):
        gate = jnp.dot(fed, weight_g, preferred_element_type=F32)
        upward = jnp.dot(fed, weight_u, preferred_element_type=F32)
        grad_active = jnp.einsum("td,fd->tf", back, weight_d, preferred_element_type=F32)
        sigmoid_gate = jax.nn.sigmoid(gate)
        active = (gate * sigmoid_gate * upward).astype(LOW)
        grad_gate = (
            grad_active * upward * sigmoid_gate * (1.0 + gate * (1.0 - sigmoid_gate))
        ).astype(LOW)
        grad_upward = (grad_active * gate * sigmoid_gate).astype(LOW)
        grads.append(
            jnp.einsum("tf,df->td", grad_gate, weight_g, preferred_element_type=F32)
            + jnp.einsum("tf,df->td", grad_upward, weight_u, preferred_element_type=F32)
        )
        outs.append(jnp.dot(active, weight_d, preferred_element_type=F32))
        actives.append(active)
        grad_gates.append(grad_gate)
        grad_upwards.append(grad_upward)

    def token_sums(parts):
        kept = [part[:tokens] + core.shift(part[tokens:].astype(LOW)).astype(F32) for part in parts]
        total = kept[1 % len(kept)]
        for step in range(2, len(kept) + 1):
            total = chip.shift(total.astype(LOW)).astype(F32) + kept[step % len(kept)]
        return total

    grad_normed2 = token_sums(grads)
    layer_output = (middle + token_sums(outs)).astype(LOW)

    fed_all = jnp.concatenate(inputs, axis=0)
    back_all = jnp.concatenate(upstream, axis=0)
    part_gate = jnp.einsum(
        "td,tf->df", fed_all, jnp.concatenate(grad_gates, axis=0), preferred_element_type=F32
    ).astype(LOW)
    part_up = jnp.einsum(
        "td,tf->df", fed_all, jnp.concatenate(grad_upwards, axis=0), preferred_element_type=F32
    ).astype(LOW)
    part_down = jnp.einsum(
        "tf,td->fd", jnp.concatenate(actives, axis=0), back_all, preferred_element_type=F32
    ).astype(LOW)

    def by_plane(part):
        return part.reshape((n_dp, n_ctx // 2, 2, rows) + part.shape[1:])

    sum_gate = plane_scatter(by_plane(part_gate), True, 1).astype(LOW)
    sum_up = plane_scatter(by_plane(part_up), False, 1).astype(LOW)
    sums = exchange(jnp.stack([sum_gate, sum_up], axis=1))
    gate_weight_grad = sums[:, 0].transpose(1, 0, 2).reshape(rows, -1).astype(F32)
    up_weight_grad = sums[:, 1].transpose(1, 0, 2).reshape(rows, -1).astype(F32)
    down_parts = part_down.reshape(n_ctx // 2, 2, width // n_ctx, D)
    down_weight_grad = jnp.concatenate(
        [
            plane_scatter(down_parts[..., : D // 2], True, 0),
            plane_scatter(down_parts[..., D // 2 :], False, 0),
        ],
        axis=1,
    )

    grad_gain_f, grad_middle = norm_back(grad_normed2, middle, inverse2, gain_f)
    grad_middle = grad_middle + cotangent.astype(F32)
    grad_attention = grad_middle.astype(LOW)
    part_output = jnp.einsum(
        "td,te->de", mixed_low, grad_attention, preferred_element_type=F32
    ).astype(LOW)
    part_output = split_owners(part_output)
    output_weight_grad = jnp.concatenate(
        [
            all_scatter(part_output[..., : D // 2], True),
            all_scatter(part_output[..., D // 2 :], False),
        ],
        axis=1,
    )
    grad_mixed = jnp.einsum(
        "te,de->td", grad_attention, weight_o, preferred_element_type=F32
    ).astype(LOW)
    grad_heads = grad_mixed.reshape(tokens, KV_HEADS, HEADS // KV_HEADS, HEAD)
    probs = jnp.exp(score_block(query_rot, key_all, allowed) - log_total)
    grad_probs = jnp.einsum(
        "tkgd,skd->kgts", grad_heads, value_heads, preferred_element_type=F32
    )
    grad_scores = (
        probs * (grad_probs - jnp.sum(probs * grad_probs, axis=-1, keepdims=True))
    ).astype(LOW)
    grad_value_part = jnp.einsum(
        "kgts,tkgd->skd", probs.astype(LOW), grad_heads, preferred_element_type=F32
    )
    key_heads = key_all.reshape(whole, KV_HEADS, HEAD)
    grouped = query_rot.reshape(tokens, KV_HEADS, HEADS // KV_HEADS, HEAD)
    grad_query_rot = jnp.einsum(
        "kgts,skd->tkgd", grad_scores, key_heads, preferred_element_type=F32
    ) * HEAD ** (-0.5)
    grad_key_part = jnp.einsum(
        "kgts,tkgd->skd", grad_scores, grouped, preferred_element_type=F32
    ) * HEAD ** (-0.5)
    plane_shape = (n_ctx // 2, 2, tokens, kv_width)
    grad_key_rot = plane_scatter(grad_key_part.reshape(plane_shape), True, 0)
    grad_values = plane_scatter(grad_value_part.reshape(plane_shape), False, 0).astype(LOW)
    grad_keys = (
        unturn(grad_key_rot.reshape(tokens, KV_HEADS, HEAD), cosine, sine)
        .reshape(tokens, kv_width)
        .astype(LOW)
    )
    grad_queries = (
        unturn(grad_query_rot.reshape(tokens, HEADS, HEAD), cosine, sine)
        .reshape(tokens, D)
        .astype(LOW)
    )
    joined = jnp.concatenate([grad_queries, grad_keys, grad_values], axis=1)
    parts_in = [joined[:, :half], joined[:, half:]]
    scattered = [
        all_scatter(
            split_owners(
                jnp.einsum("td,te->de", normed, part, preferred_element_type=F32).astype(LOW)
            ),
            first,
        )
        for part, first in zip(parts_in, (True, False))
    ]
    in_grads = jnp.concatenate(scattered, axis=1)
    grad_normed = sum(
        jnp.einsum("te,de->td", part, weight, preferred_element_type=F32)
        for part, weight in zip(parts_in, weight_in)
    )
    grad_gain_a, grad_hidden = norm_back(grad_normed, hidden, inverse, gain_a)
    input_grad = grad_middle + grad_hidden
    bias_sums = jnp.sum(joined.astype(F32), axis=0)
    owners = n_dp * n_ctx
    small = jnp.concatenate(
        [
            part.reshape(owners, -1)
            for part in (
                grad_gain_a,
                grad_gain_f,
                bias_sums[:D],
                bias_sums[D : D + kv_width],
                bias_sums[D + kv_width :],
            )
        ],
        axis=1,
    )
    small = all_scatter(split_owners(small), True, F32)
    small_gain_a, small_gain_f, small_q, small_k, small_v = jnp.split(small[0], cuts)
    return (
        layer_output,
        input_grad,
        small_gain_a,
        in_grads[:, :D],
        in_grads[:, D : D + kv_width],
        in_grads[:, D + kv_width :],
        small_q,
        small_k,
        small_v,
        output_weight_grad,
        small_gain_f,
        gate_weight_grad,
        up_weight_grad,
        down_weight_grad,
    )


def solution(mesh):
    split = P(("dp", "ctx"), None)
    vector = P(("dp", "ctx"))
    placed = (
        split,
        split,
        P("dp", None),
        vector,
        split,
        split,
        split,
        vector,
        vector,
        vector,
        split,
        vector,
        split,
        split,
        split,
    )
    results = (
        split,
        split,
        vector,
        split,
        split,
        split,
        vector,
        vector,
        vector,
        split,
        vector,
        split,
        split,
        split,
    )
    return jax.shard_map(
        per_device, mesh=mesh, in_specs=placed, out_specs=results, check_vma=False
    )
```

time: 1910 us -> 986 us (0.52)
  waiting for transfers between devices: 1300 us -> 463 us
  blocking collectives: 287 us -> 0 us
  local copies, waits for them, and re-layouts: 64.2 us -> 179 us
  starting transfers between devices: 1.16 us -> 81.5 us
  other arithmetic: 39.5 us -> 81.1 us
  matrix products: 201 us -> 162 us
    all_gather x14 -> x0, waiting for transfers between devices: 1020 us -> none  [the longest x1 168 us: per_device(): gate_piece = lax.all_gather(grad_gate, 'ctx', axis=0, tiled=True)]
    ppermute x0 -> x126, waiting for transfers between devices: none -> 463 us  [the longest x112 379 us: shift(): return lax.ppermute(value, self.axis, self.up)]
    reduce_scatter x9 -> x0, waiting for transfers between devices: 275 us -> none  [the longest x1 74.3 us: per_device(): lax.psum_scatter(part_gate.astype(jnp.bfloat16), 'dp', scatter_dimension=...]
    all_gather x6 -> x0, blocking collectives: 205 us -> none  [the longest x1 74.8 us: per_device(): lax.all_gather(value_weight, ('dp', 'ctx'), axis=0, tiled=True)]
    unnamed x2 -> x0, blocking collectives: 82.3 us -> none
    ppermute x0 -> x126, starting transfers between devices: none -> 81.5 us  [the longest x112 71.2 us: shift(): return lax.ppermute(value, self.axis, self.up)]
    dot_general x23 -> x38, matrix products: 182 us -> 142 us  [the longest x4 18.8 us: per_device(): jnp.einsum('td,fd->tf', back, weight_d, preferred_element_type=F32)]
    all_gather x3 -> x0, local copies, waits for them, and re-layouts: 33.9 us -> none  [the longest x1 24.5 us: per_device(): active_piece = lax.all_gather(active, 'ctx', axis=0, tiled=True)]
  transfers between devices with their start and end apart: 23 -> 126, of which waited for: 17 -> 68; matrix products, arithmetic and copies ran while one was open for 15% -> 42% of each run, Pallas kernels for 0% -> 0%
where the time goes in v1:
time: 986 us; the launch traced here: 969 us
  waiting for transfers between devices  463 us (47%)
  local copies, waits for them, and re-layouts  179 us (18%)
  matrix products  162 us (16%)
  starting transfers between devices  81.5 us (8%)
  other arithmetic  81.1 us (8%)
    ppermute x112, waiting for transfers between devices, shift(): return lax.ppermute(value, self.axis, self.up)  379 us
    ppermute x14, waiting for transfers between devices, exchange(): lax.ppermute(there, 'dp', [(i, (i + step) % n_dp) for i in range(n_dp)])  83.9 us
    ppermute x112, starting transfers between devices, shift(): return lax.ppermute(value, self.axis, self.up)  71.2 us
    unnamed x314, local copies, waits for them, and re-layouts  44.7 us
    dynamic_slice x14, local copies, waits for them, and re-layouts, pick(): lax.dynamic_index_in_dim(blocks, (self.place - step) % self.size, dim, Fa...  25.7 us
    another operation x53, other arithmetic, ordered(): jnp.stack([jnp.where(first, parts[0], parts[1]), jnp.where(first, parts[1...  21.2 us
  transfers between devices with their start and end apart: 126, of which 68 were waited for; matrix products, arithmetic and copies ran while one was open for 42% of the time, Pallas kernels for 0%

profile of v1, /device:TPU:0, one launch (start us, length us, event | category | flops | bytes accessed | tf_op | source)
XLA Modules:
  0.0 969.4 jit_solution(491276500396688069)
XLA Ops:
  32.5 4.6 constant_dynamic-slice_fusion.25
  94.3 4.8 collective-permute-done.29
  99.2 6.3 collective-permute-done.23
  106.2 6.4 collective-permute-done.7
  113.2 6.0 collective-permute-done.17
  119.8 6.7 collective-permute-done.36
  126.6 7.9 collective-permute-done.37
  134.5 8.5 collective-permute-done.38
  143.0 10.3 %collective-permute-done.39 = bf16[1,2,48,1120]{3,2,1,0:T(8,128)(2,1)S(1)} collective-permute-done((bf16[1,2,48,1120]{3,2,1,0:T(8,128)(2,1)}, bf16[1,2,48,1120]{3,2,1,0:T(8,128)(2,1)S(1)}, u32[]{:S(2)}, u32[]{:S(2)}) %collective-permute-start.39) | collective-permute-done | bytes 215072 | tf_op jit(solution)/shard_map/ppermute | solution.py:190
  153.4 6.8 collective-permute-done.40
  163.7 4.7 collective-permute-done.41
  178.7 6.5 collective-permute-done.24
  185.2 6.5 collective-permute-done.8
  192.4 5.8 collective-permute-done.18
  200.9 6.6 collective-permute-done.31
  208.0 16.0 %collective-permute-done.25 = bf16[4,48,768]{2,1,0:T(8,128)(2,1)S(1)} collective-permute-done((bf16[4,48,768]{2,1,0:T(8,128)(2,1)S(1)}, bf16[4,48,768]{2,1,0:T(8,128)(2,1)S(1)}, u32[]{:S(2)}, u32[]{:S(2)}) %collective-permute-start.25) | collective-permute-done | bytes 294944 | tf_op jit(solution)/shard_map/ppermute | solution.py:70
  227.3 6.5 collective-permute-done.19
  247.8 29.9 %collective-permute-done.26 = bf16[4,2,48,768]{3,2,0,1:T(8,128)(2,1)S(1)} collective-permute-done((bf16[4,2,48,768]{3,2,0,1:T(8,128)(2,1)S(1)}, bf16[4,2,48,768]{3,2,0,1:T(8,128)(2,1)S(1)}, u32[]{:S(2)}, u32[]{:S(2)}) %collective-permute-start.26) | collective-permute-done | bytes 589856 | tf_op jit(solution)/shard_map/ppermute | solution.py:70
  283.3 7.3 collective-permute-done.20
  302.7 15.0 %collective-permute-done.71 = bf16[256,1536]{1,0:T(8,128)(2,1)} collective-permute-done((bf16[256,1536]{1,0:T(8,128)(2,1)S(1)}, bf16[256,1536]{1,0:T(8,128)(2,1)}, u32[]{:S(2)}, u32[]{:S(2)}) %collective-permute-start.71) | collective-permute-done | bytes 786464 | tf_op jit(solution)/shard_map/ppermute | solution.py:70
  321.3 15.3 %collective-permute-done.44 = bf16[8,2,48,1120]{3,2,0,1:T(8,128)(2,1)S(1)} collective-permute-done((bf16[8,2,48,1120]{3,2,0,1:T(8,128)(2,1)S(1)}, bf16[8,2,48,1120]{3,2,0,1:T(8,128)(2,1)S(1)}, u32[]{:S(2)}, u32[]{:S(2)}) %collective-permute-start.44) | collective-permute-done | bytes 1720352 | tf_op jit(solution)/shard_map/ppermute | solution.py:70
  410.0 4.9 collective-permute-done.34
  432.6 8.1 collective-permute-done.53
  452.5 5.4 multiply_convert_fusion.4
  478.6 5.2 multiply_convert_fusion.2
  489.2 9.7 %convolution_convert_fusion.2 = bf16[1120,1536]{1,0:T(8,128)(2,1)} fusion(bf16[2048,1536]{1,0:T(8,128)(2,1)S(1)} %bitcast.689, bf16[512,1120]{0,1:T(8,128)(2,1)} %copy-done.138, bf16[512,1120]{0,1:T(8,128)(2,1)S(1)} %copy-done.137, bf16[512,1120]{0,1:T(8,128)(2,1)S(1)} %copy-done.136, bf16[512,1120]{0,1:T(8,128)(2,1)S(1)} %copy-done.134), kind=kOutput, calls=%fused_computation.13 | convolution fusion | flops 7066501120 | bytes 14319616 | tf_op jit(solution)/shard_map/tf,td->fd/dot_general | solution.py:305
  502.9 8.7 convolution_convert_fusion.1
  511.6 8.6 convolution_convert_fusion
  524.6 7.3 convolution_add_fusion.1
  549.1 4.5 collective-permute-start.56
  556.7 14.5 %collective-permute-done.56 = bf16[256,1536]{1,0:T(8,128)(2,1)S(1)} collective-permute-done((bf16[256,1536]{1,0:T(8,128)(2,1)S(1)}, bf16[256,1536]{1,0:T(8,128)(2,1)S(1)}, u32[]{:S(2)}, u32[]{:S(2)}) %collective-permute-start.56) | collective-permute-done | bytes 786464 | tf_op jit(solution)/shard_map/ppermute | solution.py:70
  574.0 18.2 %collective-permute-done.122 = bf16[2,280,768]{2,1,0:T(8,128)(2,1)S(1)} collective-permute-done((bf16[2,280,768]{2,1,0:T(8,128)(2,1)S(1)}, bf16[2,280,768]{2,1,0:T(8,128)(2,1)S(1)}, u32[]{:S(2)}, u32[]{:S(2)}) %collective-permute-start.122) | collective-permute-done | bytes 860192 | tf_op jit(solution)/shard_map/ppermute | solution.py:70
  594.9 46.2 %collective-permute-done.125 = bf16[280,768]{1,0:T(8,128)(2,1)S(1)} collective-permute-done((bf16[280,768]{1,0:T(8,128)(2,1)S(1)}, bf16[280,768]{1,0:T(8,128)(2,1)S(1)}, u32[]{:S(2)}, u32[]{:S(2)}) %collective-permute-start.125) | collective-permute-done | bytes 430112 | tf_op jit(solution)/shard_map/ppermute | solution.py:70
  644.8 18.5 %collective-permute-done.74 = bf16[256,1536]{1,0:T(8,128)(2,1)S(1)} collective-permute-done((bf16[256,1536]{1,0:T(8,128)(2,1)S(1)}, bf16[256,1536]{1,0:T(8,128)(2,1)S(1)}, u32[]{:S(2)}, u32[]{:S(2)}) %collective-permute-start.74) | collective-permute-done | bytes 786464 | tf_op jit(solution)/shard_map/ppermute | solution.py:70
  664.7 12.6 %collective-permute-done.60 = bf16[256,1536]{1,0:T(8,128)(2,1)S(1)} collective-permute-done((bf16[256,1536]{1,0:T(8,128)(2,1)S(1)}, bf16[256,1536]{1,0:T(8,128)(2,1)S(1)}, u32[]{:S(2)}, u32[]{:S(2)}) %collective-permute-start.60) | collective-permute-done | bytes 786464 | tf_op jit(solution)/shard_map/ppermute | solution.py:70
  686.1 9.0 fusion.77
  702.3 4.8 convolution_convert_fusion.3
  707.0 10.2 %fusion = (f32[2,6,256]{2,1,0:T(8,128)}, f32[2,1024,256,6]{2,1,3,0:T(8,128)}) fusion(f32[2,6,256]{2,1,0:T(8,128)S(1)} %copy-done.95, f32[2,1024,256,6]{2,1,3,0:T(8,128)} %copy-done, pred[256,1024]{0,1:T(8,128)(4,1)S(1)} %copy-done.8, bf16[256,2,6,128]{0,3,2,1:T(8,128)(2,1)S(1)} %bitcast.647, bf16[1024,2,128,1]{2,1,0,3:T(2,128)(2,1)S(1)} %bitcast.657), kind=kOutput, calls=%fused_computation.2 | convolution fusion | flops 821031936 | bytes 26763264 | tf_op jit(solution)/shard_map/tkgd,skd->kgts/dot_general | solution.py:345
  730.5 6.8 fusion.2
  768.9 4.7 collective-permute-done.77
  778.5 18.4 %collective-permute-done.78 = bf16[256,256]{1,0:T(8,128)(2,1)} collective-permute-done((bf16[256,256]{1,0:T(8,128)(2,1)}, bf16[256,256]{1,0:T(8,128)(2,1)}, u32[]{:S(2)}, u32[]{:S(2)}) %collective-permute-start.78) | collective-permute-done | bytes 131104 | tf_op jit(solution)/shard_map/ppermute | solution.py:70
  803.5 5.2 fusion.44
  848.9 7.7 collective-permute-done.115
  858.5 6.7 collective-permute-done.116
  866.3 10.0 %collective-permute-done.117 = bf16[1,2,48,1120]{3,2,0,1:T(8,128)(2,1)S(1)} collective-permute-done((bf16[1,2,48,1120]{3,2,0,1:T(8,128)(2,1)S(1)}, bf16[1,2,48,1120]{3,2,0,1:T(8,128)(2,1)S(1)}, u32[]{:S(2)}, u32[]{:S(2)}) %collective-permute-start.117) | collective-permute-done | bytes 215072 | tf_op jit(solution)/shard_map/ppermute | solution.py:190
  876.3 10.5 %collective-permute-done.118 = bf16[1,2,48,1120]{3,2,0,1:T(8,128)(2,1)S(1)} collective-permute-done((bf16[1,2,48,1120]{3,2,0,1:T(8,128)(2,1)S(1)}, bf16[1,2,48,1120]{3,2,0,1:T(8,128)(2,1)S(1)}, u32[]{:S(2)}, u32[]{:S(2)}) %collective-permute-start.118) | collective-permute-done | bytes 215072 | tf_op jit(solution)/shard_map/ppermute | solution.py:190
  939.6 6.0 collective-permute-done.95
  947.2 4.9 collective-permute-done.96
  (854 shorter events, 499.8 us)
Async XLA Ops:
  0.7 234.9 %collective-permute-start.75 = (bf16[256,1536]{1,0:T(8,128)(2,1)}, bf16[256,1536]{1,0:T(8,128)(2,1)}, u32[]{:S(2)}, u32[]{:S(2)}) collective-permute-start(bf16[256,1536]{1,0:T(8,128)(2,1)} %param.16), channel_id=1, source_target_pairs={{0,4},{4,0},{8,12},{12,8},{16,20},{20,16},{24,28},{28,24},{1,5},{5... | collective-permute-start | bytes 2359304 | tf_op jit(solution)/shard_map/ppermute | solution.py:70
  1.2 238.1 %collective-permute-start.63 = (bf16[256,1536]{1,0:T(8,128)(2,1)}, bf16[256,1536]{1,0:T(8,128)(2,1)}, u32[]{:S(2)}, u32[]{:S(2)}) collective-permute-start(bf16[256,1536]{1,0:T(8,128)(2,1)} %param.16), channel_id=1, source_target_pairs={{0,8},{4,12},{8,16},{12,20},{16,24},{20,28},{24,0},{28,4},{1,9},{5... | collective-permute-start | bytes 2359304 | tf_op jit(solution)/shard_map/ppermute | solution.py:70
  7.8 33.6 %collective-permute-start = (bf16[1,160]{1,0:T(2,128)(2,1)}, bf16[1,160]{1,0:T(2,128)(2,1)}, u32[]{:S(2)}, u32[]{:S(2)}) collective-permute-start(bf16[1,160]{1,0:T(2,128)(2,1)} %broadcast_in_dim.73), channel_id=1, source_target_pairs={{0,8},{4,12},{8,16},{12,20},{16,24},{20,28},{24,0},{28,4},{1,9},{5... | collective-permute-start | bytes 968 | tf_op jit(solution)/shard_map/ppermute | solution.py:70
  11.0 81.9 %collective-permute-start.16 = (bf16[48,1024]{1,0:T(8,128)(2,1)}, bf16[48,1024]{1,0:T(8,128)(2,1)}, u32[]{:S(2)}, u32[]{:S(2)}) collective-permute-start(bf16[48,1024]{1,0:T(8,128)(2,1)} %slice.181), channel_id=1, source_target_pairs={{0,8},{4,12},{8,16},{12,20},{16,24},{20,28},{24,0},{28,4},{1,9},{5... | collective-permute-start | bytes 294920 | tf_op jit(solution)/shard_map/ppermute | solution.py:70
  14.1 69.8 %collective-permute-start.22 = (bf16[48,768]{1,0:T(8,128)(2,1)}, bf16[48,768]{1,0:T(8,128)(2,1)}, u32[]{:S(2)}, u32[]{:S(2)}) collective-permute-start(bf16[48,768]{1,0:T(8,128)(2,1)} %get-tuple-element.150), channel_id=1, source_target_pairs={{0,8},{4,12},{8,16},{12,20},{16,24},{20,28},{24,0},{28,4},{1,9},{5... | collective-permute-start | bytes 221192 | tf_op jit(solution)/shard_map/ppermute | solution.py:70
  84.5 115.1 %collective-permute-start.47 = (bf16[280,768]{1,0:T(8,128)(2,1)}, bf16[280,768]{1,0:T(8,128)(2,1)S(1)}, u32[]{:S(2)}, u32[]{:S(2)}) collective-permute-start(bf16[280,768]{1,0:T(8,128)(2,1)} %get-tuple-element.114), channel_id=1, source_target_pairs={{0,1},{1,0},{2,3},{3,2},{4,5},{5,4},{6,7},{7,6},{8,9},{9,8},{10,11... | collective-permute-start | bytes 1290248 | tf_op jit(solution)/shard_map/ppermute | solution.py:70
  90.5 109.8 %collective-permute-start.49 = (bf16[280,768]{1,0:T(8,128)(2,1)}, bf16[280,768]{1,0:T(8,128)(2,1)S(1)}, u32[]{:S(2)}, u32[]{:S(2)}) collective-permute-start(bf16[280,768]{1,0:T(8,128)(2,1)} %get-tuple-element.115), channel_id=1, source_target_pairs={{0,2},{1,3},{2,0},{3,1},{4,6},{5,7},{6,4},{7,5},{8,10},{9,11},{10,... | collective-permute-start | bytes 1290248 | tf_op jit(solution)/shard_map/ppermute | solution.py:70
  198.1 43.7 %collective-permute-start.43 = (bf16[8,48,1120]{2,1,0:T(8,128)(2,1)S(1)}, bf16[8,48,1120]{2,1,0:T(8,128)(2,1)S(1)}, u32[]{:S(2)}, u32[]{:S(2)}) collective-permute-start(bf16[8,48,1120]{2,1,0:T(8,128)(2,1)S(1)} %get-tuple-element.78), channel_id=1, source_target_pairs={{0,1},{1,0},{2,3},{3,2},{4,5},{5,4},{6,7},{7,6},{8,9},{9,8},{10,11... | collective-permute-start | bytes 2580488 | tf_op jit(solution)/shard_map/ppermute | solution.py:70
  199.7 24.4 %collective-permute-start.25 = (bf16[4,48,768]{2,1,0:T(8,128)(2,1)S(1)}, bf16[4,48,768]{2,1,0:T(8,128)(2,1)S(1)}, u32[]{:S(2)}, u32[]{:S(2)}) collective-permute-start(bf16[4,48,768]{2,1,0:T(8,128)(2,1)S(1)} %bitcast_dynamic-update-slice_fusion.20), channel_id=1, source_target_pairs={{0,1},{1,0},{2,3},{3,2},{4,5},{5,4},{6,7},{7,6},{8,9},{9,8},{10,11... | collective-permute-start | bytes 884744 | tf_op jit(solution)/shard_map/ppermute | solution.py:70
  224.0 22.6 %collective-permute-start.45 = (bf16[8,48,1120]{2,1,0:T(8,128)(2,1)S(1)}, bf16[8,48,1120]{2,1,0:T(8,128)(2,1)S(1)}, u32[]{:S(2)}, u32[]{:S(2)}) collective-permute-start(bf16[8,48,1120]{2,1,0:T(8,128)(2,1)S(1)} %get-tuple-element.79), channel_id=1, source_target_pairs={{0,2},{1,3},{2,0},{3,1},{4,6},{5,7},{6,4},{7,5},{8,10},{9,11},{10,... | collective-permute-start | bytes 2580488 | tf_op jit(solution)/shard_map/ppermute | solution.py:70
  233.9 45.9 %collective-permute-start.50 = (bf16[2,280,768]{2,1,0:T(8,128)(2,1)S(1)}, bf16[2,280,768]{2,1,0:T(8,128)(2,1)S(1)}, u32[]{:S(2)}, u32[]{:S(2)}) collective-permute-start(bf16[2,280,768]{2,1,0:T(8,128)(2,1)S(1)} %pad_maximum_fusion.29), channel_id=1, source_target_pairs={{0,1},{1,0},{2,3},{3,2},{4,5},{5,4},{6,7},{7,6},{8,9},{9,8},{10,11... | collective-permute-start | bytes 2580488 | tf_op jit(solution)/shard_map/ppermute | solution.py:70
  235.6 45.7 %collective-permute-start.48 = (bf16[2,280,768]{2,1,0:T(8,128)(2,1)S(1)}, bf16[2,280,768]{2,1,0:T(8,128)(2,1)S(1)}, u32[]{:S(2)}, u32[]{:S(2)}) collective-permute-start(bf16[2,280,768]{2,1,0:T(8,128)(2,1)S(1)} %pad_maximum_fusion.28), channel_id=1, source_target_pairs={{0,2},{1,3},{2,0},{3,1},{4,6},{5,7},{6,4},{7,5},{8,10},{9,11},{10,... | collective-permute-start | bytes 2580488 | tf_op jit(solution)/shard_map/ppermute | solution.py:70
  239.3 38.4 %collective-permute-start.26 = (bf16[4,2,48,768]{3,2,0,1:T(8,128)(2,1)S(1)}, bf16[4,2,48,768]{3,2,0,1:T(8,128)(2,1)S(1)}, u32[]{:S(2)}, u32[]{:S(2)}) collective-permute-start(bf16[4,2,48,768]{3,2,0,1:T(8,128)(2,1)S(1)} %pad_maximum_fusion.34), channel_id=1, source_target_pairs={{0,2},{1,3},{2,0},{3,1},{4,6},{5,7},{6,4},{7,5},{8,10},{9,11},{10,... | collective-permute-start | bytes 1769480 | tf_op jit(solution)/shard_map/ppermute | solution.py:70
  241.9 37.6 %collective-permute-start.32 = (bf16[4,2,48,768]{3,2,1,0:T(8,128)(2,1)S(1)}, bf16[4,2,48,768]{3,2,1,0:T(8,128)(2,1)S(1)}, u32[]{:S(2)}, u32[]{:S(2)}) collective-permute-start(bf16[4,2,48,768]{3,2,1,0:T(8,128)(2,1)S(1)} %pad_maximum_fusion.35), channel_id=1, source_target_pairs={{0,1},{1,0},{2,3},{3,2},{4,5},{5,4},{6,7},{7,6},{8,9},{9,8},{10,11... | collective-permute-start | bytes 1769480 | tf_op jit(solution)/shard_map/ppermute | solution.py:70
  246.6 44.0 %collective-permute-start.20 = (bf16[4,2,48,1024]{3,2,1,0:T(8,128)(2,1)S(1)}, bf16[4,2,48,1024]{3,2,1,0:T(8,128)(2,1)S(1)}, u32[]{:S(2)}, u32[]{:S(2)}) collective-permute-start(bf16[4,2,48,1024]{3,2,1,0:T(8,128)(2,1)S(1)} %pad_maximum_fusion.31), channel_id=1, source_target_pairs={{0,2},{1,3},{2,0},{3,1},{4,6},{5,7},{6,4},{7,5},{8,10},{9,11},{10,... | collective-permute-start | bytes 2359304 | tf_op jit(solution)/shard_map/ppermute | solution.py:70
  281.3 58.3 %collective-permute-start.46 = (bf16[8,2,48,1120]{3,2,1,0:T(8,128)(2,1)S(1)}, bf16[8,2,48,1120]{3,2,1,0:T(8,128)(2,1)S(1)}, u32[]{:S(2)}, u32[]{:S(2)}) collective-permute-start(bf16[8,2,48,1120]{3,2,1,0:T(8,128)(2,1)S(1)} %pad_maximum_fusion.15), channel_id=1, source_target_pairs={{0,1},{1,0},{2,3},{3,2},{4,5},{5,4},{6,7},{7,6},{8,9},{9,8},{10,11... | collective-permute-start | bytes 5160968 | tf_op jit(solution)/shard_map/ppermute | solution.py:70
  295.5 41.1 %collective-permute-start.44 = (bf16[8,2,48,1120]{3,2,0,1:T(8,128)(2,1)S(1)}, bf16[8,2,48,1120]{3,2,0,1:T(8,128)(2,1)S(1)}, u32[]{:S(2)}, u32[]{:S(2)}) collective-permute-start(bf16[8,2,48,1120]{3,2,0,1:T(8,128)(2,1)S(1)} %pad_maximum_fusion.14), channel_id=1, source_target_pairs={{0,2},{1,3},{2,0},{3,1},{4,6},{5,7},{6,4},{7,5},{8,10},{9,11},{10,... | collective-permute-start | bytes 5160968 | tf_op jit(solution)/shard_map/ppermute | solution.py:70
  300.3 41.6 %collective-permute-start.21 = (bf16[4,2,2,48,1024]{4,3,2,1,0:T(8,128)(2,1)S(1)}, bf16[4,2,2,48,1024]{4,3,2,1,0:T(8,128)(2,1)S(1)}, u32[]{:S(2)}, u32[]{:S(2)}) collective-permute-start(bf16[4,2,2,48,1024]{4,3,2,1,0:T(8,128)(2,1)S(1)} %pad_maximum_fusion.21), channel_id=1, source_target_pairs={{0,4},{4,0},{8,12},{12,8},{16,20},{20,16},{24,28},{28,24},{1,5},{5... | collective-permute-start | bytes 4718600 | tf_op jit(solution)/shard_map/ppermute | solution.py:70
  317.7 25.2 %collective-permute-start.11 = (bf16[4,2,2,48,1024]{4,3,2,1,0:T(8,128)(2,1)S(1)}, bf16[4,2,2,48,1024]{4,3,2,1,0:T(8,128)(2,1)S(1)}, u32[]{:S(2)}, u32[]{:S(2)}) collective-permute-start(bf16[4,2,2,48,1024]{4,3,2,1,0:T(8,128)(2,1)S(1)} %copy.340), channel_id=1, source_target_pairs={{0,4},{4,0},{8,12},{12,8},{16,20},{20,16},{24,28},{28,24},{1,5},{5... | collective-permute-start | bytes 4718600 | tf_op jit(solution)/shard_map/ppermute | solution.py:70
  317.7 73.2 %collective-permute-start.72 = (bf16[256,1536]{1,0:T(8,128)(2,1)}, bf16[256,1536]{1,0:T(8,128)(2,1)}, u32[]{:S(2)}, u32[]{:S(2)}) collective-permute-start(bf16[256,1536]{1,0:T(8,128)(2,1)} %collective-permute-done.71), channel_id=1, source_target_pairs={{0,4},{4,0},{8,12},{12,8},{16,20},{20,16},{24,28},{28,24},{1,5},{5... | collective-permute-start | bytes 2359304 | tf_op jit(solution)/shard_map/ppermute | solution.py:70
  407.7 257.0 %collective-permute-start.62 = (bf16[256,1536]{1,0:T(8,128)(2,1)}, bf16[256,1536]{1,0:T(8,128)(2,1)}, u32[]{:S(2)}, u32[]{:S(2)}) collective-permute-start(bf16[256,1536]{1,0:T(8,128)(2,1)} %slice.371), channel_id=1, source_target_pairs={{0,4},{4,0},{8,12},{12,8},{16,20},{20,16},{24,28},{28,24},{1,5},{5... | collective-permute-start | bytes 2359304 | tf_op jit(solution)/shard_map/ppermute | solution.py:70
  418.9 21.8 %collective-permute-start.53 = (bf16[256,1536]{1,0:T(8,128)(2,1)S(1)}, bf16[256,1536]{1,0:T(8,128)(2,1)S(1)}, u32[]{:S(2)}, u32[]{:S(2)}) collective-permute-start(bf16[256,1536]{1,0:T(8,128)(2,1)S(1)} %collective-permute-done.34), channel_id=1, source_target_pairs={{0,8},{4,12},{8,16},{12,20},{16,24},{20,28},{24,0},{28,4},{1,9},{5... | collective-permute-start | bytes 2359304 | tf_op jit(solution)/shard_map/ppermute | solution.py:70
  443.8 23.2 %collective-permute-start.57 = (bf16[256,1536]{1,0:T(8,128)(2,1)S(1)}, bf16[256,1536]{1,0:T(8,128)(2,1)S(1)}, u32[]{:S(2)}, u32[]{:S(2)}) collective-permute-start(bf16[256,1536]{1,0:T(8,128)(2,1)S(1)} %collective-permute-done.53), channel_id=1, source_target_pairs={{0,8},{4,12},{8,16},{12,20},{16,24},{20,28},{24,0},{28,4},{1,9},{5... | collective-permute-start | bytes 2359304 | tf_op jit(solution)/shard_map/ppermute | solution.py:70
  451.9 93.6 %collective-permute-start.52 = (bf16[256,1536]{1,0:T(8,128)(2,1)}, bf16[256,1536]{1,0:T(8,128)(2,1)}, u32[]{:S(2)}, u32[]{:S(2)}) collective-permute-start(bf16[256,1536]{1,0:T(8,128)(2,1)} %fusion.58), channel_id=1, source_target_pairs={{0,8},{4,12},{8,16},{12,20},{16,24},{20,28},{24,0},{28,4},{1,9},{5... | collective-permute-start | bytes 2359304 | tf_op jit(solution)/shard_map/ppermute | solution.py:70
  463.3 83.3 %collective-permute-start.55 = (bf16[256,1536]{1,0:T(8,128)(2,1)}, bf16[256,1536]{1,0:T(8,128)(2,1)}, u32[]{:S(2)}, u32[]{:S(2)}) collective-permute-start(bf16[256,1536]{1,0:T(8,128)(2,1)} %slice.373), channel_id=1, source_target_pairs={{0,4},{4,0},{8,12},{12,8},{16,20},{20,16},{24,28},{28,24},{1,5},{5... | collective-permute-start | bytes 2359304 | tf_op jit(solution)/shard_map/ppermute | solution.py:70
  464.5 84.6 %collective-permute-start.66 = (bf16[256,1536]{1,0:T(8,128)(2,1)}, bf16[256,1536]{1,0:T(8,128)(2,1)}, u32[]{:S(2)}, u32[]{:S(2)}) collective-permute-start(bf16[256,1536]{1,0:T(8,128)(2,1)} %fusion.50), channel_id=1, source_target_pairs={{0,8},{4,12},{8,16},{12,20},{16,24},{20,28},{24,0},{28,4},{1,9},{5... | collective-permute-start | bytes 2359304 | tf_op jit(solution)/shard_map/ppermute | solution.py:70
  471.6 82.0 %collective-permute-start.69 = (bf16[256,1536]{1,0:T(8,128)(2,1)}, bf16[256,1536]{1,0:T(8,128)(2,1)}, u32[]{:S(2)}, u32[]{:S(2)}) collective-permute-start(bf16[256,1536]{1,0:T(8,128)(2,1)} %slice.369), channel_id=1, source_target_pairs={{0,4},{4,0},{8,12},{12,8},{16,20},{20,16},{24,28},{28,24},{1,5},{5... | collective-permute-start | bytes 2359304 | tf_op jit(solution)/shard_map/ppermute | solution.py:70
  546.2 98.2 %collective-permute-start.76 = (bf16[256,1536]{1,0:T(8,128)(2,1)S(1)}, bf16[256,1536]{1,0:T(8,128)(2,1)S(1)}, u32[]{:S(2)}, u32[]{:S(2)}) collective-permute-start(bf16[256,1536]{1,0:T(8,128)(2,1)S(1)} %copy-done.90), channel_id=1, source_target_pairs={{0,4},{4,0},{8,12},{12,8},{16,20},{20,16},{24,28},{28,24},{1,5},{5... | collective-permute-start | bytes 2359304 | tf_op jit(solution)/shard_map/ppermute | solution.py:70
  546.6 25.0 %collective-permute-start.124 = (bf16[2,280,768]{2,1,0:T(8,128)(2,1)S(1)}, bf16[2,280,768]{2,1,0:T(8,128)(2,1)S(1)}, u32[]{:S(2)}, u32[]{:S(2)}) collective-permute-start(bf16[2,280,768]{2,1,0:T(8,128)(2,1)S(1)} %dynamic-slice_bitcast_fusion.1), channel_id=1, source_target_pairs={{0,2},{1,3},{2,0},{3,1},{4,6},{5,7},{6,4},{7,5},{8,10},{9,11},{10,... | collective-permute-start | bytes 2580488 | tf_op jit(solution)/shard_map/ppermute | solution.py:70
  549.1 22.2 %collective-permute-start.56 = (bf16[256,1536]{1,0:T(8,128)(2,1)S(1)}, bf16[256,1536]{1,0:T(8,128)(2,1)S(1)}, u32[]{:S(2)}, u32[]{:S(2)}) collective-permute-start(bf16[256,1536]{1,0:T(8,128)(2,1)S(1)} %fusion.57), channel_id=1, source_target_pairs={{0,8},{4,12},{8,16},{12,20},{16,24},{20,28},{24,0},{28,4},{1,9},{5... | collective-permute-start | bytes 2359304 | tf_op jit(solution)/shard_map/ppermute | solution.py:70
  571.7 22.8 %collective-permute-start.70 = (bf16[256,1536]{1,0:T(8,128)(2,1)S(1)}, bf16[256,1536]{1,0:T(8,128)(2,1)S(1)}, u32[]{:S(2)}, u32[]{:S(2)}) collective-permute-start(bf16[256,1536]{1,0:T(8,128)(2,1)S(1)} %fusion.49), channel_id=1, source_target_pairs={{0,8},{4,12},{8,16},{12,20},{16,24},{20,28},{24,0},{28,4},{1,9},{5... | collective-permute-start | bytes 2359304 | tf_op jit(solution)/shard_map/ppermute | solution.py:70
  592.2 173.8 %collective-permute-start.111 = (bf16[8,2,48,1120]{3,2,1,0:T(8,128)(2,1)}, bf16[8,2,48,1120]{3,2,1,0:T(8,128)(2,1)}, u32[]{:S(2)}, u32[]{:S(2)}) collective-permute-start(bf16[8,2,48,1120]{3,2,1,0:T(8,128)(2,1)} %dynamic-slice_bitcast_fusion), channel_id=1, source_target_pairs={{0,1},{1,0},{2,3},{3,2},{4,5},{5,4},{6,7},{7,6},{8,9},{9,8},{10,11... | collective-permute-start | bytes 5160968 | tf_op jit(solution)/shard_map/ppermute | solution.py:70
  592.7 48.4 %collective-permute-start.125 = (bf16[280,768]{1,0:T(8,128)(2,1)S(1)}, bf16[280,768]{1,0:T(8,128)(2,1)S(1)}, u32[]{:S(2)}, u32[]{:S(2)}) collective-permute-start(bf16[280,768]{1,0:T(8,128)(2,1)S(1)} %fusion.104), channel_id=1, source_target_pairs={{0,1},{1,0},{2,3},{3,2},{4,5},{5,4},{6,7},{7,6},{8,9},{9,8},{10,11... | collective-permute-start | bytes 1290248 | tf_op jit(solution)/shard_map/ppermute | solution.py:70
  594.5 47.7 %collective-permute-start.123 = (bf16[280,768]{1,0:T(8,128)(2,1)S(1)}, bf16[280,768]{1,0:T(8,128)(2,1)S(1)}, u32[]{:S(2)}, u32[]{:S(2)}) collective-permute-start(bf16[280,768]{1,0:T(8,128)(2,1)S(1)} %fusion.103), channel_id=1, source_target_pairs={{0,2},{1,3},{2,0},{3,1},{4,6},{5,7},{6,4},{7,5},{8,10},{9,11},{10,... | collective-permute-start | bytes 1290248 | tf_op jit(solution)/shard_map/ppermute | solution.py:70
  641.1 22.3 %collective-permute-start.74 = (bf16[256,1536]{1,0:T(8,128)(2,1)S(1)}, bf16[256,1536]{1,0:T(8,128)(2,1)S(1)}, u32[]{:S(2)}, u32[]{:S(2)}) collective-permute-start(bf16[256,1536]{1,0:T(8,128)(2,1)S(1)} %fusion.47), channel_id=1, source_target_pairs={{0,8},{4,12},{8,16},{12,20},{16,24},{20,28},{24,0},{28,4},{1,9},{5... | collective-permute-start | bytes 2359304 | tf_op jit(solution)/shard_map/ppermute | solution.py:70
  642.2 35.0 %collective-permute-start.60 = (bf16[256,1536]{1,0:T(8,128)(2,1)S(1)}, bf16[256,1536]{1,0:T(8,128)(2,1)S(1)}, u32[]{:S(2)}, u32[]{:S(2)}) collective-permute-start(bf16[256,1536]{1,0:T(8,128)(2,1)S(1)} %fusion.55), channel_id=1, source_target_pairs={{0,8},{4,12},{8,16},{12,20},{16,24},{20,28},{24,0},{28,4},{1,9},{5... | collective-permute-start | bytes 2359304 | tf_op jit(solution)/shard_map/ppermute | solution.py:70
  644.4 166.4 %collective-permute-start.113 = (bf16[8,2,48,1120]{3,2,0,1:T(8,128)(2,1)}, bf16[8,2,48,1120]{3,2,0,1:T(8,128)(2,1)}, u32[]{:S(2)}, u32[]{:S(2)}) collective-permute-start(bf16[8,2,48,1120]{3,2,0,1:T(8,128)(2,1)} %bitcast.596), channel_id=1, source_target_pairs={{0,2},{1,3},{2,0},{3,1},{4,6},{5,7},{6,4},{7,5},{8,10},{9,11},{10,... | collective-permute-start | bytes 5160968 | tf_op jit(solution)/shard_map/ppermute | solution.py:70
  722.5 53.9 %collective-permute-start.79 = (bf16[2,256,256]{2,1,0:T(8,128)(2,1)}, bf16[2,256,256]{2,1,0:T(8,128)(2,1)}, u32[]{:S(2)}, u32[]{:S(2)}) collective-permute-start(bf16[2,256,256]{2,1,0:T(8,128)(2,1)} %bitcast.679), channel_id=1, source_target_pairs={{0,2},{1,3},{2,0},{3,1},{4,6},{5,7},{6,4},{7,5},{8,10},{9,11},{10,... | collective-permute-start | bytes 786440 | tf_op jit(solution)/shard_map/ppermute | solution.py:70
  729.4 114.9 %collective-permute-start.99 = (bf16[4,2,2,48,768]{4,3,0,1,2:T(8,128)(2,1)}, bf16[4,2,2,48,768]{4,3,0,1,2:T(8,128)(2,1)}, u32[]{:S(2)}, u32[]{:S(2)}) collective-permute-start(bf16[4,2,2,48,768]{4,3,0,1,2:T(8,128)(2,1)} %bitcast.600), channel_id=1, source_target_pairs={{0,4},{4,0},{8,12},{12,8},{16,20},{20,16},{24,28},{28,24},{1,5},{5... | collective-permute-start | bytes 3538952 | tf_op jit(solution)/shard_map/ppermute | solution.py:70
  729.4 117.7 %collective-permute-start.105 = (bf16[4,2,2,48,768]{4,3,0,2,1:T(8,128)(2,1)}, bf16[4,2,2,48,768]{4,3,0,2,1:T(8,128)(2,1)}, u32[]{:S(2)}, u32[]{:S(2)}) collective-permute-start(bf16[4,2,2,48,768]{4,3,0,2,1:T(8,128)(2,1)} %bitcast.599), channel_id=1, source_target_pairs={{0,4},{4,0},{8,12},{12,8},{16,20},{20,16},{24,28},{28,24},{1,5},{5... | collective-permute-start | bytes 3538952 | tf_op jit(solution)/shard_map/ppermute | solution.py:70
  773.7 64.2 %collective-permute-start.112 = (bf16[8,48,1120]{2,1,0:T(8,128)(2,1)S(1)}, bf16[8,48,1120]{2,1,0:T(8,128)(2,1)}, u32[]{:S(2)}, u32[]{:S(2)}) collective-permute-start(bf16[8,48,1120]{2,1,0:T(8,128)(2,1)S(1)} %fusion.87), channel_id=1, source_target_pairs={{0,2},{1,3},{2,0},{3,1},{4,6},{5,7},{6,4},{7,5},{8,10},{9,11},{10,... | collective-permute-start | bytes 2580488 | tf_op jit(solution)/shard_map/ppermute | solution.py:70
  814.0 25.8 %collective-permute-start.114 = (bf16[8,48,1120]{2,1,0:T(8,128)(2,1)S(1)}, bf16[8,48,1120]{2,1,0:T(8,128)(2,1)S(1)}, u32[]{:S(2)}, u32[]{:S(2)}) collective-permute-start(bf16[8,48,1120]{2,1,0:T(8,128)(2,1)S(1)} %fusion.88), channel_id=1, source_target_pairs={{0,1},{1,0},{2,3},{3,2},{4,5},{5,4},{6,7},{7,6},{8,9},{9,8},{10,11... | collective-permute-start | bytes 2580488 | tf_op jit(solution)/shard_map/ppermute | solution.py:70
  836.7 71.4 %collective-permute-start.87 = (bf16[4,2,2,48,1024]{4,3,0,1,2:T(8,128)(2,1)}, bf16[4,2,2,48,1024]{4,3,0,1,2:T(8,128)(2,1)}, u32[]{:S(2)}, u32[]{:S(2)}) collective-permute-start(bf16[4,2,2,48,1024]{4,3,0,1,2:T(8,128)(2,1)} %bitcast.598), channel_id=1, source_target_pairs={{0,4},{4,0},{8,12},{12,8},{16,20},{20,16},{24,28},{28,24},{1,5},{5... | collective-permute-start | bytes 4718600 | tf_op jit(solution)/shard_map/ppermute | solution.py:70
  837.9 73.6 %collective-permute-start.93 = (bf16[4,2,2,48,1024]{4,3,0,2,1:T(8,128)(2,1)}, bf16[4,2,2,48,1024]{4,3,0,2,1:T(8,128)(2,1)}, u32[]{:S(2)}, u32[]{:S(2)}) collective-permute-start(bf16[4,2,2,48,1024]{4,3,0,2,1:T(8,128)(2,1)} %bitcast.597), channel_id=1, source_target_pairs={{0,4},{4,0},{8,12},{12,8},{16,20},{20,16},{24,28},{28,24},{1,5},{5... | collective-permute-start | bytes 4718600 | tf_op jit(solution)/shard_map/ppermute | solution.py:70
  840.1 47.8 %collective-permute-start.120 = (bf16[1,2,48,1120]{3,2,0,1:T(8,128)(2,1)S(1)}, bf16[1,2,48,1120]{3,2,0,1:T(8,128)(2,1)S(1)}, u32[]{:S(2)}, u32[]{:S(2)}) collective-permute-start(bf16[1,2,48,1120]{3,2,0,1:T(8,128)(2,1)S(1)} %get-tuple-element.74), channel_id=1, source_target_pairs={{0,24},{4,28},{8,0},{12,4},{16,8},{20,12},{24,16},{28,20},{1,25},{... | collective-permute-start | bytes 645128 | tf_op jit(solution)/shard_map/ppermute | solution.py:190
  844.3 42.6 %collective-permute-start.119 = (bf16[1,2,48,1120]{3,2,0,1:T(8,128)(2,1)S(1)}, bf16[1,2,48,1120]{3,2,0,1:T(8,128)(2,1)S(1)}, u32[]{:S(2)}, u32[]{:S(2)}) collective-permute-start(bf16[1,2,48,1120]{3,2,0,1:T(8,128)(2,1)S(1)} %get-tuple-element.75), channel_id=1, source_target_pairs={{0,20},{4,24},{8,28},{12,0},{16,4},{20,8},{24,12},{28,16},{1,21},{... | collective-permute-start | bytes 645128 | tf_op jit(solution)/shard_map/ppermute | solution.py:190
  910.3 26.8 %collective-permute-start.88 = (bf16[4,2,48,1024]{3,2,0,1:T(8,128)(2,1)S(1)}, bf16[4,2,48,1024]{3,2,0,1:T(8,128)(2,1)S(1)}, u32[]{:S(2)}, u32[]{:S(2)}) collective-permute-start(bf16[4,2,48,1024]{3,2,0,1:T(8,128)(2,1)S(1)} %fusion.91), channel_id=1, source_target_pairs={{0,1},{1,0},{2,3},{3,2},{4,5},{5,4},{6,7},{7,6},{8,9},{9,8},{10,11... | collective-permute-start | bytes 2359304 | tf_op jit(solution)/shard_map/ppermute | solution.py:70
  913.8 22.0 %collective-permute-start.94 = (bf16[4,2,48,1024]{3,2,0,1:T(8,128)(2,1)S(1)}, bf16[4,2,48,1024]{3,2,0,1:T(8,128)(2,1)S(1)}, u32[]{:S(2)}, u32[]{:S(2)}) collective-permute-start(bf16[4,2,48,1024]{3,2,0,1:T(8,128)(2,1)S(1)} %fusion.92), channel_id=1, source_target_pairs={{0,2},{1,3},{2,0},{3,1},{4,6},{5,7},{6,4},{7,5},{8,10},{9,11},{10,... | collective-permute-start | bytes 2359304 | tf_op jit(solution)/shard_map/ppermute | solution.py:70
  (222 other events, 2421.8 us)

commit v2 on v1

v2 whole, which is shorter than its diff:
```python
import jax
import jax.numpy as jnp
from jax import lax
from jax.sharding import PartitionSpec as P

D = 1536
HEADS = 12
KV_HEADS = 2
HEAD = 128
DOCS = 5


EPS = 1e-06
F32 = jnp.float32
LOW = jnp.bfloat16


def turn(values, cosine, sine):
    half = values.shape[-1] // 2
    first = values[..., :half]
    second = values[..., half:]
    cosine = cosine[:, None, :]
    sine = sine[:, None, :]
    return jnp.concatenate(
        [first * cosine - second * sine, second * cosine + first * sine], axis=-1
    )


def unturn(grads, cosine, sine):
    half = grads.shape[-1] // 2
    first = grads[..., :half]
    second = grads[..., half:]
    cosine = cosine[:, None, :]
    sine = sine[:, None, :]
    return jnp.concatenate(
        [first * cosine + second * sine, second * cosine - first * sine], axis=-1
    )


def score_block(query_rot, key_all, allowed):
    tokens = query_rot.shape[0]
    grouped = query_rot.reshape(tokens, KV_HEADS, HEADS // KV_HEADS, HEAD)
    keyed = key_all.reshape(key_all.shape[0], KV_HEADS, HEAD)
    scores = jnp.einsum(
        "tkgd,skd->kgts", grouped, keyed, preferred_element_type=F32
    ) * HEAD ** (-0.5)
    return jnp.where(allowed[None, None], scores, -1e30)


def norm_back(grad_normed, hidden, inverse, gain):
    scaled = grad_normed * gain
    grad_gain = jnp.sum(grad_normed * hidden * inverse, axis=0)
    grad_hidden = inverse * scaled - hidden * inverse**3 * jnp.mean(
        scaled * hidden, axis=1, keepdims=True
    )
    return (grad_gain, grad_hidden)


def hold(value, *others):
    for other in others:
        first = other[(0,) * other.ndim]
        value = jnp.where(first != first, jnp.zeros_like(value), value)
    return value


class Line:
    def __init__(self, axis, size, stride):
        self.axis, self.size, self.stride = axis, size, stride
        total = lax.axis_size(axis)
        self.place = (lax.axis_index(axis) // stride) % size
        self.up = []
        for i in range(total):
            place = (i // stride) % size
            self.up.append((i, i + ((place + 1) % size - place) * stride))

    def shift(self, value):
        return lax.ppermute(value, self.axis, self.up)

    def ring(self, value):
        parts = [value]
        for _ in range(self.size - 1):
            parts.append(self.shift(parts[-1]))
        return parts

    def ordered(self, parts, dim):
        if self.size == 2:
            first = self.place == 0
            return jnp.stack(
                [jnp.where(first, parts[0], parts[1]), jnp.where(first, parts[1], parts[0])], dim
            )
        shape = parts[0].shape
        whole = jnp.zeros(shape[:dim] + (self.size,) + shape[dim:], parts[0].dtype)
        for step, part in enumerate(parts):
            whole = lax.dynamic_update_slice_in_dim(
                whole, jnp.expand_dims(part, dim), (self.place - step) % self.size, dim
            )
        return whole

    def gather(self, value, dim):
        return self.ordered(self.ring(value), dim)

    def direct(self, blocks, dim, *waits):
        total = self.pick(blocks, dim, 0).astype(F32)
        sent = [hold(self.pick(blocks, dim, -step), *waits) for step in range(1, self.size)]
        for step, block in enumerate(sent, 1):
            total = total + lax.ppermute(
                block, self.axis, [(i, self.there(i, step)) for i in range(len(self.up))]
            ).astype(F32)
        return total

    def there(self, i, step):
        place = (i // self.stride) % self.size
        return i + ((place + step) % self.size - place) * self.stride

    def pick(self, blocks, dim, step):
        return lax.dynamic_index_in_dim(blocks, (self.place - step) % self.size, dim, False)

    def scatter(self, blocks, dim, kind=LOW):
        total = self.pick(blocks, dim, 1)
        for step in range(2, self.size + 1):
            total = self.shift(total.astype(kind)).astype(F32)
            total = total + self.pick(blocks, dim, step).astype(F32)
        return total


def per_device(
    layer_input,
    cotangent,
    doc_lengths,
    attention_gain,
    query_weight,
    key_weight,
    value_weight,
    query_bias,
    key_bias,
    value_bias,
    output_weight,
    feedforward_gain,
    gate_weight,
    up_weight,
    down_weight,
):
    tokens = layer_input.shape[0]
    n_dp = lax.axis_size("dp")
    n_ctx = lax.axis_size("ctx")
    here = lax.axis_index("dp")
    which = lax.axis_index("ctx")
    chip = Line("dp", n_dp // 2, 2)
    core = Line("dp", 2, 1)
    outer = Line("ctx", n_ctx // 2, 2)
    inner = Line("ctx", 2, 1)
    row = Line("ctx", n_ctx, 1)
    rows = query_weight.shape[0]
    kv_width = KV_HEADS * HEAD

    def plane_gather(value, first, dim):
        if first:
            return outer.gather(inner.gather(value, dim), dim)
        return inner.gather(outer.gather(value, dim), dim + 1)

    def plane_scatter(blocks, first, dim, kind=LOW):
        if first:
            return outer.scatter(inner.scatter(blocks, dim + 1, kind), dim, kind)
        return inner.scatter(outer.scatter(blocks, dim, kind), dim, kind)

    def plane_gather_halves(value, cut, dim):
        return (
            plane_gather(value[..., :cut], True, dim),
            plane_gather(value[..., cut:], False, dim),
        )

    def plane_sums(array, cut, *waits):
        blocks = array.reshape((n_dp // 2, 2, n_ctx // 2, 2, rows) + array.shape[1:])
        blocks = hold(core.scatter(blocks, 1).astype(LOW), *waits)
        return [
            plane_scatter(part, first, 1).astype(LOW)
            for part, first in ((blocks[..., :cut], True), (blocks[..., cut:], False))
        ]

    few = key_bias.shape[0]
    tile = jnp.stack(
        [attention_gain, feedforward_gain, query_bias]
        + [jnp.pad(part, (0, rows - few)) for part in (key_bias, value_bias)],
        axis=1,
    )
    tile = jnp.pad(tile, ((0, 0), (0, HEAD - tile.shape[1])))
    mixed_width = D + 2 * kv_width
    half = D + kv_width
    ring_in = chip.ring(
        jnp.concatenate([query_weight, key_weight, value_weight, output_weight, tile], axis=1)
    )
    plane_in = plane_gather_halves(chip.ordered(ring_in, 0), half, 1)
    weight_qk, weight_rest = [core.gather(part, 1).reshape(D, -1) for part in plane_in]
    weight_v = weight_rest[:, :kv_width]
    weight_o = weight_rest[:, kv_width : kv_width + D]
    vectors = weight_rest[:, kv_width + D :].astype(F32).T
    gain_a, gain_f, bias_q = vectors[0], vectors[1], vectors[2]
    bias_k, bias_v = (
        vectors[i].reshape(-1, rows)[:, :few].reshape(-1) for i in (3, 4)
    )

    real = gate_weight.shape[1] // n_dp
    width = -(-real // HEAD) * HEAD
    weight_d = jnp.concatenate(
        [part.reshape(real, D // 2) for part in plane_gather_halves(down_weight, D // 2, 0)],
        axis=1,
    )
    weight_d = jnp.pad(weight_d, ((0, width - real), (0, 0)))
    units = jnp.stack(
        [gate_weight.reshape(rows, n_dp, real), up_weight.reshape(rows, n_dp, real)]
    ).transpose(2, 0, 1, 3)
    units = jnp.pad(units, ((0, 0), (0, 0), (0, 0), (0, width - real)))
    units = lax.all_to_all(hold(units, ring_in[-1]), "dp", 0, 0, tiled=True)
    units = units.transpose(1, 0, 2, 3).reshape(2 * n_dp * rows, width)
    units_all = lax.all_gather(hold(units, weight_qk), "ctx", axis=0, tiled=True)
    units_all = units_all.reshape(n_ctx, 2, n_dp * rows, width)
    weight_g, weight_u = (units_all[:, i].reshape(D, width) for i in (0, 1))
    place = jnp.arange(D, dtype=jnp.int32)
    source = ((place // rows) % n_dp * n_ctx + place // (rows * n_dp)) * rows + place % rows
    order = (place[:, None] == source[None, :]).astype(LOW)

    upstream_all = lax.all_gather(hold(cotangent, ring_in[-1]), "dp", axis=0, tiled=True)

    whole = tokens * n_ctx
    places = jnp.arange(whole, dtype=jnp.int32)
    lengths = doc_lengths[0]
    entry = jnp.arange(DOCS, dtype=jnp.int32)
    ends = jnp.sum(jnp.where(entry[None, :] <= entry[:, None], lengths[None, :], 0), axis=1)
    starts = ends - lengths
    segment = jnp.sum((places[:, None] >= ends[None, :]).astype(jnp.int32), axis=1)
    chosen = (segment[:, None] == entry[None, :]).astype(jnp.int32)
    offsets = places - jnp.sum(chosen * starts[None, :], axis=1)
    padded = segment == DOCS - 1
    first_row = which * tokens
    mine = lax.dynamic_slice_in_dim(places, first_row, tokens)
    my_segment = lax.dynamic_slice_in_dim(segment, first_row, tokens)
    my_offsets = lax.dynamic_slice_in_dim(offsets, first_row, tokens)
    allowed = (places[None, :] <= mine[:, None]) & (segment[None, :] == my_segment[:, None])
    allowed = allowed & (jnp.logical_not(padded)[None, :] | (places[None, :] == mine[:, None]))
    freqs = 10000.0 ** (-jnp.arange(0, HEAD // 2, dtype=F32) * 2.0 / HEAD)
    angles = my_offsets.astype(F32)[:, None] * freqs[None, :]
    cosine = jnp.cos(angles)
    sine = jnp.sin(angles)

    hidden = layer_input.astype(F32)
    inverse = lax.rsqrt(jnp.mean(hidden * hidden, axis=1, keepdims=True) + EPS)
    normed = (hidden * inverse * gain_a).astype(LOW)
    projected = jnp.dot(normed, weight_qk, preferred_element_type=F32)
    queries = projected[:, :D] + bias_q
    keys = projected[:, D:] + bias_k
    values = jnp.dot(normed, weight_v, preferred_element_type=F32) + bias_v
    query_rot = turn(queries.reshape(tokens, HEADS, HEAD), cosine, sine).astype(LOW)
    key_rot = (
        turn(keys.reshape(tokens, KV_HEADS, HEAD), cosine, sine)
        .astype(LOW)
        .reshape(tokens, kv_width)
    )
    value_low = values.astype(LOW)
    both = jnp.concatenate([key_rot, value_low], axis=1)
    both_all = jnp.zeros((n_ctx,) + both.shape, LOW)
    for step in range(n_ctx):
        arrived = both
        if step:
            arrived = lax.ppermute(both, "ctx", [(i, (i + step) % n_ctx) for i in range(n_ctx)])
        both_all = lax.dynamic_update_slice_in_dim(
            both_all, arrived[None], (which - step) % n_ctx, 0
        )
    both_all = both_all.reshape(whole, 2 * kv_width)
    key_all, value_all = both_all[:, :kv_width], both_all[:, kv_width:]
    scores = score_block(query_rot, key_all, allowed)
    top = jnp.max(scores, axis=-1, keepdims=True)
    weights = jnp.exp(scores - top)
    totals = jnp.sum(weights, axis=-1, keepdims=True)
    probs = weights / totals
    log_total = top + jnp.log(totals)
    value_heads = value_all.reshape(whole, KV_HEADS, HEAD)
    mixed = jnp.einsum(
        "kgts,skd->tkgd", probs.astype(LOW), value_heads, preferred_element_type=F32
    )
    mixed_low = mixed.reshape(tokens, D).astype(LOW)
    middle = hidden + jnp.dot(mixed_low, weight_o, preferred_element_type=F32)

    inverse2 = lax.rsqrt(jnp.mean(middle * middle, axis=1, keepdims=True) + EPS)
    normed2 = (middle * inverse2 * gain_f).astype(LOW)
    normed2 = jnp.dot(normed2, order, preferred_element_type=F32).astype(LOW)
    upstream_own = [
        lax.dynamic_slice_in_dim(
            upstream_all, ((chip.place - step) % chip.size * 2 + core.place) * tokens, tokens, 0
        )
        for step in range(n_dp // 2)
    ]
    upstream_other = [
        lax.dynamic_slice_in_dim(
            upstream_all, ((chip.place - step) % chip.size * 2 + 1 - core.place) * tokens, tokens, 0
        )
        for step in range(n_dp // 2)
    ]
    upstream = [
        jnp.concatenate([own, other], axis=0) for own, other in zip(upstream_own, upstream_other)
    ]
    grad_actives = [
        jnp.einsum("td,fd->tf", back, weight_d, preferred_element_type=F32).astype(LOW)
        for back in upstream
    ]
    normed2 = hold(normed2, weight_g, weight_u, *grad_actives[:1])
    inputs_own = chip.ring(normed2)

    def both_cores(part, *waits):
        part = hold(part, *waits)
        return jnp.concatenate([part, core.shift(part)], axis=0)

    def core_sum(part):
        return part[:tokens] + core.shift(part[tokens:].astype(LOW)).astype(F32)

    inputs, actives, grad_gates, grad_upwards, grads, kept, grad_sums, outs = ([] for _ in range(8))
    out_all = jnp.zeros((n_dp * tokens, D), LOW)
    for step, fed in enumerate(inputs_own):
        fed = both_cores(fed, *actives[-1:])
        inputs.append(fed)
        grad_active = grad_actives[step].astype(F32)
        if step > 1:
            fed = hold(fed, *kept, *grad_sums[1:], *outs[-1:])
        gate = jnp.dot(fed, weight_g, preferred_element_type=F32)
        upward = jnp.dot(fed, weight_u, preferred_element_type=F32)
        sigmoid_gate = jax.nn.sigmoid(gate)
        active = (gate * sigmoid_gate * upward).astype(LOW)
        grad_gate = (
            grad_active * upward * sigmoid_gate * (1.0 + gate * (1.0 - sigmoid_gate))
        ).astype(LOW)
        grad_upward = (grad_active * gate * sigmoid_gate).astype(LOW)
        grads.append(
            jnp.einsum("tf,df->td", grad_gate, weight_g, preferred_element_type=F32)
            + jnp.einsum("tf,df->td", grad_upward, weight_u, preferred_element_type=F32)
        )
        kept.append(core_sum(grads[-1]))
        if step == 1:
            grad_sums.append(kept[1])
        if step > 1:
            arrived = chip.shift(grad_sums[-1].astype(LOW)).astype(F32)
            grad_sums.append(arrived + kept[step])
        actives.append(active)
        outs.append(jnp.dot(active, weight_d, preferred_element_type=F32).astype(LOW))
        for side in range(2):
            index = (chip.place - step) % chip.size * 2 + (core.place + side) % 2
            piece = outs[-1][side * tokens : (side + 1) * tokens]
            out_all = lax.dynamic_update_slice_in_dim(out_all, piece, index * tokens, 0)
        grad_gates.append(grad_gate)
        grad_upwards.append(grad_upward)
    arrived = chip.shift(grad_sums[-1].astype(LOW)).astype(F32)
    grad_normed2 = (arrived + kept[0]).astype(LOW)

    fed_all = jnp.concatenate(inputs, axis=0)
    part_gate = jnp.einsum(
        "td,tf->df",
        fed_all,
        hold(jnp.concatenate(grad_gates, axis=0), grad_sums[-1]),
        preferred_element_type=F32,
    ).astype(LOW)
    def plane_sum(part):
        total = lax.psum_scatter(part, "ctx", scatter_dimension=0, tiled=True)
        return total.reshape(n_dp, rows, width)


    grad_normed2 = hold(grad_normed2, part_gate)
    grad_normed2 = jnp.einsum("te,de->td", grad_normed2, order, preferred_element_type=F32)
    grad_gain_f, grad_middle = norm_back(grad_normed2, middle, inverse2, gain_f)
    grad_middle = grad_middle + cotangent.astype(F32)
    grad_attention = grad_middle.astype(LOW)
    part_up = jnp.einsum(
        "td,tf->df",
        fed_all,
        hold(jnp.concatenate(grad_upwards, axis=0), grad_attention),
        preferred_element_type=F32,
    ).astype(LOW)
    sums = jnp.stack([plane_sum(part_gate), plane_sum(part_up)], axis=1)
    part_output = jnp.einsum(
        "td,te->de", mixed_low, grad_attention, preferred_element_type=F32
    ).astype(LOW)
    grad_mixed = jnp.einsum(
        "te,de->td", grad_attention, weight_o, preferred_element_type=F32
    ).astype(LOW)
    grad_heads = grad_mixed.reshape(tokens, KV_HEADS, HEADS // KV_HEADS, HEAD)
    probs = jnp.exp(score_block(query_rot, key_all, allowed) - log_total)
    grad_probs = jnp.einsum(
        "tkgd,skd->kgts", grad_heads, value_heads, preferred_element_type=F32
    )
    grad_scores = (
        probs * (grad_probs - jnp.sum(probs * grad_probs, axis=-1, keepdims=True))
    ).astype(LOW)
    grad_value_part = jnp.einsum(
        "kgts,tkgd->skd", probs.astype(LOW), grad_heads, preferred_element_type=F32
    )
    key_heads = key_all.reshape(whole, KV_HEADS, HEAD)
    grouped = query_rot.reshape(tokens, KV_HEADS, HEADS // KV_HEADS, HEAD)
    grad_query_rot = jnp.einsum(
        "kgts,skd->tkgd", grad_scores, key_heads, preferred_element_type=F32
    ) * HEAD ** (-0.5)
    grad_key_part = jnp.einsum(
        "kgts,tkgd->skd", grad_scores, grouped, preferred_element_type=F32
    ) * HEAD ** (-0.5)
    both_part = jnp.concatenate(
        [grad_key_part.reshape(whole, kv_width), grad_value_part.reshape(whole, kv_width)], axis=1
    )
    both_part = both_part.astype(LOW).reshape(n_ctx, tokens, 2 * kv_width)
    both_sum = row.direct(both_part, 0)
    grad_key_rot = both_sum[:, :kv_width]
    grad_values = both_sum[:, kv_width:].astype(LOW)
    part_out = lax.psum_scatter(out_all, "dp", scatter_dimension=0, tiled=True)
    sums = lax.all_to_all(hold(sums, both_part), "dp", 0, 0, tiled=True)
    gate_weight_grad = sums[:, 0, :, :real].transpose(1, 0, 2).reshape(rows, -1).astype(F32)
    up_weight_grad = sums[:, 1, :, :real].transpose(1, 0, 2).reshape(rows, -1).astype(F32)
    plane_output = plane_sums(part_output, D // 2, grad_key_rot)
    grad_keys = (
        unturn(grad_key_rot.reshape(tokens, KV_HEADS, HEAD), cosine, sine)
        .reshape(tokens, kv_width)
        .astype(LOW)
    )
    grad_queries = (
        unturn(grad_query_rot.reshape(tokens, HEADS, HEAD), cosine, sine)
        .reshape(tokens, D)
        .astype(LOW)
    )
    joined = jnp.concatenate([grad_queries, grad_keys, grad_values], axis=1)
    grad_normed = jnp.einsum(
        "te,de->td", joined[:, :half], weight_qk, preferred_element_type=F32
    ) + jnp.einsum("te,de->td", grad_values, weight_v, preferred_element_type=F32)
    grad_gain_a, grad_hidden = norm_back(grad_normed, hidden, inverse, gain_a)
    input_grad = grad_middle + grad_hidden
    part_in = jnp.einsum("td,te->de", normed, joined, preferred_element_type=F32).astype(LOW)
    bias_sums = jnp.sum(joined.astype(F32), axis=0)
    short = [
        jnp.pad(part.reshape(-1, few), ((0, 0), (0, rows - few))).reshape(D)
        for part in (bias_sums[D : D + kv_width], bias_sums[D + kv_width :])
    ]
    tile = jnp.stack([grad_gain_a, grad_gain_f, bias_sums[:D]] + short, axis=1).astype(LOW)
    tile = jnp.pad(tile, ((0, 0), (0, HEAD - tile.shape[1])))
    part_in = jnp.concatenate([part_in, tile], axis=1)
    part_down = jnp.einsum(
        "tf,td->fd",
        hold(jnp.concatenate(actives, axis=0), part_in),
        jnp.concatenate(upstream, axis=0),
        preferred_element_type=F32,
    ).astype(LOW)[:real]
    part_down = lax.psum_scatter(part_down, "ctx", scatter_dimension=0, tiled=True)
    plane_grads = plane_sums(part_in, mixed_width // 2, sums)
    plane_grads = jnp.concatenate(plane_grads + plane_output, axis=-1)
    layer_output = (middle + hold(part_out, plane_grads).astype(F32)).astype(LOW)
    down_weight_grad = hold(part_down, plane_grads).astype(F32)
    in_grads = chip.scatter(plane_grads, 0)
    output_weight_grad = in_grads[:, mixed_width + HEAD :]
    small = in_grads[:, mixed_width : mixed_width + HEAD].T
    return (
        layer_output,
        input_grad,
        small[0],
        in_grads[:, :D],
        in_grads[:, D : D + kv_width],
        in_grads[:, D + kv_width : mixed_width],
        small[2],
        small[3, :few],
        small[4, :few],
        output_weight_grad,
        small[1],
        gate_weight_grad,
        up_weight_grad,
        down_weight_grad,
    )


def solution(mesh):
    split = P(("dp", "ctx"), None)
    vector = P(("dp", "ctx"))
    placed = (
        split,
        split,
        P("dp", None),
        vector,
        split,
        split,
        split,
        vector,
        vector,
        vector,
        split,
        vector,
        split,
        split,
        split,
    )
    results = (
        split,
        split,
        vector,
        split,
        split,
        split,
        vector,
        vector,
        vector,
        split,
        vector,
        split,
        split,
        split,
    )
    return jax.shard_map(
        per_device, mesh=mesh, in_specs=placed, out_specs=results, check_vma=False
    )
```

time: 986 us -> 720 us (0.73)
  waiting for transfers between devices: 463 us -> 231 us
  between operations: 3.73 us -> 46 us
  local copies, waits for them, and re-layouts: 179 us -> 144 us
  starting transfers between devices: 81.5 us -> 50.9 us
    ppermute x112 -> x40, waiting for transfers between devices: 379 us -> 188 us  [shift(): return lax.ppermute(value, self.axis, self.up)]
    ppermute x14 -> x6, waiting for transfers between devices: 83.9 us -> 8.33 us  [the longest x3 5.79 us: per_device(): lax.ppermute(both, 'ctx', [(i, (i + step) % n_ctx) for i in range(n_ctx)])]
    ppermute x112 -> x40, starting transfers between devices: 71.2 us -> 33.3 us  [shift(): return lax.ppermute(value, self.axis, self.up)]
    all_to_all x0 -> x2, waiting for transfers between devices: none -> 30 us  [the longest x1 16.9 us: per_device(): units = lax.all_to_all(hold(units, ring_in[-1]), 'dp', 0, 0, tiled=True)]
    dynamic_slice x14 -> x4, local copies, waits for them, and re-layouts: 25.7 us -> 6.25 us  [pick(): lax.dynamic_index_in_dim(blocks, (self.place - step) % self.size, dim, Fa...]
    slice x14 -> x46, local copies, waits for them, and re-layouts: 16.7 us -> 36.2 us  [the longest x22 15 us: hold(): first = other[(0,) * other.ndim]]
    convert_element_type x11 -> x4, local copies, waits for them, and re-layouts: 21.5 us -> 4.61 us  [the longest x2 2.3 us: per_device(): sums[:, 1, :, :real].transpose(1, 0, 2).reshape(rows, -1).astype(F32)]
    add x31 -> x5, other arithmetic: 17.1 us -> 1.87 us  [scatter(): total = total + self.pick(blocks, dim, step).astype(F32)]
  transfers between devices with their start and end apart: 126 -> 54, of which waited for: 68 -> 28; matrix products, arithmetic and copies ran while one was open for 42% -> 48% of each run, Pallas kernels for 0% -> 0%
where the time goes in v2:
time: 720 us; the launch traced here: 711 us
  waiting for transfers between devices  231 us (32%)
  matrix products  162 us (22%)
  local copies, waits for them, and re-layouts  144 us (20%)
  other arithmetic  77 us (11%)
  starting transfers between devices  50.9 us (7%)
  between operations  46 us (6%)
    ppermute x40, waiting for transfers between devices, shift(): return lax.ppermute(value, self.axis, self.up)  188 us
    unnamed x248, local copies, waits for them, and re-layouts  42.5 us
    ppermute x40, starting transfers between devices, shift(): return lax.ppermute(value, self.axis, self.up)  33.3 us
    another operation x19, other arithmetic, ordered(): jnp.stack([jnp.where(first, parts[0], parts[1]), jnp.where(first, parts[1...  23.1 us
    all_to_all x1, waiting for transfers between devices, per_device(): units = lax.all_to_all(hold(units, ring_in[-1]), 'dp', 0, 0, tiled=True)  16.9 us
    dot_general x4, matrix products, per_device(): jnp.einsum('td,fd->tf', back, weight_d, preferred_element_type=F32)  16.9 us
    slice x22, local copies, waits for them, and re-layouts, hold(): first = other[(0,) * other.ndim]  15 us
  transfers between devices with their start and end apart: 54, of which 28 were waited for; matrix products, arithmetic and copies ran while one was open for 48% of the time, Pallas kernels for 0%

profile of v2, /device:TPU:0, one launch (start us, length us, event | category | flops | bytes accessed | tf_op | source)
XLA Modules:
  0.0 711.3 jit_solution(11720698998528188707)
XLA Ops:
  12.2 3.1 collective-permute-start
  20.3 5.2 collective-permute-done
  25.9 11.0 %collective-permute-done.1 = bf16[48,3712]{1,0:T(8,128)(2,1)S(1)} collective-permute-done((bf16[48,3712]{1,0:T(8,128)(2,1)S(1)}, bf16[48,3712]{1,0:T(8,128)(2,1)S(1)}, u32[]{:S(2)}, u32[]{:S(2)}) %collective-permute-start.1) | collective-permute-done | bytes 356384 | tf_op jit(solution)/shard_map/ppermute | solution.py:77
  37.1 10.2 %collective-permute-done.2 = bf16[48,3712]{1,0:T(8,128)(2,1)S(1)} collective-permute-done((bf16[48,3712]{1,0:T(8,128)(2,1)S(1)}, bf16[48,3712]{1,0:T(8,128)(2,1)S(1)}, u32[]{:S(2)}, u32[]{:S(2)}) %collective-permute-start.2) | collective-permute-done | bytes 356384 | tf_op jit(solution)/shard_map/ppermute | solution.py:77
  54.9 3.5 stack_reshape.21
  62.5 3.8 collective-permute-done.6
  68.7 11.7 %collective-permute-done.3 = bf16[4,48,1920]{2,1,0:T(8,128)(2,1)S(1)} collective-permute-done((bf16[4,48,1920]{2,1,0:T(8,128)(2,1)S(1)}, bf16[4,48,1920]{2,1,0:T(8,128)(2,1)S(1)}, u32[]{:S(2)}, u32[]{:S(2)}) %collective-permute-start.3) | collective-permute-done | bytes 737312 | tf_op jit(solution)/shard_map/ppermute | solution.py:77
  86.4 19.4 %collective-permute-done.7 = bf16[4,2,48,1792]{3,2,0,1:T(8,128)(2,1)S(1)} collective-permute-done((bf16[4,2,48,1792]{3,2,0,1:T(8,128)(2,1)S(1)}, bf16[4,2,48,1792]{3,2,0,1:T(8,128)(2,1)S(1)}, u32[]{:S(2)}, u32[]{:S(2)}) %collective-permute-start.7) | collective-permute-done | bytes 1376288 | tf_op jit(solution)/shard_map/ppermute | solution.py:77
  112.7 4.3 all-to-all-start
  142.2 16.9 %all-to-all-done = bf16[8,2,48,1152]{3,2,1,0:T(8,128)(2,1)} async-done(((bf16[8,2,48,1152]{3,2,1,0:T(8,128)(2,1)}), bf16[8,2,48,1152]{3,2,1,0:T(8,128)(2,1)}, u32[]{:S(2)}, u32[]{:S(2)}) %all-to-all-start) | async-done | bytes 1769504 | tf_op jit(solution)/shard_map/all_to_all | solution.py:213
  169.2 4.9 fusion.202
  185.2 3.1 copy.215
  193.4 5.7 collective-permute-done.10
  219.9 3.8 fusion.98
  223.7 4.1 multiply_reduce_fusion.2
  243.7 4.7 all-gather.5.cloned.1.call-done
  248.4 3.6 fusion.217
  268.1 3.7 fusion.62
  273.8 12.3 %collective-permute-done.17 = bf16[256,1536]{1,0:T(8,128)(2,1)S(1)} collective-permute-done((bf16[256,1536]{1,0:T(8,128)(2,1)S(1)}, bf16[256,1536]{1,0:T(8,128)(2,1)S(1)}, u32[]{:S(2)}, u32[]{:S(2)}) %collective-permute-start.17) | collective-permute-done | bytes 786464 | tf_op jit(solution)/shard_map/ppermute | solution.py:77
  291.6 3.6 fusion.115
  295.2 3.6 fusion.116
  298.9 6.6 multiply_convert_fusion.6
  331.0 4.0 multiply_convert_fusion.3
  348.6 11.1 %collective-permute-done.25 = bf16[256,1536]{1,0:T(8,128)(2,1)S(1)} collective-permute-done((bf16[256,1536]{1,0:T(8,128)(2,1)S(1)}, bf16[256,1536]{1,0:T(8,128)(2,1)S(1)}, u32[]{:S(2)}, u32[]{:S(2)}) %collective-permute-start.25) | collective-permute-done | bytes 786464 | tf_op jit(solution)/shard_map/ppermute | solution.py:77
  368.8 4.1 multiply_convert_fusion.1
  377.7 7.1 collective-permute-done.27
  387.0 10.2 %convolution_convert_fusion.3 = bf16[1536,1152]{1,0:T(8,128)(2,1)} fusion(bf16[2048,1536]{1,0:T(8,128)(2,1)S(1)} %constant_dynamic-update-slice_fusion.5, bf16[512,1152]{1,0:T(8,128)(2,1)S(1)} %copy-done.100, bf16[512,1152]{1,0:T(8,128)(2,1)S(1)} %copy-done.98, bf16[512,1152]{1,0:T(8,128)(2,1)S(1)} %copy-done.96, bf16[512,1152]{1,0:T(8,128)(2,1)S(1)} %copy-done.94, ...), kind=kOutput, calls=%fused_computation.19 | convolution fusion | flops 7270760448 | bytes 14548993 | tf_op jit(solution)/shard_map/td,tf->df/dot_general | solution.py:353
  399.8 17.3 %collective-permute-done.29 = bf16[256,1536]{1,0:T(8,128)(2,1)S(1)} collective-permute-done((bf16[256,1536]{1,0:T(8,128)(2,1)S(1)}, bf16[256,1536]{1,0:T(8,128)(2,1)S(1)}, u32[]{:S(2)}, u32[]{:S(2)}) %collective-permute-start.29) | collective-permute-done | bytes 786464 | tf_op jit(solution)/shard_map/ppermute | solution.py:77
  417.1 4.0 multiply_reduce_fusion
  425.0 9.9 %convolution_convert_fusion.2 = bf16[1536,1152]{1,0:T(8,128)(2,1)} fusion(bf16[2048,1536]{1,0:T(8,128)(2,1)S(1)} %copy-done.86, bf16[512,1152]{1,0:T(8,128)(2,1)S(1)} %copy-done.108, bf16[512,1152]{1,0:T(8,128)(2,1)S(1)} %copy-done.106, bf16[512,1152]{1,0:T(8,128)(2,1)S(1)} %copy-done.104, bf16[512,1152]{1,0:T(8,128)(2,1)S(1)} %copy-done.102, pred[]{:T(512)} %bitcast.88), kind=kOutput, calls=%fused_computation.18 | convolution fusion | flops 7270760448 | bytes 14548993 | tf_op jit(solution)/shard_map/td,tf->df/dot_general | solution.py:369
  436.5 4.1 convolution_convert_fusion.5
  453.3 3.8 fusion.54
  457.4 8.3 %fusion.107 = bf16[1024,2,128]{0,2,1:T(8,128)(2,1)S(1)} fusion(bf16[256,2,6,128]{0,3,2,1:T(8,128)(2,1)S(1)} %bitcast.391, f32[2,6,256]{2,1,0:T(8,128)S(1)} %log_add_fusion, f32[2,1024,256,6]{2,1,3,0:T(8,128)} %copy-done, pred[256,1024]{0,1:T(8,128)(4,1)S(1)} %copy-done.7), kind=kOutput, calls=%fused_computation.204 | convolution fusion | flops 818151424 | bytes 14168064 | tf_op jit(solution)/shard_map/kgts,tkgd->skd/dot_general | solution.py:390
  472.7 6.8 fusion.1
  479.5 6.7 fusion.3
  488.9 3.2 fusion.110
  499.4 4.2 convolution_multiply_fusion
  517.6 4.6 fusion.119
  526.8 3.1 convolution_convert_fusion
  543.6 4.3 all-to-all-start.1
  548.2 12.4 %fusion.28 = bf16[1152,1536]{1,0:T(8,128)(2,1)S(1)} fusion(bf16[2048,1536]{1,0:T(8,128)(2,1)} %get-tuple-element.28, bf16[512,1152]{1,0:T(8,128)(2,1)} %get-tuple-element.71, bf16[512,1152]{1,0:T(8,128)(2,1)} %copy-done.90, bf16[512,1152]{1,0:T(8,128)(2,1)} %copy-done.89, bf16[512,1152]{1,0:T(8,128)(2,1)} %copy-done.88, pred[]{:T(512)} %bitcast.140), kind=kOutput, calls=%fused_computation.47 | convolution fusion | flops 7268990976 | bytes 14548993 | tf_op jit(solution)/shard_map/tf,td->fd/dot_general | solution.py:438
  574.3 9.2 %collective-permute-done.41 = bf16[4,2,48,768]{3,2,0,1:T(8,128)(2,1)S(1)} collective-permute-done((bf16[4,2,48,768]{3,2,0,1:T(8,128)(2,1)S(1)}, bf16[4,2,48,768]{3,2,0,1:T(8,128)(2,1)S(1)}, u32[]{:S(2)}, u32[]{:S(2)}) %collective-permute-start.41) | collective-permute-done | bytes 589856 | tf_op jit(solution)/shard_map/ppermute | solution.py:77
  587.4 13.1 %all-to-all-done.1 = bf16[8,2,48,1152]{3,2,1,0:T(8,128)(2,1)} async-done(((bf16[8,2,48,1152]{3,2,1,0:T(8,128)(2,1)}), bf16[8,2,48,1152]{3,2,1,0:T(8,128)(2,1)}, u32[]{:S(2)}, u32[]{:S(2)}) %all-to-all-start.1) | async-done | bytes 1769504 | tf_op jit(solution)/shard_map/all_to_all | solution.py:409
  612.4 25.1 %collective-permute-done.34 = bf16[4,2,48,1024]{3,2,0,1:T(8,128)(2,1)S(1)} collective-permute-done((bf16[4,2,48,1024]{3,2,0,1:T(8,128)(2,1)S(1)}, bf16[4,2,48,1024]{3,2,0,1:T(8,128)(2,1)S(1)}, u32[]{:S(2)}, u32[]{:S(2)}) %collective-permute-start.34) | collective-permute-done | bytes 786464 | tf_op jit(solution)/shard_map/ppermute | solution.py:77
  641.9 7.7 %collective-permute-done.40 = bf16[4,48,768]{2,1,0:T(8,128)(2,1)S(1)} collective-permute-done((bf16[4,48,768]{2,1,0:T(8,128)(2,1)S(1)}, bf16[4,48,768]{2,1,0:T(8,128)(2,1)S(1)}, u32[]{:S(2)}, u32[]{:S(2)}) %collective-permute-start.40) | collective-permute-done | bytes 294944 | tf_op jit(solution)/shard_map/ppermute | solution.py:77
  649.6 14.0 %collective-permute-done.35 = bf16[4,48,1024]{2,1,0:T(8,128)(2,1)S(1)} collective-permute-done((bf16[4,48,1024]{2,1,0:T(8,128)(2,1)S(1)}, bf16[4,48,1024]{2,1,0:T(8,128)(2,1)S(1)}, u32[]{:S(2)}, u32[]{:S(2)}) %collective-permute-start.35) | collective-permute-done | bytes 393248 | tf_op jit(solution)/shard_map/ppermute | solution.py:77
  681.0 8.9 %collective-permute-done.44 = bf16[48,3712]{1,0:T(8,128)(2,1)} collective-permute-done((bf16[48,3712]{1,0:T(8,128)(2,1)}, bf16[48,3712]{1,0:T(8,128)(2,1)}, u32[]{:S(2)}, u32[]{:S(2)}) %collective-permute-start.44) | collective-permute-done | bytes 356384 | tf_op jit(solution)/shard_map/ppermute | solution.py:77
  693.6 7.4 %collective-permute-done.45 = bf16[48,3712]{1,0:T(8,128)(2,1)S(1)} collective-permute-done((bf16[48,3712]{1,0:T(8,128)(2,1)S(1)}, bf16[48,3712]{1,0:T(8,128)(2,1)S(1)}, u32[]{:S(2)}, u32[]{:S(2)}) %collective-permute-start.45) | collective-permute-done | bytes 356384 | tf_op jit(solution)/shard_map/ppermute | solution.py:77
  (573 shorter events, 301.6 us)
Async XLA Ops:
  7.2 221.3 %all-gather.3.cloned.1.call-start = ((), (), s32[]{:S(2)}) async-start(), calls=%async_computation.6 | async-start | bytes 7077888 | tf_op jit(solution)/shard_map/all_gather | solution.py:222
  12.2 13.4 %collective-permute-start = (bf16[48,3712]{1,0:T(8,128)(2,1)S(1)}, bf16[48,3712]{1,0:T(8,128)(2,1)S(1)}, u32[]{:S(2)}, u32[]{:S(2)}) collective-permute-start(bf16[48,3712]{1,0:T(8,128)(2,1)S(1)} %constant_dynamic-update-slice_fusion), channel_id=1, source_target_pairs={{0,8},{4,12},{8,16},{12,20},{16,24},{20,28},{24,0},{28,4},{1,9},{5... | collective-permute-start | bytes 1069064 | tf_op jit(solution)/shard_map/ppermute | solution.py:77
  17.3 65.6 %collective-permute-start.12 = (bf16[280,768]{1,0:T(8,128)(2,1)}, bf16[280,768]{1,0:T(8,128)(2,1)}, u32[]{:S(2)}, u32[]{:S(2)}) collective-permute-start(bf16[280,768]{1,0:T(8,128)(2,1)} %get-tuple-element.112), channel_id=1, source_target_pairs={{0,1},{1,0},{2,3},{3,2},{4,5},{5,4},{6,7},{7,6},{8,9},{9,8},{10,11... | collective-permute-start | bytes 1290248 | tf_op jit(solution)/shard_map/ppermute | solution.py:77
  18.8 64.1 %collective-permute-start.14 = (bf16[280,768]{1,0:T(8,128)(2,1)}, bf16[280,768]{1,0:T(8,128)(2,1)}, u32[]{:S(2)}, u32[]{:S(2)}) collective-permute-start(bf16[280,768]{1,0:T(8,128)(2,1)} %get-tuple-element.113), channel_id=1, source_target_pairs={{0,2},{1,3},{2,0},{3,1},{4,6},{5,7},{6,4},{7,5},{8,10},{9,11},{10,... | collective-permute-start | bytes 1290248 | tf_op jit(solution)/shard_map/ppermute | solution.py:77
  25.6 11.3 %collective-permute-start.1 = (bf16[48,3712]{1,0:T(8,128)(2,1)S(1)}, bf16[48,3712]{1,0:T(8,128)(2,1)S(1)}, u32[]{:S(2)}, u32[]{:S(2)}) collective-permute-start(bf16[48,3712]{1,0:T(8,128)(2,1)S(1)} %collective-permute-done), channel_id=1, source_target_pairs={{0,8},{4,12},{8,16},{12,20},{16,24},{20,28},{24,0},{28,4},{1,9},{5... | collective-permute-start | bytes 1069064 | tf_op jit(solution)/shard_map/ppermute | solution.py:77
  36.9 10.4 %collective-permute-start.2 = (bf16[48,3712]{1,0:T(8,128)(2,1)S(1)}, bf16[48,3712]{1,0:T(8,128)(2,1)S(1)}, u32[]{:S(2)}, u32[]{:S(2)}) collective-permute-start(bf16[48,3712]{1,0:T(8,128)(2,1)S(1)} %collective-permute-done.1), channel_id=1, source_target_pairs={{0,8},{4,12},{8,16},{12,20},{16,24},{20,28},{24,0},{28,4},{1,9},{5... | collective-permute-start | bytes 1069064 | tf_op jit(solution)/shard_map/ppermute | solution.py:77
  51.2 15.1 %collective-permute-start.6 = (bf16[4,48,1792]{2,1,0:T(8,128)(2,1)}, bf16[4,48,1792]{2,1,0:T(8,128)(2,1)}, u32[]{:S(2)}, u32[]{:S(2)}) collective-permute-start(bf16[4,48,1792]{2,1,0:T(8,128)(2,1)} %slice.393), channel_id=1, source_target_pairs={{0,1},{1,0},{2,3},{3,2},{4,5},{5,4},{6,7},{7,6},{8,9},{9,8},{10,11... | collective-permute-start | bytes 2064392 | tf_op jit(solution)/shard_map/ppermute | solution.py:77
  60.9 19.5 %collective-permute-start.3 = (bf16[4,48,1920]{2,1,0:T(8,128)(2,1)S(1)}, bf16[4,48,1920]{2,1,0:T(8,128)(2,1)S(1)}, u32[]{:S(2)}, u32[]{:S(2)}) collective-permute-start(bf16[4,48,1920]{2,1,0:T(8,128)(2,1)S(1)} %slice.390), channel_id=1, source_target_pairs={{0,2},{1,3},{2,0},{3,1},{4,6},{5,7},{6,4},{7,5},{8,10},{9,11},{10,... | collective-permute-start | bytes 2211848 | tf_op jit(solution)/shard_map/ppermute | solution.py:77
  67.6 38.2 %collective-permute-start.7 = (bf16[4,2,48,1792]{3,2,0,1:T(8,128)(2,1)S(1)}, bf16[4,2,48,1792]{3,2,0,1:T(8,128)(2,1)S(1)}, u32[]{:S(2)}, u32[]{:S(2)}) collective-permute-start(bf16[4,2,48,1792]{3,2,0,1:T(8,128)(2,1)S(1)} %pad_maximum_fusion.10), channel_id=1, source_target_pairs={{0,2},{1,3},{2,0},{3,1},{4,6},{5,7},{6,4},{7,5},{8,10},{9,11},{10,... | collective-permute-start | bytes 4128776 | tf_op jit(solution)/shard_map/ppermute | solution.py:77
  81.9 35.5 %collective-permute-start.4 = (bf16[4,2,48,1920]{3,2,1,0:T(8,128)(2,1)}, bf16[4,2,48,1920]{3,2,1,0:T(8,128)(2,1)}, u32[]{:S(2)}, u32[]{:S(2)}) collective-permute-start(bf16[4,2,48,1920]{3,2,1,0:T(8,128)(2,1)} %pad_maximum_fusion.8), channel_id=1, source_target_pairs={{0,1},{1,0},{2,3},{3,2},{4,5},{5,4},{6,7},{7,6},{8,9},{9,8},{10,11... | collective-permute-start | bytes 4423688 | tf_op jit(solution)/shard_map/ppermute | solution.py:77
  85.4 41.5 %collective-permute-start.15 = (bf16[2,280,768]{2,1,0:T(8,128)(2,1)}, bf16[2,280,768]{2,1,0:T(8,128)(2,1)}, u32[]{:S(2)}, u32[]{:S(2)}) collective-permute-start(bf16[2,280,768]{2,1,0:T(8,128)(2,1)} %pad_maximum_fusion.17), channel_id=1, source_target_pairs={{0,1},{1,0},{2,3},{3,2},{4,5},{5,4},{6,7},{7,6},{8,9},{9,8},{10,11... | collective-permute-start | bytes 2580488 | tf_op jit(solution)/shard_map/ppermute | solution.py:77
  108.5 25.5 %collective-permute-start.8 = (bf16[4,2,2,48,1792]{4,3,0,2,1:T(8,128)(2,1)}, bf16[4,2,2,48,1792]{4,3,0,2,1:T(8,128)(2,1)}, u32[]{:S(2)}, u32[]{:S(2)}) collective-permute-start(bf16[4,2,2,48,1792]{4,3,0,2,1:T(8,128)(2,1)} %pad_maximum_fusion.3), channel_id=1, source_target_pairs={{0,4},{4,0},{8,12},{12,8},{16,20},{20,16},{24,28},{28,24},{1,5},{5... | collective-permute-start | bytes 8257544 | tf_op jit(solution)/shard_map/ppermute | solution.py:77
  109.5 21.8 %collective-permute-start.13 = (bf16[2,280,768]{2,1,0:T(8,128)(2,1)}, bf16[2,280,768]{2,1,0:T(8,128)(2,1)}, u32[]{:S(2)}, u32[]{:S(2)}) collective-permute-start(bf16[2,280,768]{2,1,0:T(8,128)(2,1)} %pad_maximum_fusion.16), channel_id=1, source_target_pairs={{0,2},{1,3},{2,0},{3,1},{4,6},{5,7},{6,4},{7,5},{8,10},{9,11},{10,... | collective-permute-start | bytes 2580488 | tf_op jit(solution)/shard_map/ppermute | solution.py:77
  112.7 46.4 %all-to-all-start = ((bf16[8,2,48,1152]{3,2,1,0:T(8,128)(2,1)}), bf16[8,2,48,1152]{3,2,1,0:T(8,128)(2,1)}, u32[]{:S(2)}, u32[]{:S(2)}) async-start(bf16[8,2,48,1152]{3,2,1,0:T(8,128)(2,1)} %copy.221), calls=%async_computation | async-start | bytes 3538944 | tf_op jit(solution)/shard_map/all_to_all | solution.py:213
  117.0 131.3 %all-gather.5.cloned.1.call-start = ((), (), s32[]{:S(2)}) async-start(), calls=%async_computation.7 | async-start | bytes 8847360 | tf_op jit(solution)/shard_map/all_gather | solution.py:215
  122.4 40.3 %collective-permute-start.5 = (bf16[4,2,2,48,1920]{4,3,2,1,0:T(8,128)(2,1)}, bf16[4,2,2,48,1920]{4,3,2,1,0:T(8,128)(2,1)}, u32[]{:S(2)}, u32[]{:S(2)}) collective-permute-start(bf16[4,2,2,48,1920]{4,3,2,1,0:T(8,128)(2,1)} %pad_maximum_fusion.2), channel_id=1, source_target_pairs={{0,4},{4,0},{8,12},{12,8},{16,20},{20,16},{24,28},{28,24},{1,5},{5... | collective-permute-start | bytes 8847368 | tf_op jit(solution)/shard_map/ppermute | solution.py:77
  162.6 375.5 %reduce-scatter.7.cloned.1.call-start = ((), (), s32[]{:S(2)}) async-start(), calls=%async_computation.8 | async-start | bytes 4423680 | tf_op jit(solution)/shard_map/reduce_scatter | solution.py:360
  179.0 20.0 %collective-permute-start.10 = (bf16[256,512]{0,1:T(8,128)(2,1)}, bf16[256,512]{0,1:T(8,128)(2,1)}, u32[]{:S(2)}, u32[]{:S(2)}) collective-permute-start(bf16[256,512]{0,1:T(8,128)(2,1)} %get-tuple-element.124), channel_id=1, source_target_pairs={{0,2},{1,3},{2,0},{3,1},{4,6},{5,7},{6,4},{7,5},{8,10},{9,11},{10,... | collective-permute-start | bytes 786440 | tf_op jit(solution)/shard_map/ppermute | solution.py:264
  179.2 21.0 %collective-permute-start.9 = (bf16[256,512]{0,1:T(8,128)(2,1)}, bf16[256,512]{0,1:T(8,128)(2,1)}, u32[]{:S(2)}, u32[]{:S(2)}) collective-permute-start(bf16[256,512]{0,1:T(8,128)(2,1)} %get-tuple-element.124), channel_id=1, source_target_pairs={{0,1},{1,2},{2,3},{3,0},{4,5},{5,6},{6,7},{7,4},{8,9},{9,10},{10,1... | collective-permute-start | bytes 786440 | tf_op jit(solution)/shard_map/ppermute | solution.py:264
  180.5 21.6 %collective-permute-start.11 = (bf16[256,512]{0,1:T(8,128)(2,1)}, bf16[256,512]{0,1:T(8,128)(2,1)}, u32[]{:S(2)}, u32[]{:S(2)}) collective-permute-start(bf16[256,512]{0,1:T(8,128)(2,1)} %get-tuple-element.124), channel_id=1, source_target_pairs={{0,3},{1,0},{2,1},{3,2},{4,7},{5,4},{6,5},{7,6},{8,11},{9,8},{10,9... | collective-permute-start | bytes 786440 | tf_op jit(solution)/shard_map/ppermute | solution.py:264
  264.4 21.7 %collective-permute-start.17 = (bf16[256,1536]{1,0:T(8,128)(2,1)S(1)}, bf16[256,1536]{1,0:T(8,128)(2,1)S(1)}, u32[]{:S(2)}, u32[]{:S(2)}) collective-permute-start(bf16[256,1536]{1,0:T(8,128)(2,1)S(1)} %get-tuple-element.139), channel_id=1, source_target_pairs={{0,8},{4,12},{8,16},{12,20},{16,24},{20,28},{24,0},{28,4},{1,9},{5... | collective-permute-start | bytes 2359304 | tf_op jit(solution)/shard_map/ppermute | solution.py:77
  291.0 26.3 %collective-permute-start.22 = (bf16[256,1536]{1,0:T(8,128)(2,1)S(1)}, bf16[256,1536]{1,0:T(8,128)(2,1)S(1)}, u32[]{:S(2)}, u32[]{:S(2)}) collective-permute-start(bf16[256,1536]{1,0:T(8,128)(2,1)S(1)} %slice.551), channel_id=1, source_target_pairs={{0,4},{4,0},{8,12},{12,8},{16,20},{20,16},{24,28},{28,24},{1,5},{5... | collective-permute-start | bytes 2359304 | tf_op jit(solution)/shard_map/ppermute | solution.py:77
  291.6 24.3 %collective-permute-start.19 = (bf16[256,1536]{1,0:T(8,128)(2,1)S(1)}, bf16[256,1536]{1,0:T(8,128)(2,1)S(1)}, u32[]{:S(2)}, u32[]{:S(2)}) collective-permute-start(bf16[256,1536]{1,0:T(8,128)(2,1)S(1)} %collective-permute-done.17), channel_id=1, source_target_pairs={{0,8},{4,12},{8,16},{12,20},{16,24},{20,28},{24,0},{28,4},{1,9},{5... | collective-permute-start | bytes 2359304 | tf_op jit(solution)/shard_map/ppermute | solution.py:77
  321.3 22.2 %collective-permute-start.23 = (bf16[256,1536]{1,0:T(8,128)(2,1)S(1)}, bf16[256,1536]{1,0:T(8,128)(2,1)S(1)}, u32[]{:S(2)}, u32[]{:S(2)}) collective-permute-start(bf16[256,1536]{1,0:T(8,128)(2,1)S(1)} %collective-permute-done.19), channel_id=1, source_target_pairs={{0,8},{4,12},{8,16},{12,20},{16,24},{20,28},{24,0},{28,4},{1,9},{5... | collective-permute-start | bytes 2359304 | tf_op jit(solution)/shard_map/ppermute | solution.py:77
  324.6 35.1 %collective-permute-start.25 = (bf16[256,1536]{1,0:T(8,128)(2,1)S(1)}, bf16[256,1536]{1,0:T(8,128)(2,1)S(1)}, u32[]{:S(2)}, u32[]{:S(2)}) collective-permute-start(bf16[256,1536]{1,0:T(8,128)(2,1)S(1)} %get-tuple-element.57), channel_id=1, source_target_pairs={{0,8},{4,12},{8,16},{12,20},{16,24},{20,28},{24,0},{28,4},{1,9},{5... | collective-permute-start | bytes 2359304 | tf_op jit(solution)/shard_map/ppermute | solution.py:77
  341.5 18.2 %collective-permute-start.26 = (bf16[256,1536]{1,0:T(8,128)(2,1)S(1)}, bf16[256,1536]{1,0:T(8,128)(2,1)S(1)}, u32[]{:S(2)}, u32[]{:S(2)}) collective-permute-start(bf16[256,1536]{1,0:T(8,128)(2,1)S(1)} %slice.550), channel_id=1, source_target_pairs={{0,4},{4,0},{8,12},{12,8},{16,20},{20,16},{24,28},{28,24},{1,5},{5... | collective-permute-start | bytes 2359304 | tf_op jit(solution)/shard_map/ppermute | solution.py:77
  344.5 19.6 %collective-permute-start.24 = (bf16[256,1536]{1,0:T(8,128)(2,1)S(1)}, bf16[256,1536]{1,0:T(8,128)(2,1)S(1)}, u32[]{:S(2)}, u32[]{:S(2)}) collective-permute-start(bf16[256,1536]{1,0:T(8,128)(2,1)S(1)} %get-tuple-element.47), channel_id=1, source_target_pairs={{0,4},{4,0},{8,12},{12,8},{16,20},{20,16},{24,28},{28,24},{1,5},{5... | collective-permute-start | bytes 2359304 | tf_op jit(solution)/shard_map/ppermute | solution.py:77
  363.8 21.0 %collective-permute-start.27 = (bf16[256,1536]{1,0:T(8,128)(2,1)S(1)}, bf16[256,1536]{1,0:T(8,128)(2,1)S(1)}, u32[]{:S(2)}, u32[]{:S(2)}) collective-permute-start(bf16[256,1536]{1,0:T(8,128)(2,1)S(1)} %get-tuple-element.54), channel_id=1, source_target_pairs={{0,8},{4,12},{8,16},{12,20},{16,24},{20,28},{24,0},{28,4},{1,9},{5... | collective-permute-start | bytes 2359304 | tf_op jit(solution)/shard_map/ppermute | solution.py:77
  397.2 143.2 %reduce-scatter.9.cloned.1.call-start = ((), (), s32[]{:S(2)}) async-start(), calls=%async_computation.9 | async-start | bytes 4423680 | tf_op jit(solution)/shard_map/reduce_scatter | solution.py:360
  397.2 19.9 %collective-permute-start.29 = (bf16[256,1536]{1,0:T(8,128)(2,1)S(1)}, bf16[256,1536]{1,0:T(8,128)(2,1)S(1)}, u32[]{:S(2)}, u32[]{:S(2)}) collective-permute-start(bf16[256,1536]{1,0:T(8,128)(2,1)S(1)} %get-tuple-element.52), channel_id=1, source_target_pairs={{0,8},{4,12},{8,16},{12,20},{16,24},{20,28},{24,0},{28,4},{1,9},{5... | collective-permute-start | bytes 2359304 | tf_op jit(solution)/shard_map/ppermute | solution.py:77
  435.0 243.8 %reduce-scatter.11.cloned.1.call-start = ((), (), s32[]{:S(2)}) async-start(), calls=%async_computation.10 | async-start | bytes 7077888 | tf_op jit(solution)/shard_map/reduce_scatter | solution.py:408
  470.3 94.8 %collective-permute-start.38 = (bf16[4,2,2,48,1536]{4,3,0,2,1:T(8,128)(2,1)}, bf16[4,2,2,48,1536]{4,3,0,2,1:T(8,128)(2,1)}, u32[]{:S(2)}, u32[]{:S(2)}) collective-permute-start(bf16[4,2,2,48,1536]{4,3,0,2,1:T(8,128)(2,1)} %bitcast.344), channel_id=1, source_target_pairs={{0,4},{4,0},{8,12},{12,8},{16,20},{20,16},{24,28},{28,24},{1,5},{5... | collective-permute-start | bytes 7077896 | tf_op jit(solution)/shard_map/ppermute | solution.py:77
  494.9 10.9 %collective-permute-start.30 = (bf16[256,512]{0,1:T(8,128)(2,1)S(1)}, bf16[256,512]{0,1:T(8,128)(2,1)S(1)}, u32[]{:S(2)}, u32[]{:S(2)}) collective-permute-start(bf16[256,512]{0,1:T(8,128)(2,1)S(1)} %get-tuple-element.105), channel_id=1, source_target_pairs={{0,1},{1,2},{2,3},{3,0},{4,5},{5,6},{6,7},{7,4},{8,9},{9,10},{10,1... | collective-permute-start | bytes 786440 | tf_op jit(solution)/shard_map/ppermute | solution.py:106
  496.4 11.9 %collective-permute-start.32 = (bf16[256,512]{0,1:T(8,128)(2,1)S(1)}, bf16[256,512]{0,1:T(8,128)(2,1)S(1)}, u32[]{:S(2)}, u32[]{:S(2)}) collective-permute-start(bf16[256,512]{0,1:T(8,128)(2,1)S(1)} %get-tuple-element.106), channel_id=1, source_target_pairs={{0,3},{1,0},{2,1},{3,2},{4,7},{5,4},{6,5},{7,6},{8,11},{9,8},{10,9... | collective-permute-start | bytes 786440 | tf_op jit(solution)/shard_map/ppermute | solution.py:106
  497.9 10.4 %collective-permute-start.31 = (bf16[256,512]{0,1:T(8,128)(2,1)S(1)}, bf16[256,512]{0,1:T(8,128)(2,1)S(1)}, u32[]{:S(2)}, u32[]{:S(2)}) collective-permute-start(bf16[256,512]{0,1:T(8,128)(2,1)S(1)} %get-tuple-element.107), channel_id=1, source_target_pairs={{0,2},{1,3},{2,0},{3,1},{4,6},{5,7},{6,4},{7,5},{8,10},{9,11},{10,... | collective-permute-start | bytes 786440 | tf_op jit(solution)/shard_map/ppermute | solution.py:106
  538.2 64.8 %collective-permute-start.33 = (bf16[4,2,2,48,2176]{4,3,0,2,1:T(8,128)(2,1)}, bf16[4,2,2,48,2176]{4,3,0,2,1:T(8,128)(2,1)}, u32[]{:S(2)}, u32[]{:S(2)}) collective-permute-start(bf16[4,2,2,48,2176]{4,3,0,2,1:T(8,128)(2,1)} %bitcast.343), channel_id=1, source_target_pairs={{0,4},{4,0},{8,12},{12,8},{16,20},{20,16},{24,28},{28,24},{1,5},{5... | collective-permute-start | bytes 10027016 | tf_op jit(solution)/shard_map/ppermute | solution.py:77
  543.6 56.9 %all-to-all-start.1 = ((bf16[8,2,48,1152]{3,2,1,0:T(8,128)(2,1)}), bf16[8,2,48,1152]{3,2,1,0:T(8,128)(2,1)}, u32[]{:S(2)}, u32[]{:S(2)}) async-start(bf16[8,2,48,1152]{3,2,1,0:T(8,128)(2,1)} %copy.231), calls=%async_computation.3 | async-start | bytes 3538944 | tf_op jit(solution)/shard_map/all_to_all | solution.py:409
  547.9 143.2 %reduce-scatter.13.cloned.1.call-start = ((), (), s32[]{:S(2)}) async-start(), calls=%async_computation.11 | async-start | bytes 4300800
  567.8 15.7 %collective-permute-start.41 = (bf16[4,2,48,768]{3,2,0,1:T(8,128)(2,1)S(1)}, bf16[4,2,48,768]{3,2,0,1:T(8,128)(2,1)S(1)}, u32[]{:S(2)}, u32[]{:S(2)}) collective-permute-start(bf16[4,2,48,768]{3,2,0,1:T(8,128)(2,1)S(1)} %dynamic-slice_bitcast_fusion.2), channel_id=1, source_target_pairs={{0,2},{1,3},{2,0},{3,1},{4,6},{5,7},{6,4},{7,5},{8,10},{9,11},{10,... | collective-permute-start | bytes 1769480 | tf_op jit(solution)/shard_map/ppermute | solution.py:77
  572.4 37.2 %collective-permute-start.39 = (bf16[4,2,48,768]{3,2,0,1:T(8,128)(2,1)}, bf16[4,2,48,768]{3,2,0,1:T(8,128)(2,1)}, u32[]{:S(2)}, u32[]{:S(2)}) collective-permute-start(bf16[4,2,48,768]{3,2,0,1:T(8,128)(2,1)} %dynamic-slice_bitcast_fusion.3), channel_id=1, source_target_pairs={{0,1},{1,0},{2,3},{3,2},{4,5},{5,4},{6,7},{7,6},{8,9},{9,8},{10,11... | collective-permute-start | bytes 1769480 | tf_op jit(solution)/shard_map/ppermute | solution.py:77
  585.5 26.0 %collective-permute-start.42 = (bf16[4,48,768]{2,1,0:T(8,128)(2,1)}, bf16[4,48,768]{2,1,0:T(8,128)(2,1)}, u32[]{:S(2)}, u32[]{:S(2)}) collective-permute-start(bf16[4,48,768]{2,1,0:T(8,128)(2,1)} %fusion.147), channel_id=1, source_target_pairs={{0,1},{1,0},{2,3},{3,2},{4,5},{5,4},{6,7},{7,6},{8,9},{9,8},{10,11... | collective-permute-start | bytes 884744 | tf_op jit(solution)/shard_map/ppermute | solution.py:77
  606.4 31.1 %collective-permute-start.34 = (bf16[4,2,48,1024]{3,2,0,1:T(8,128)(2,1)S(1)}, bf16[4,2,48,1024]{3,2,0,1:T(8,128)(2,1)S(1)}, u32[]{:S(2)}, u32[]{:S(2)}) collective-permute-start(bf16[4,2,48,1024]{3,2,0,1:T(8,128)(2,1)S(1)} %dynamic-slice_bitcast_fusion.1), channel_id=1, source_target_pairs={{0,1},{1,0},{2,3},{3,2},{4,5},{5,4},{6,7},{7,6},{8,9},{9,8},{10,11... | collective-permute-start | bytes 2359304 | tf_op jit(solution)/shard_map/ppermute | solution.py:77
  608.0 32.0 %collective-permute-start.36 = (bf16[4,2,48,1152]{3,2,0,1:T(8,128)(2,1)S(1)}, bf16[4,2,48,1152]{3,2,0,1:T(8,128)(2,1)S(1)}, u32[]{:S(2)}, u32[]{:S(2)}) collective-permute-start(bf16[4,2,48,1152]{3,2,0,1:T(8,128)(2,1)S(1)} %dynamic-slice_bitcast_fusion), channel_id=1, source_target_pairs={{0,2},{1,3},{2,0},{3,1},{4,6},{5,7},{6,4},{7,5},{8,10},{9,11},{10,... | collective-permute-start | bytes 2654216 | tf_op jit(solution)/shard_map/ppermute | solution.py:77
  610.8 38.7 %collective-permute-start.40 = (bf16[4,48,768]{2,1,0:T(8,128)(2,1)S(1)}, bf16[4,48,768]{2,1,0:T(8,128)(2,1)S(1)}, u32[]{:S(2)}, u32[]{:S(2)}) collective-permute-start(bf16[4,48,768]{2,1,0:T(8,128)(2,1)S(1)} %fusion.146), channel_id=1, source_target_pairs={{0,2},{1,3},{2,0},{3,1},{4,6},{5,7},{6,4},{7,5},{8,10},{9,11},{10,... | collective-permute-start | bytes 884744 | tf_op jit(solution)/shard_map/ppermute | solution.py:77
  637.9 25.7 %collective-permute-start.35 = (bf16[4,48,1024]{2,1,0:T(8,128)(2,1)S(1)}, bf16[4,48,1024]{2,1,0:T(8,128)(2,1)S(1)}, u32[]{:S(2)}, u32[]{:S(2)}) collective-permute-start(bf16[4,48,1024]{2,1,0:T(8,128)(2,1)S(1)} %fusion.144), channel_id=1, source_target_pairs={{0,2},{1,3},{2,0},{3,1},{4,6},{5,7},{6,4},{7,5},{8,10},{9,11},{10,... | collective-permute-start | bytes 1179656 | tf_op jit(solution)/shard_map/ppermute | solution.py:77
  640.3 23.4 %collective-permute-start.37 = (bf16[4,48,1152]{2,1,0:T(8,128)(2,1)S(1)}, bf16[4,48,1152]{2,1,0:T(8,128)(2,1)S(1)}, u32[]{:S(2)}, u32[]{:S(2)}) collective-permute-start(bf16[4,48,1152]{2,1,0:T(8,128)(2,1)S(1)} %fusion.142), channel_id=1, source_target_pairs={{0,1},{1,0},{2,3},{3,2},{4,5},{5,4},{6,7},{7,6},{8,9},{9,8},{10,11... | collective-permute-start | bytes 1327112 | tf_op jit(solution)/shard_map/ppermute | solution.py:77
  664.8 12.0 %collective-permute-start.43 = (bf16[48,3712]{1,0:T(8,128)(2,1)}, bf16[48,3712]{1,0:T(8,128)(2,1)}, u32[]{:S(2)}, u32[]{:S(2)}) collective-permute-start(bf16[48,3712]{1,0:T(8,128)(2,1)} %dynamic-slice_bitcast_fusion.4), channel_id=1, source_target_pairs={{0,8},{4,12},{8,16},{12,20},{16,24},{20,28},{24,0},{28,4},{1,9},{5... | collective-permute-start | bytes 1069064 | tf_op jit(solution)/shard_map/ppermute | solution.py:77
  678.8 11.2 %collective-permute-start.44 = (bf16[48,3712]{1,0:T(8,128)(2,1)}, bf16[48,3712]{1,0:T(8,128)(2,1)}, u32[]{:S(2)}, u32[]{:S(2)}) collective-permute-start(bf16[48,3712]{1,0:T(8,128)(2,1)} %fusion.131), channel_id=1, source_target_pairs={{0,8},{4,12},{8,16},{12,20},{16,24},{20,28},{24,0},{28,4},{1,9},{5... | collective-permute-start | bytes 1069064 | tf_op jit(solution)/shard_map/ppermute | solution.py:77
  (121 other events, 1253.2 us)
Sparse Core Ops, SparseCore 0:
  50.2 63.6 all-gather.2
  162.8 85.5 all-gather.4
  397.3 44.4 reduce-scatter.6
  444.8 47.2 reduce-scatter.8
  494.2 79.4 reduce-scatter.10
  576.6 86.4 reduce-scatter.12

commit v3 on v2

--- a/solution.py
+++ b/solution.py
@@ -1,6 +1,8 @@
 import jax
 import jax.numpy as jnp
 from jax import lax
+from jax.experimental import pallas as pl
+from jax.experimental.pallas import tpu as pltpu
 from jax.sharding import PartitionSpec as P
 
 D = 1536
@@ -13,6 +15,10 @@
 EPS = 1e-06
 F32 = jnp.float32
 LOW = jnp.bfloat16
+GROUP = HEADS // KV_HEADS
+VMEM_BYTES = 32 * 2**20
+LAST = (((1,), (1,)), ((), ()))
+FIRST = (((0,), (0,)), ((), ()))
 
 
 def turn(values, cosine, sine):
@@ -37,14 +43,88 @@
     )
 
 
-def score_block(query_rot, key_all, allowed):
-    tokens = query_rot.shape[0]
-    grouped = query_rot.reshape(tokens, KV_HEADS, HEADS // KV_HEADS, HEAD)
-    keyed = key_all.reshape(key_all.shape[0], KV_HEADS, HEAD)
-    scores = jnp.einsum(
-        "tkgd,skd->kgts", grouped, keyed, preferred_element_type=F32
-    ) * HEAD ** (-0.5)
-    return jnp.where(allowed[None, None], scores, -1e30)
+def product(left, right, contract):
+    return lax.dot_general(left, right, contract, preferred_element_type=F32)
+
+
+def attend_kernel(q_ref, k_ref, v_ref, bias_ref, o_ref):
+    scores = product(q_ref[...], k_ref[...], LAST) * HEAD ** (-0.5) + bias_ref[...]
+    weights = jnp.exp(scores - jnp.max(scores, axis=1, keepdims=True))
+    probs = weights * (1.0 / jnp.sum(weights, axis=1, keepdims=True))
+    o_ref[...] = jnp.dot(probs.astype(LOW), v_ref[...], preferred_element_type=F32).astype(LOW)
+
+
+def attend(query_rot, both_all, bias):
+    tokens, whole = bias.shape
+    return pl.pallas_call(
+        attend_kernel,
+        grid=(HEADS,),
+        in_specs=[
+            pl.BlockSpec((tokens, HEAD), lambda h: (0, h)),
+            pl.BlockSpec((whole, HEAD), lambda h: (0, h // GROUP)),
+            pl.BlockSpec((whole, HEAD), lambda h: (0, KV_HEADS + h // GROUP)),
+            pl.BlockSpec((tokens, whole), lambda h: (0, 0)),
+        ],
+        out_specs=pl.BlockSpec((tokens, HEAD), lambda h: (0, h)),
+        out_shape=jax.ShapeDtypeStruct(query_rot.shape, LOW),
+        compiler_params=pltpu.CompilerParams(vmem_limit_bytes=VMEM_BYTES),
+        cost_estimate=pl.CostEstimate(flops=10**10, bytes_accessed=10**6, transcendentals=0),
+    )(query_rot, both_all, both_all, bias)
+
+
+def attend_back_kernel(q_ref, g_ref, k_ref, v_ref, bias_ref, dq_ref, dkv_ref, dk_sum, dv_sum):
+    step = pl.program_id(0) % GROUP
+    query, grad, key = q_ref[...], g_ref[...], k_ref[...]
+    scores = product(key, query, LAST) * HEAD ** (-0.5) + bias_ref[...]
+    weights = jnp.exp(scores - jnp.max(scores, axis=0, keepdims=True))
+    probs = weights * (1.0 / jnp.sum(weights, axis=0, keepdims=True))
+    grad_probs = product(v_ref[...], grad, LAST)
+    mean = jnp.sum(probs * grad_probs, axis=0, keepdims=True)
+    grad_scores = (probs * (grad_probs - mean)).astype(LOW)
+    dq_ref[...] = product(grad_scores, key, FIRST) * HEAD ** (-0.5)
+    dv = jnp.dot(probs.astype(LOW), grad, preferred_element_type=F32)
+    dk = jnp.dot(grad_scores, query, preferred_element_type=F32)
+
+    @pl.when(step == 0)
+    def _():
+        dv_sum[...] = dv
+        dk_sum[...] = dk
+
+    @pl.when(step > 0)
+    def _():
+        dv_sum[...] += dv
+        dk_sum[...] += dk
+
+    @pl.when(step == GROUP - 1)
+    def _():
+        dkv_ref[0] = (dk_sum[...] * HEAD ** (-0.5)).astype(LOW)
+        dkv_ref[1] = dv_sum[...].astype(LOW)
+
+
+def attend_back(query_rot, grad_mixed, both_all, bias):
+    whole, tokens = bias.shape
+    return pl.pallas_call(
+        attend_back_kernel,
+        grid=(HEADS,),
+        in_specs=[
+            pl.BlockSpec((tokens, HEAD), lambda h: (0, h)),
+            pl.BlockSpec((tokens, HEAD), lambda h: (0, h)),
+            pl.BlockSpec((whole, HEAD), lambda h: (0, h // GROUP)),
+            pl.BlockSpec((whole, HEAD), lambda h: (0, KV_HEADS + h // GROUP)),
+            pl.BlockSpec((whole, tokens), lambda h: (0, 0)),
+        ],
+        out_specs=[
+            pl.BlockSpec((tokens, HEAD), lambda h: (0, h)),
+            pl.BlockSpec((2, whole, HEAD), lambda h: (0, 0, h // GROUP)),
+        ],
+        out_shape=[
+            jax.ShapeDtypeStruct(query_rot.shape, F32),
+            jax.ShapeDtypeStruct((2, whole, KV_HEADS * HEAD), LOW),
+        ],
+        scratch_shapes=[pltpu.VMEM((whole, HEAD), F32), pltpu.VMEM((whole, HEAD), F32)],
+        compiler_params=pltpu.CompilerParams(vmem_limit_bytes=VMEM_BYTES),
+        cost_estimate=pl.CostEstimate(flops=2 * 10**10, bytes_accessed=10**6, transcendentals=0),
+    )(query_rot, grad_mixed, both_all, both_all, bias)
 
 
 def norm_back(grad_normed, hidden, inverse, gain):
@@ -164,18 +244,13 @@
         return inner.scatter(outer.scatter(blocks, dim, kind), dim, kind)
 
     def plane_gather_halves(value, cut, dim):
-        return (
-            plane_gather(value[..., :cut], True, dim),
-            plane_gather(value[..., cut:], False, dim),
-        )
-
-    def plane_sums(array, cut, *waits):
+        first = (inner.gather(value[..., :cut], dim), outer.gather(value[..., cut:], dim))
+        first = (hold(first[0], first[1]), hold(first[1], first[0]))
+        return (outer.gather(first[0], dim), inner.gather(first[1], dim + 1))
+
+    def core_sums(array):
         blocks = array.reshape((n_dp // 2, 2, n_ctx // 2, 2, rows) + array.shape[1:])
-        blocks = hold(core.scatter(blocks, 1).astype(LOW), *waits)
-        return [
-            plane_scatter(part, first, 1).astype(LOW)
-            for part, first in ((blocks[..., :cut], True), (blocks[..., cut:], False))
-        ]
+        return core.scatter(blocks, 1).astype(LOW)
 
     few = key_bias.shape[0]
     tile = jnp.stack(
@@ -189,8 +264,19 @@
     ring_in = chip.ring(
         jnp.concatenate([query_weight, key_weight, value_weight, output_weight, tile], axis=1)
     )
-    plane_in = plane_gather_halves(chip.ordered(ring_in, 0), half, 1)
-    weight_qk, weight_rest = [core.gather(part, 1).reshape(D, -1) for part in plane_in]
+    cut = D // 2
+    down_first = (inner.gather(down_weight[:, :cut], 0), outer.gather(down_weight[:, cut:], 0))
+    plane_in = plane_gather_halves(hold(chip.ordered(ring_in, 0), *down_first), half, 1)
+    upstream_all = lax.all_gather(hold(cotangent, ring_in[-1]), "dp", axis=0, tiled=True)
+
+    real = gate_weight.shape[1] // n_dp
+    width = -(-real // HEAD) * HEAD
+    units = jnp.stack(
+        [gate_weight.reshape(rows, n_dp, real), up_weight.reshape(rows, n_dp, real)]
+    ).transpose(2, 0, 1, 3)
+    units = jnp.pad(units, ((0, 0), (0, 0), (0, 0), (0, width - real)))
+    units = lax.all_to_all(hold(units, *plane_in), "dp", 0, 0, tiled=True)
+    weight_qk, weight_rest = [core.gather(hold(part, *plane_in), 1).reshape(D, -1) for part in plane_in]
     weight_v = weight_rest[:, :kv_width]
     weight_o = weight_rest[:, kv_width : kv_width + D]
     vectors = weight_rest[:, kv_width + D :].astype(F32).T
@@ -199,27 +285,9 @@
         vectors[i].reshape(-1, rows)[:, :few].reshape(-1) for i in (3, 4)
     )
 
-    real = gate_weight.shape[1] // n_dp
-    width = -(-real // HEAD) * HEAD
-    weight_d = jnp.concatenate(
-        [part.reshape(real, D // 2) for part in plane_gather_halves(down_weight, D // 2, 0)],
-        axis=1,
-    )
-    weight_d = jnp.pad(weight_d, ((0, width - real), (0, 0)))
-    units = jnp.stack(
-        [gate_weight.reshape(rows, n_dp, real), up_weight.reshape(rows, n_dp, real)]
-    ).transpose(2, 0, 1, 3)
-    units = jnp.pad(units, ((0, 0), (0, 0), (0, 0), (0, width - real)))
-    units = lax.all_to_all(hold(units, ring_in[-1]), "dp", 0, 0, tiled=True)
-    units = units.transpose(1, 0, 2, 3).reshape(2 * n_dp * rows, width)
-    units_all = lax.all_gather(hold(units, weight_qk), "ctx", axis=0, tiled=True)
-    units_all = units_all.reshape(n_ctx, 2, n_dp * rows, width)
-    weight_g, weight_u = (units_all[:, i].reshape(D, width) for i in (0, 1))
     place = jnp.arange(D, dtype=jnp.int32)
     source = ((place // rows) % n_dp * n_ctx + place // (rows * n_dp)) * rows + place % rows
     order = (place[:, None] == source[None, :]).astype(LOW)
-
-    upstream_all = lax.all_gather(hold(cotangent, ring_in[-1]), "dp", axis=0, tiled=True)
 
     whole = tokens * n_ctx
     places = jnp.arange(whole, dtype=jnp.int32)
@@ -237,6 +305,10 @@
     my_offsets = lax.dynamic_slice_in_dim(offsets, first_row, tokens)
     allowed = (places[None, :] <= mine[:, None]) & (segment[None, :] == my_segment[:, None])
     allowed = allowed & (jnp.logical_not(padded)[None, :] | (places[None, :] == mine[:, None]))
+    bias = jnp.where(allowed, 0.0, -1e30).astype(F32)
+    turned = (places[:, None] <= mine[None, :]) & (segment[:, None] == my_segment[None, :])
+    turned = turned & (jnp.logical_not(padded)[:, None] | (places[:, None] == mine[None, :]))
+    bias_turned = jnp.where(turned, 0.0, -1e30).astype(F32)
     freqs = 10000.0 ** (-jnp.arange(0, HEAD // 2, dtype=F32) * 2.0 / HEAD)
     angles = my_offsets.astype(F32)[:, None] * freqs[None, :]
     cosine = jnp.cos(angles)
@@ -256,7 +328,13 @@
         .reshape(tokens, kv_width)
     )
     value_low = values.astype(LOW)
-    both = jnp.concatenate([key_rot, value_low], axis=1)
+    down_parts = (
+        outer.gather(hold(down_first[0], weight_qk), 0),
+        inner.gather(hold(down_first[1], weight_qk), 1),
+    )
+    weight_d = jnp.concatenate([part.reshape(real, cut) for part in down_parts], axis=1)
+    weight_d = jnp.pad(weight_d, ((0, width - real), (0, 0)))
+    both = hold(jnp.concatenate([key_rot, value_low], axis=1), *down_parts)
     both_all = jnp.zeros((n_ctx,) + both.shape, LOW)
     for step in range(n_ctx):
         arrived = both
@@ -266,60 +344,43 @@
             both_all, arrived[None], (which - step) % n_ctx, 0
         )
     both_all = both_all.reshape(whole, 2 * kv_width)
-    key_all, value_all = both_all[:, :kv_width], both_all[:, kv_width:]
-    scores = score_block(query_rot, key_all, allowed)
-    top = jnp.max(scores, axis=-1, keepdims=True)
-    weights = jnp.exp(scores - top)
-    totals = jnp.sum(weights, axis=-1, keepdims=True)
-    probs = weights / totals
-    log_total = top + jnp.log(totals)
-    value_heads = value_all.reshape(whole, KV_HEADS, HEAD)
-    mixed = jnp.einsum(
-        "kgts,skd->tkgd", probs.astype(LOW), value_heads, preferred_element_type=F32
-    )
-    mixed_low = mixed.reshape(tokens, D).astype(LOW)
+    units = units.transpose(1, 0, 2, 3).reshape(2 * n_dp * rows, width)
+    units_all = lax.all_gather(hold(units, both), "ctx", axis=0, tiled=True)
+    units_all = units_all.reshape(n_ctx, 2, n_dp * rows, width)
+    weight_g, weight_u = (units_all[:, i].reshape(D, width) for i in (0, 1))
+    mixed_low = attend(query_rot.reshape(tokens, D), both_all, bias)
     middle = hidden + jnp.dot(mixed_low, weight_o, preferred_element_type=F32)
 
     inverse2 = lax.rsqrt(jnp.mean(middle * middle, axis=1, keepdims=True) + EPS)
     normed2 = (middle * inverse2 * gain_f).astype(LOW)
     normed2 = jnp.dot(normed2, order, preferred_element_type=F32).astype(LOW)
-    upstream_own = [
+    upstream = [
         lax.dynamic_slice_in_dim(
-            upstream_all, ((chip.place - step) % chip.size * 2 + core.place) * tokens, tokens, 0
+            upstream_all, (chip.place - step) % chip.size * 2 * tokens, 2 * tokens, 0
         )
         for step in range(n_dp // 2)
-    ]
-    upstream_other = [
-        lax.dynamic_slice_in_dim(
-            upstream_all, ((chip.place - step) % chip.size * 2 + 1 - core.place) * tokens, tokens, 0
-        )
-        for step in range(n_dp // 2)
-    ]
-    upstream = [
-        jnp.concatenate([own, other], axis=0) for own, other in zip(upstream_own, upstream_other)
     ]
     grad_actives = [
         jnp.einsum("td,fd->tf", back, weight_d, preferred_element_type=F32).astype(LOW)
         for back in upstream
     ]
-    normed2 = hold(normed2, weight_g, weight_u, *grad_actives[:1])
     inputs_own = chip.ring(normed2)
 
     def both_cores(part, *waits):
         part = hold(part, *waits)
-        return jnp.concatenate([part, core.shift(part)], axis=0)
+        return core.ordered([part, core.shift(part)], 0).reshape(2 * tokens, D)
+
+    def half_of(part, side):
+        return lax.dynamic_slice_in_dim(part, (core.place + side) % 2 * tokens, tokens, 0)
 
     def core_sum(part):
-        return part[:tokens] + core.shift(part[tokens:].astype(LOW)).astype(F32)
+        return half_of(part, 0) + core.shift(half_of(part, 1).astype(LOW)).astype(F32)
 
     inputs, actives, grad_gates, grad_upwards, grads, kept, grad_sums, outs = ([] for _ in range(8))
-    out_all = jnp.zeros((n_dp * tokens, D), LOW)
     for step, fed in enumerate(inputs_own):
         fed = both_cores(fed, *actives[-1:])
         inputs.append(fed)
         grad_active = grad_actives[step].astype(F32)
-        if step > 1:
-            fed = hold(fed, *kept, *grad_sums[1:], *outs[-1:])
         gate = jnp.dot(fed, weight_g, preferred_element_type=F32)
         upward = jnp.dot(fed, weight_u, preferred_element_type=F32)
         sigmoid_gate = jax.nn.sigmoid(gate)
@@ -328,88 +389,77 @@
             grad_active * upward * sigmoid_gate * (1.0 + gate * (1.0 - sigmoid_gate))
         ).astype(LOW)
         grad_upward = (grad_active * gate * sigmoid_gate).astype(LOW)
+        back_gate, back_upward = grad_gate, grad_upward
+        if step == 1:
+            back_gate = hold(grad_gate, grads[0])
+        if step > 1:
+            arrived = chip.shift(grad_sums[-1].astype(LOW))
+            back_gate, back_upward = hold(grad_gate, arrived), hold(grad_upward, arrived)
         grads.append(
-            jnp.einsum("tf,df->td", grad_gate, weight_g, preferred_element_type=F32)
-            + jnp.einsum("tf,df->td", grad_upward, weight_u, preferred_element_type=F32)
+            jnp.einsum("tf,df->td", back_gate, weight_g, preferred_element_type=F32)
+            + jnp.einsum("tf,df->td", back_upward, weight_u, preferred_element_type=F32)
         )
         kept.append(core_sum(grads[-1]))
-        if step == 1:
-            grad_sums.append(kept[1])
-        if step > 1:
-            arrived = chip.shift(grad_sums[-1].astype(LOW)).astype(F32)
-            grad_sums.append(arrived + kept[step])
+        if step > 0:
+            grad_sums.append(kept[-1] if step == 1 else arrived.astype(F32) + kept[-1])
         actives.append(active)
         outs.append(jnp.dot(active, weight_d, preferred_element_type=F32).astype(LOW))
-        for side in range(2):
-            index = (chip.place - step) % chip.size * 2 + (core.place + side) % 2
-            piece = outs[-1][side * tokens : (side + 1) * tokens]
-            out_all = lax.dynamic_update_slice_in_dim(out_all, piece, index * tokens, 0)
         grad_gates.append(grad_gate)
         grad_upwards.append(grad_upward)
     arrived = chip.shift(grad_sums[-1].astype(LOW)).astype(F32)
     grad_normed2 = (arrived + kept[0]).astype(LOW)
 
     fed_all = jnp.concatenate(inputs, axis=0)
-    part_gate = jnp.einsum(
-        "td,tf->df",
-        fed_all,
-        hold(jnp.concatenate(grad_gates, axis=0), grad_sums[-1]),
-        preferred_element_type=F32,
-    ).astype(LOW)
-    def plane_sum(part):
+    def plane_sum(parts, wait):
+        part = jnp.einsum(
+            "td,tf->df",
+            fed_all,
+            hold(jnp.concatenate(parts, axis=0), wait),
+            preferred_element_type=F32,
+        ).astype(LOW)
         total = lax.psum_scatter(part, "ctx", scatter_dimension=0, tiled=True)
-        return total.reshape(n_dp, rows, width)
-
-
-    grad_normed2 = hold(grad_normed2, part_gate)
+        return part, total.reshape(n_dp, rows, width)
+
+    part_gate, sum_gate = plane_sum(grad_gates, grad_sums[-1])
+
+    others = core.shift(jnp.stack([half_of(part, 1) for part in outs]))
+    out_parts = [
+        half_of(part, 0).astype(F32) + others[step].astype(F32) for step, part in enumerate(outs)
+    ]
+    grad_normed2 = hold(grad_normed2, part_gate, *out_parts[1:2])
     grad_normed2 = jnp.einsum("te,de->td", grad_normed2, order, preferred_element_type=F32)
     grad_gain_f, grad_middle = norm_back(grad_normed2, middle, inverse2, gain_f)
     grad_middle = grad_middle + cotangent.astype(F32)
     grad_attention = grad_middle.astype(LOW)
-    part_up = jnp.einsum(
-        "td,tf->df",
-        fed_all,
-        hold(jnp.concatenate(grad_upwards, axis=0), grad_attention),
-        preferred_element_type=F32,
-    ).astype(LOW)
-    sums = jnp.stack([plane_sum(part_gate), plane_sum(part_up)], axis=1)
-    part_output = jnp.einsum(
-        "td,te->de", mixed_low, grad_attention, preferred_element_type=F32
-    ).astype(LOW)
     grad_mixed = jnp.einsum(
         "te,de->td", grad_attention, weight_o, preferred_element_type=F32
     ).astype(LOW)
-    grad_heads = grad_mixed.reshape(tokens, KV_HEADS, HEADS // KV_HEADS, HEAD)
-    probs = jnp.exp(score_block(query_rot, key_all, allowed) - log_total)
-    grad_probs = jnp.einsum(
-        "tkgd,skd->kgts", grad_heads, value_heads, preferred_element_type=F32
-    )
-    grad_scores = (
-        probs * (grad_probs - jnp.sum(probs * grad_probs, axis=-1, keepdims=True))
+    out_sums = [hold(out_parts[1 % len(outs)], grad_attention).astype(LOW)]
+    out_first = chip.shift(out_sums[0]).astype(F32)
+    grad_query_rot, both_part = attend_back(
+        query_rot.reshape(tokens, D), grad_mixed, both_all, bias_turned
+    )
+    out_sums.append(out_first + out_parts[2 % len(outs)])
+    part_output = jnp.einsum(
+        "td,te->de", mixed_low, hold(grad_attention, both_part), preferred_element_type=F32
     ).astype(LOW)
-    grad_value_part = jnp.einsum(
-        "kgts,tkgd->skd", probs.astype(LOW), grad_heads, preferred_element_type=F32
-    )
-    key_heads = key_all.reshape(whole, KV_HEADS, HEAD)
-    grouped = query_rot.reshape(tokens, KV_HEADS, HEADS // KV_HEADS, HEAD)
-    grad_query_rot = jnp.einsum(
-        "kgts,skd->tkgd", grad_scores, key_heads, preferred_element_type=F32
-    ) * HEAD ** (-0.5)
-    grad_key_part = jnp.einsum(
-        "kgts,tkgd->skd", grad_scores, grouped, preferred_element_type=F32
-    ) * HEAD ** (-0.5)
-    both_part = jnp.concatenate(
-        [grad_key_part.reshape(whole, kv_width), grad_value_part.reshape(whole, kv_width)], axis=1
-    )
-    both_part = both_part.astype(LOW).reshape(n_ctx, tokens, 2 * kv_width)
-    both_sum = row.direct(both_part, 0)
-    grad_key_rot = both_sum[:, :kv_width]
-    grad_values = both_sum[:, kv_width:].astype(LOW)
-    part_out = lax.psum_scatter(out_all, "dp", scatter_dimension=0, tiled=True)
+    core_output = core_sums(part_output)
+    both_part = hold(both_part, out_first).reshape(2, n_ctx, tokens, kv_width)
+    both_sum = row.direct(both_part, 1)
+    grad_key_rot = both_sum[0]
+    grad_values = both_sum[1].astype(LOW)
+    part_up, sum_up = plane_sum(grad_upwards, both_part)
+    sums = jnp.stack([sum_gate, sum_up], axis=1)
+    part_down = jnp.einsum(
+        "tf,td->fd",
+        hold(jnp.concatenate(actives, axis=0), both_sum),
+        jnp.concatenate(upstream, axis=0),
+        preferred_element_type=F32,
+    ).astype(LOW)[:real]
+    part_down = lax.psum_scatter(part_down, "ctx", scatter_dimension=0, tiled=True)
     sums = lax.all_to_all(hold(sums, both_part), "dp", 0, 0, tiled=True)
     gate_weight_grad = sums[:, 0, :, :real].transpose(1, 0, 2).reshape(rows, -1).astype(F32)
     up_weight_grad = sums[:, 1, :, :real].transpose(1, 0, 2).reshape(rows, -1).astype(F32)
-    plane_output = plane_sums(part_output, D // 2, grad_key_rot)
     grad_keys = (
         unturn(grad_key_rot.reshape(tokens, KV_HEADS, HEAD), cosine, sine)
         .reshape(tokens, kv_width)
@@ -421,6 +471,8 @@
         .astype(LOW)
     )
     joined = jnp.concatenate([grad_queries, grad_keys, grad_values], axis=1)
+    out_second = chip.shift(hold(out_sums[1].astype(LOW), both_part)).astype(F32)
+    joined = hold(joined, out_second)
     grad_normed = jnp.einsum(
         "te,de->td", joined[:, :half], weight_qk, preferred_element_type=F32
     ) + jnp.einsum("te,de->td", grad_values, weight_v, preferred_element_type=F32)
@@ -435,18 +487,32 @@
     tile = jnp.stack([grad_gain_a, grad_gain_f, bias_sums[:D]] + short, axis=1).astype(LOW)
     tile = jnp.pad(tile, ((0, 0), (0, HEAD - tile.shape[1])))
     part_in = jnp.concatenate([part_in, tile], axis=1)
-    part_down = jnp.einsum(
-        "tf,td->fd",
-        hold(jnp.concatenate(actives, axis=0), part_in),
-        jnp.concatenate(upstream, axis=0),
-        preferred_element_type=F32,
-    ).astype(LOW)[:real]
-    part_down = lax.psum_scatter(part_down, "ctx", scatter_dimension=0, tiled=True)
-    plane_grads = plane_sums(part_in, mixed_width // 2, sums)
+    out_sums.append(out_second + out_parts[3 % len(outs)])
+    core_grads = core_sums(part_in)
+    for step in range(4, n_dp // 2 + 1):
+        sent = hold(out_sums[-1].astype(LOW), part_in)
+        out_sums.append(chip.shift(sent).astype(F32) + out_parts[step % len(outs)])
+    first_output = (
+        inner.scatter(core_output[..., : D // 2], 2).astype(LOW),
+        outer.scatter(core_output[..., D // 2 :], 1).astype(LOW),
+    )
+    plane_output = [
+        outer.scatter(first_output[0], 1).astype(LOW),
+        inner.scatter(first_output[1], 1).astype(LOW),
+    ]
+    middle_cut = mixed_width // 2
+    first_grads = (
+        inner.scatter(core_grads[..., :middle_cut], 2).astype(LOW),
+        outer.scatter(core_grads[..., middle_cut:], 1).astype(LOW),
+    )
+    plane_grads = [
+        outer.scatter(hold(first_grads[0], sums), 1).astype(LOW),
+        inner.scatter(hold(first_grads[1], sums), 1).astype(LOW),
+    ]
     plane_grads = jnp.concatenate(plane_grads + plane_output, axis=-1)
-    layer_output = (middle + hold(part_out, plane_grads).astype(F32)).astype(LOW)
-    down_weight_grad = hold(part_down, plane_grads).astype(F32)
-    in_grads = chip.scatter(plane_grads, 0)
+    layer_output = (middle + out_sums[-1]).astype(LOW)
+    down_weight_grad = part_down.astype(F32)
+    in_grads = chip.scatter(hold(plane_grads, out_sums[-1]), 0)
     output_weight_grad = in_grads[:, mixed_width + HEAD :]
     small = in_grads[:, mixed_width : mixed_width + HEAD].T
     return (

time: 720 us -> 704 us (0.978)
  matrix products: 162 us -> 131 us
  Pallas kernels: 0 us -> 30.3 us
  local copies, waits for them, and re-layouts: 144 us -> 116 us
  other arithmetic: 77 us -> 99.6 us
  waiting for transfers between devices: 231 us -> 211 us
  between operations: 46 us -> 55.7 us
    pallas_call x0 -> x2, Pallas kernels: none -> 30.3 us  [the longest x1 20 us: attend_back(): pl.pallas_call(attend_back_kernel, grid=(HEADS,), in_specs=[pl.BlockSpec(...]
    dot_general x18 -> x12, matrix products: 81.1 us -> 56.1 us  [the longest x2 24.2 us: plane_sum(): jnp.einsum('td,tf->df', fed_all, hold(jnp.concatenate(parts, axis=0), wai...]
    unnamed x248 -> x250, local copies, waits for them, and re-layouts: 42.5 us -> 20.6 us
    ppermute x40 -> x44, waiting for transfers between devices: 188 us -> 169 us  [shift(): return lax.ppermute(value, self.axis, self.up)]
    all_to_all x1, waiting for transfers between devices: 16.9 us -> 0.01 us  [per_device(): units = lax.all_to_all(hold(units, *plane_in), 'dp', 0, 0, tiled=True)]
    select_n x6 -> x22, other arithmetic: 8.93 us -> 23.7 us  [hold(): value = jnp.where(first != first, jnp.zeros_like(value), value)]
    ppermute x3, waiting for transfers between devices: 2.53 us -> 14.5 us  [direct(): lax.ppermute(block, self.axis, [(i, self.there(i, step)) for i in range(l...]
    ppermute x3, waiting for transfers between devices: 5.79 us -> 14.7 us  [per_device(): lax.ppermute(both, 'ctx', [(i, (i + step) % n_ctx) for i in range(n_ctx)])]
  transfers between devices with their start and end apart: 54 -> 57, of which waited for: 28 -> 29; matrix products, arithmetic and copies ran while one was open for 48% -> 45% of each run, Pallas kernels for 0% -> 4%
where the time goes in v3:
time: 704 us; the launch traced here: 694 us
  waiting for transfers between devices  211 us (30%)
  matrix products  131 us (19%)
  local copies, waits for them, and re-layouts  116 us (16%)
  other arithmetic  99.6 us (14%)
  between operations  55.7 us (8%)
  starting transfers between devices  50.2 us (7%)
  Pallas kernels  30.3 us (4%)
    ppermute x44, waiting for transfers between devices, shift(): return lax.ppermute(value, self.axis, self.up)  169 us
    ppermute x44, starting transfers between devices, shift(): return lax.ppermute(value, self.axis, self.up)  28.8 us
    another operation x21, other arithmetic, ordered(): jnp.stack([jnp.where(first, parts[0], parts[1]), jnp.where(first, parts[1...  26 us
    dot_general x2, matrix products, plane_sum(): jnp.einsum('td,tf->df', fed_all, hold(jnp.concatenate(parts, axis=0), wai...  24.2 us
    select_n x22, other arithmetic, hold(): value = jnp.where(first != first, jnp.zeros_like(value), value)  23.7 us
    unnamed x250, local copies, waits for them, and re-layouts  20.6 us
    pallas_call x1, Pallas kernels, attend_back(): pl.pallas_call(attend_back_kernel, grid=(HEADS,), in_specs=[pl.BlockSpec(...  20 us
    slice x29, local copies, waits for them, and re-layouts, hold(): first = other[(0,) * other.ndim]  18.9 us
  transfers between devices with their start and end apart: 57, of which 29 were waited for; matrix products, arithmetic and copies ran while one was open for 45% of the time, Pallas kernels for 4%

profile of v3, /device:TPU:0, one launch (start us, length us, event | category | flops | bytes accessed | tf_op | source)
XLA Modules:
  0.0 693.9 jit_solution(1880166757288104393)
XLA Ops:
  12.1 3.1 collective-permute-start.2
  20.5 5.1 collective-permute-done.2
  37.7 9.8 %collective-permute-done.4 = bf16[48,3712]{1,0:T(8,128)(2,1)S(1)} collective-permute-done((bf16[48,3712]{1,0:T(8,128)(2,1)S(1)}, bf16[48,3712]{1,0:T(8,128)(2,1)S(1)}, u32[]{:S(2)}, u32[]{:S(2)}) %collective-permute-start.4) | collective-permute-done | bytes 356384 | tf_op jit(solution)/shard_map/ppermute | solution.py:157
  52.3 10.3 %collective-permute-done.5 = bf16[4,48,1792]{2,1,0:T(8,128)(2,1)S(1)} collective-permute-done((bf16[4,48,1792]{2,1,0:T(8,128)(2,1)S(1)}, bf16[4,48,1792]{2,1,0:T(8,128)(2,1)S(1)}, u32[]{:S(2)}, u32[]{:S(2)}) %collective-permute-start.5) | collective-permute-done | bytes 688160 | tf_op jit(solution)/shard_map/ppermute | solution.py:157
  72.4 26.1 %collective-permute-done.8 = bf16[4,2,48,1792]{3,2,0,1:T(8,128)(2,1)} collective-permute-done((bf16[4,2,48,1792]{3,2,0,1:T(8,128)(2,1)}, bf16[4,2,48,1792]{3,2,0,1:T(8,128)(2,1)}, u32[]{:S(2)}, u32[]{:S(2)}) %collective-permute-start.8) | collective-permute-done | bytes 1376288 | tf_op jit(solution)/shard_map/ppermute | solution.py:157
  112.3 3.5 stack_reshape.20
  115.8 3.4 stack_reshape.21
  123.6 4.3 all-to-all-start
  141.5 3.1 pad_maximum_fusion.1
  147.7 4.2 fusion.172
  156.3 3.7 collective-permute-done.11
  185.7 8.8 %collective-permute-done.13 = bf16[256,512]{0,1:T(8,128)(2,1)} collective-permute-done((bf16[256,512]{0,1:T(8,128)(2,1)}, bf16[256,512]{0,1:T(8,128)(2,1)}, u32[]{:S(2)}, u32[]{:S(2)}) %collective-permute-start.13) | collective-permute-done | bytes 262176 | tf_op jit(solution)/shard_map/ppermute | solution.py:342
  195.6 5.0 collective-permute-done.14
  206.2 10.3 %shard_map.254 = bf16[256,1536]{1,0:T(8,128)(2,1)S(1)} custom-call(bf16[256,1536]{1,0:T(8,128)(2,1)S(1)} %copy.166.q_ref, bf16[1024,512]{1,0:T(8,128)(2,1)S(1)} %bitcast.320, bf16[1024,512]{1,0:T(8,128)(2,1)S(1)} %bitcast.321, f32[256,1024]{1,0:T(8,128)S(1)} %fusion.94.bias_ref), custom_call_target="tpu_custom_call" | custom-call | flops 10000000000 | bytes 1000000 | tf_op jit(solution)/shard_map/pallas_call | solution.py:59
  216.5 4.1 multiply_reduce_fusion.2
  227.2 16.3 %collective-permute-done.17 = bf16[256,1536]{1,0:T(8,128)(2,1)} collective-permute-done((bf16[256,1536]{1,0:T(8,128)(2,1)}, bf16[256,1536]{1,0:T(8,128)(2,1)}, u32[]{:S(2)}, u32[]{:S(2)}) %collective-permute-start.17) | collective-permute-done | bytes 786464 | tf_op jit(solution)/shard_map/ppermute | solution.py:157
  246.3 15.5 %collective-permute-done.19 = bf16[256,1536]{1,0:T(8,128)(2,1)S(1)} collective-permute-done((bf16[256,1536]{1,0:T(8,128)(2,1)}, bf16[256,1536]{1,0:T(8,128)(2,1)S(1)}, u32[]{:S(2)}, u32[]{:S(2)}) %collective-permute-start.19) | collective-permute-done | bytes 786464 | tf_op jit(solution)/shard_map/ppermute | solution.py:157
  261.8 5.7 constant_dynamic-slice_fusion.10
  267.5 3.7 fusion.186
  275.7 4.3 multiply_convert_fusion.6
  298.3 4.1 multiply_convert_fusion.4
  317.8 3.9 multiply_convert_fusion.2
  333.6 12.9 %collective-permute-done.25 = bf16[256,1536]{1,0:T(8,128)(2,1)S(1)} collective-permute-done((bf16[256,1536]{1,0:T(8,128)(2,1)S(1)}, bf16[256,1536]{1,0:T(8,128)(2,1)S(1)}, u32[]{:S(2)}, u32[]{:S(2)}) %collective-permute-start.25) | collective-permute-done | bytes 786464 | tf_op jit(solution)/shard_map/ppermute | solution.py:157
  353.0 3.9 multiply_convert_fusion
  360.3 18.8 %collective-permute-done.27 = bf16[256,1536]{1,0:T(8,128)(2,1)S(1)} collective-permute-done((bf16[256,1536]{1,0:T(8,128)(2,1)S(1)}, bf16[256,1536]{1,0:T(8,128)(2,1)S(1)}, u32[]{:S(2)}, u32[]{:S(2)}) %collective-permute-start.27) | collective-permute-done | bytes 786464 | tf_op jit(solution)/shard_map/ppermute | solution.py:157
  397.6 11.2 %convolution_convert_fusion.3 = bf16[1536,1152]{1,0:T(8,128)(2,1)S(1)} fusion(bf16[512,1152]{1,0:T(8,128)(2,1)} %copy-done.114, bf16[512,1152]{1,0:T(8,128)(2,1)} %copy-done.113, bf16[512,1152]{1,0:T(8,128)(2,1)} %copy-done.112, bf16[512,1152]{1,0:T(8,128)(2,1)} %copy-done.115, pred[]{:T(512)} %bitcast.91, bf16[512,1536]{1,0:T(8,128)(2,1)} %bitcast.383, ...), kind=kOutput, calls=%fused_computation.8 | convolution fusion | flops 7295926272 | bytes 14548993 | tf_op jit(solution)/shard_map/td,tf->df/dot_general | solution.py:414
  415.5 4.1 collective-permute-done.29
  419.7 4.6 multiply_reduce_fusion
  429.0 4.1 fusion.53.g_ref
  433.1 20.0 %shard_map.255 = (f32[256,1536]{1,0:T(8,128)S(1)}, bf16[2,1024,256]{2,1,0:T(8,128)(2,1)S(1)}) custom-call(bf16[256,1536]{1,0:T(8,128)(2,1)S(1)} %copy-done.6, bf16[256,1536]{1,0:T(8,128)(2,1)S(1)} %fusion.53.g_ref, bf16[1024,512]{1,0:T(8,128)(2,1)S(1)} %bitcast.322, bf16[1024,512]{1,0:T(8,128)(2,1)S(1)} %bitcast.323, f32[1024,256]{1,0:T(8,128)S(1)} %copy-done.2), custom_call_target="tpu_custom_call" | custom-call | flops 20000000000 | bytes 1000000 | tf_op jit(solution)/shard_map/pallas_call | solution.py:106
  466.8 13.0 %convolution_convert_fusion.2 = bf16[1536,1152]{1,0:T(8,128)(2,1)} fusion(bf16[512,1152]{1,0:T(8,128)(2,1)} %copy-done.117, bf16[512,1152]{1,0:T(8,128)(2,1)} %copy-done.116, bf16[512,1152]{1,0:T(8,128)(2,1)} %copy-done.119, bf16[512,1152]{1,0:T(8,128)(2,1)} %copy-done.118, pred[]{:T(512)} %bitcast.96, bf16[512,1536]{1,0:T(8,128)(2,1)} %bitcast.384, ...), kind=kOutput, calls=%fused_computation.7 | convolution fusion | flops 7295926272 | bytes 14548993 | tf_op jit(solution)/shard_map/td,tf->df/dot_general | solution.py:414
  486.8 3.3 collective-permute-start.34
  491.9 3.4 collective-permute-start.35
  499.0 8.4 %collective-permute-done.34 = bf16[2,256,256]{1,2,0:T(8,128)(2,1)} collective-permute-done((bf16[2,256,256]{1,2,0:T(8,128)(2,1)}, bf16[2,256,256]{1,2,0:T(8,128)(2,1)}, u32[]{:S(2)}, u32[]{:S(2)}) %collective-permute-start.34) | collective-permute-done | bytes 262176 | tf_op jit(solution)/shard_map/ppermute | solution.py:186
  507.4 6.1 collective-permute-done.35
  526.8 4.8 fusion.100
  536.2 3.2 convolution_convert_fusion
  546.3 11.4 %fusion.7 = bf16[1152,1536]{1,0:T(8,128)(2,1)S(1)} fusion(bf16[512,1536]{1,0:T(8,128)(2,1)} %get-tuple-element.45, bf16[512,1536]{1,0:T(8,128)(2,1)} %get-tuple-element.46, bf16[512,1536]{1,0:T(8,128)(2,1)} %get-tuple-element.44, bf16[512,1536]{1,0:T(8,128)(2,1)} %get-tuple-element.47, bf16[512,1152]{1,0:T(8,128)(2,1)} %copy-done.120, ...), kind=kOutput, calls=%fused_computation.17 | convolution fusion | flops 7294156800 | bytes 14548993 | tf_op jit(solution)/shard_map/tf,td->fd/dot_general | solution.py:453
  574.7 6.2 all-to-all-start.1
  582.1 5.6 collective-permute-done.36
  587.7 3.1 add_convert_fusion
  592.6 6.4 collective-permute-done.43
  612.8 12.4 %all-to-all-done.1 = bf16[8,2,48,1152]{3,2,1,0:T(8,128)(2,1)} async-done(((bf16[8,2,48,1152]{3,2,1,0:T(8,128)(2,1)}), bf16[8,2,48,1152]{3,2,1,0:T(8,128)(2,1)}, u32[]{:S(2)}, u32[]{:S(2)}) %all-to-all-start.1) | async-done | bytes 1769504 | tf_op jit(solution)/shard_map/all_to_all | solution.py:460
  627.7 6.3 collective-permute-done.38
  640.8 5.0 collective-permute-done.39
  645.8 4.0 collective-permute-done.41
  653.4 8.0 %collective-permute-done.47 = bf16[48,3712]{1,0:T(8,128)(2,1)S(1)} collective-permute-done((bf16[48,3712]{1,0:T(8,128)(2,1)S(1)}, bf16[48,3712]{1,0:T(8,128)(2,1)S(1)}, u32[]{:S(2)}, u32[]{:S(2)}) %collective-permute-start.47) | collective-permute-done | bytes 356384 | tf_op jit(solution)/shard_map/ppermute | solution.py:157
  679.9 3.2 collective-permute-done.49
  (585 shorter events, 286.5 us)
Async XLA Ops:
  7.2 254.6 %all-gather.5.cloned.1.call-start = ((), (), s32[]{:S(2)}) async-start(), calls=%async_computation.6 | async-start | bytes 7077888 | tf_op jit(solution)/shard_map/all_gather | solution.py:270
  12.1 13.5 %collective-permute-start.2 = (bf16[48,3712]{1,0:T(8,128)(2,1)S(1)}, bf16[48,3712]{1,0:T(8,128)(2,1)}, u32[]{:S(2)}, u32[]{:S(2)}) collective-permute-start(bf16[48,3712]{1,0:T(8,128)(2,1)S(1)} %pad_dynamic-update-slice_fusion), channel_id=1, source_target_pairs={{0,8},{4,12},{8,16},{12,20},{16,24},{20,28},{24,0},{28,4},{1,9},{5... | collective-permute-start | bytes 1069064 | tf_op jit(solution)/shard_map/ppermute | solution.py:157
  17.2 11.6 %collective-permute-start = (bf16[280,768]{1,0:T(8,128)(2,1)}, bf16[280,768]{1,0:T(8,128)(2,1)S(1)}, u32[]{:S(2)}, u32[]{:S(2)}) collective-permute-start(bf16[280,768]{1,0:T(8,128)(2,1)} %get-tuple-element.107), channel_id=1, source_target_pairs={{0,2},{1,3},{2,0},{3,1},{4,6},{5,7},{6,4},{7,5},{8,10},{9,11},{10,... | collective-permute-start | bytes 1290248 | tf_op jit(solution)/shard_map/ppermute | solution.py:157
  18.8 11.4 %collective-permute-start.1 = (bf16[280,768]{1,0:T(8,128)(2,1)}, bf16[280,768]{1,0:T(8,128)(2,1)}, u32[]{:S(2)}, u32[]{:S(2)}) collective-permute-start(bf16[280,768]{1,0:T(8,128)(2,1)} %get-tuple-element.108), channel_id=1, source_target_pairs={{0,1},{1,0},{2,3},{3,2},{4,5},{5,4},{6,7},{7,6},{8,9},{9,8},{10,11... | collective-permute-start | bytes 1290248 | tf_op jit(solution)/shard_map/ppermute | solution.py:157
  25.6 11.5 %collective-permute-start.3 = (bf16[48,3712]{1,0:T(8,128)(2,1)}, bf16[48,3712]{1,0:T(8,128)(2,1)S(1)}, u32[]{:S(2)}, u32[]{:S(2)}) collective-permute-start(bf16[48,3712]{1,0:T(8,128)(2,1)} %collective-permute-done.2), channel_id=1, source_target_pairs={{0,8},{4,12},{8,16},{12,20},{16,24},{20,28},{24,0},{28,4},{1,9},{5... | collective-permute-start | bytes 1069064 | tf_op jit(solution)/shard_map/ppermute | solution.py:157
  37.1 10.4 %collective-permute-start.4 = (bf16[48,3712]{1,0:T(8,128)(2,1)S(1)}, bf16[48,3712]{1,0:T(8,128)(2,1)S(1)}, u32[]{:S(2)}, u32[]{:S(2)}) collective-permute-start(bf16[48,3712]{1,0:T(8,128)(2,1)S(1)} %collective-permute-done.3), channel_id=1, source_target_pairs={{0,8},{4,12},{8,16},{12,20},{16,24},{20,28},{24,0},{28,4},{1,9},{5... | collective-permute-start | bytes 1069064 | tf_op jit(solution)/shard_map/ppermute | solution.py:157
  47.8 14.8 %collective-permute-start.5 = (bf16[4,48,1792]{2,1,0:T(8,128)(2,1)S(1)}, bf16[4,48,1792]{2,1,0:T(8,128)(2,1)S(1)}, u32[]{:S(2)}, u32[]{:S(2)}) collective-permute-start(bf16[4,48,1792]{2,1,0:T(8,128)(2,1)S(1)} %slice.366), channel_id=1, source_target_pairs={{0,1},{1,0},{2,3},{3,2},{4,5},{5,4},{6,7},{7,6},{8,9},{9,8},{10,11... | collective-permute-start | bytes 2064392 | tf_op jit(solution)/shard_map/ppermute | solution.py:157
  48.9 15.6 %collective-permute-start.6 = (bf16[4,48,1920]{2,1,0:T(8,128)(2,1)S(1)}, bf16[4,48,1920]{2,1,0:T(8,128)(2,1)S(1)}, u32[]{:S(2)}, u32[]{:S(2)}) collective-permute-start(bf16[4,48,1920]{2,1,0:T(8,128)(2,1)S(1)} %slice.368), channel_id=1, source_target_pairs={{0,2},{1,3},{2,0},{3,1},{4,6},{5,7},{6,4},{7,5},{8,10},{9,11},{10,... | collective-permute-start | bytes 2211848 | tf_op jit(solution)/shard_map/ppermute | solution.py:157
  66.0 35.9 %collective-permute-start.7 = (bf16[4,2,48,1920]{3,2,1,0:T(8,128)(2,1)}, bf16[4,2,48,1920]{3,2,1,0:T(8,128)(2,1)}, u32[]{:S(2)}, u32[]{:S(2)}) collective-permute-start(bf16[4,2,48,1920]{3,2,1,0:T(8,128)(2,1)} %maximum_select_fusion.9), channel_id=1, source_target_pairs={{0,1},{1,0},{2,3},{3,2},{4,5},{5,4},{6,7},{7,6},{8,9},{9,8},{10,11... | collective-permute-start | bytes 4423688 | tf_op jit(solution)/shard_map/ppermute | solution.py:157
  70.1 28.4 %collective-permute-start.8 = (bf16[4,2,48,1792]{3,2,0,1:T(8,128)(2,1)}, bf16[4,2,48,1792]{3,2,0,1:T(8,128)(2,1)}, u32[]{:S(2)}, u32[]{:S(2)}) collective-permute-start(bf16[4,2,48,1792]{3,2,0,1:T(8,128)(2,1)} %maximum_select_fusion.11), channel_id=1, source_target_pairs={{0,2},{1,3},{2,0},{3,1},{4,6},{5,7},{6,4},{7,5},{8,10},{9,11},{10,... | collective-permute-start | bytes 4128776 | tf_op jit(solution)/shard_map/ppermute | solution.py:157
  107.5 20.7 %collective-permute-start.10 = (bf16[4,2,2,48,1792]{4,3,0,2,1:T(8,128)(2,1)}, bf16[4,2,2,48,1792]{4,3,0,2,1:T(8,128)(2,1)}, u32[]{:S(2)}, u32[]{:S(2)}) collective-permute-start(bf16[4,2,2,48,1792]{4,3,0,2,1:T(8,128)(2,1)} %fusion.51), channel_id=1, source_target_pairs={{0,4},{4,0},{8,12},{12,8},{16,20},{20,16},{24,28},{28,24},{1,5},{5... | collective-permute-start | bytes 8257544 | tf_op jit(solution)/shard_map/ppermute | solution.py:157
  109.9 29.3 %collective-permute-start.9 = (bf16[4,2,2,48,1920]{4,3,2,1,0:T(8,128)(2,1)}, bf16[4,2,2,48,1920]{4,3,2,1,0:T(8,128)(2,1)}, u32[]{:S(2)}, u32[]{:S(2)}) collective-permute-start(bf16[4,2,2,48,1920]{4,3,2,1,0:T(8,128)(2,1)} %fusion.48), channel_id=1, source_target_pairs={{0,4},{4,0},{8,12},{12,8},{16,20},{20,16},{24,28},{28,24},{1,5},{5... | collective-permute-start | bytes 8847368 | tf_op jit(solution)/shard_map/ppermute | solution.py:157
  123.6 48.9 %all-to-all-start = ((bf16[8,2,48,1152]{3,2,1,0:T(8,128)(2,1)}), bf16[8,2,48,1152]{3,2,1,0:T(8,128)(2,1)}, u32[]{:S(2)}, u32[]{:S(2)}) async-start(bf16[8,2,48,1152]{3,2,1,0:T(8,128)(2,1)} %copy.167), calls=%async_computation | async-start | bytes 3538944 | tf_op jit(solution)/shard_map/all_to_all | solution.py:278
  127.9 139.6 %all-gather.3.cloned.1.call-start = ((), (), s32[]{:S(2)}) async-start(), calls=%async_computation.5 | async-start | bytes 8847360 | tf_op jit(solution)/shard_map/all_gather | solution.py:348
  136.2 28.1 %collective-permute-start.12 = (bf16[2,280,768]{2,1,0:T(8,128)(2,1)}, bf16[2,280,768]{2,1,0:T(8,128)(2,1)}, u32[]{:S(2)}, u32[]{:S(2)}) collective-permute-start(bf16[2,280,768]{2,1,0:T(8,128)(2,1)} %maximum_select_fusion.14), channel_id=1, source_target_pairs={{0,2},{1,3},{2,0},{3,1},{4,6},{5,7},{6,4},{7,5},{8,10},{9,11},{10,... | collective-permute-start | bytes 2580488 | tf_op jit(solution)/shard_map/ppermute | solution.py:157
  138.5 21.4 %collective-permute-start.11 = (bf16[2,280,768]{2,1,0:T(8,128)(2,1)}, bf16[2,280,768]{2,1,0:T(8,128)(2,1)}, u32[]{:S(2)}, u32[]{:S(2)}) collective-permute-start(bf16[2,280,768]{2,1,0:T(8,128)(2,1)} %maximum_select_fusion.13), channel_id=1, source_target_pairs={{0,1},{1,0},{2,3},{3,2},{4,5},{5,4},{6,7},{7,6},{8,9},{9,8},{10,11... | collective-permute-start | bytes 2580488 | tf_op jit(solution)/shard_map/ppermute | solution.py:157
  176.1 394.2 %reduce-scatter.6.cloned.1.call-start = ((), (), s32[]{:S(2)}) async-start(), calls=%async_computation.7 | async-start | bytes 4423680 | tf_op jit(solution)/shard_map/reduce_scatter | solution.py:420
  181.2 13.3 %collective-permute-start.13 = (bf16[256,512]{0,1:T(8,128)(2,1)}, bf16[256,512]{0,1:T(8,128)(2,1)}, u32[]{:S(2)}, u32[]{:S(2)}) collective-permute-start(bf16[256,512]{0,1:T(8,128)(2,1)} %fusion.139), channel_id=1, source_target_pairs={{0,1},{1,2},{2,3},{3,0},{4,5},{5,6},{6,7},{7,4},{8,9},{9,10},{10,1... | collective-permute-start | bytes 786440 | tf_op jit(solution)/shard_map/ppermute | solution.py:342
  181.9 18.7 %collective-permute-start.14 = (bf16[256,512]{0,1:T(8,128)(2,1)}, bf16[256,512]{0,1:T(8,128)(2,1)S(1)}, u32[]{:S(2)}, u32[]{:S(2)}) collective-permute-start(bf16[256,512]{0,1:T(8,128)(2,1)} %fusion.139), channel_id=1, source_target_pairs={{0,2},{1,3},{2,0},{3,1},{4,6},{5,7},{6,4},{7,5},{8,10},{9,11},{10,... | collective-permute-start | bytes 786440 | tf_op jit(solution)/shard_map/ppermute | solution.py:342
  183.2 20.1 %collective-permute-start.15 = (bf16[256,512]{0,1:T(8,128)(2,1)}, bf16[256,512]{0,1:T(8,128)(2,1)}, u32[]{:S(2)}, u32[]{:S(2)}) collective-permute-start(bf16[256,512]{0,1:T(8,128)(2,1)} %fusion.139), channel_id=1, source_target_pairs={{0,3},{1,0},{2,1},{3,2},{4,7},{5,4},{6,5},{7,6},{8,11},{9,8},{10,9... | collective-permute-start | bytes 786440 | tf_op jit(solution)/shard_map/ppermute | solution.py:342
  224.2 19.4 %collective-permute-start.17 = (bf16[256,1536]{1,0:T(8,128)(2,1)}, bf16[256,1536]{1,0:T(8,128)(2,1)}, u32[]{:S(2)}, u32[]{:S(2)}) collective-permute-start(bf16[256,1536]{1,0:T(8,128)(2,1)} %fusion.52), channel_id=1, source_target_pairs={{0,8},{4,12},{8,16},{12,20},{16,24},{20,28},{24,0},{28,4},{1,9},{5... | collective-permute-start | bytes 2359304 | tf_op jit(solution)/shard_map/ppermute | solution.py:157
  225.7 17.8 %collective-permute-start.16 = (bf16[256,1536]{1,0:T(8,128)(2,1)}, bf16[256,1536]{1,0:T(8,128)(2,1)}, u32[]{:S(2)}, u32[]{:S(2)}) collective-permute-start(bf16[256,1536]{1,0:T(8,128)(2,1)} %fusion.52), channel_id=1, source_target_pairs={{0,4},{4,0},{8,12},{12,8},{16,20},{20,16},{24,28},{28,24},{1,5},{5... | collective-permute-start | bytes 2359304 | tf_op jit(solution)/shard_map/ppermute | solution.py:157
  243.5 18.3 %collective-permute-start.19 = (bf16[256,1536]{1,0:T(8,128)(2,1)}, bf16[256,1536]{1,0:T(8,128)(2,1)S(1)}, u32[]{:S(2)}, u32[]{:S(2)}) collective-permute-start(bf16[256,1536]{1,0:T(8,128)(2,1)} %collective-permute-done.17), channel_id=1, source_target_pairs={{0,8},{4,12},{8,16},{12,20},{16,24},{20,28},{24,0},{28,4},{1,9},{5... | collective-permute-start | bytes 2359304 | tf_op jit(solution)/shard_map/ppermute | solution.py:157
  261.8 61.8 %collective-permute-start.21 = (bf16[256,1536]{1,0:T(8,128)(2,1)S(1)}, bf16[256,1536]{1,0:T(8,128)(2,1)S(1)}, u32[]{:S(2)}, u32[]{:S(2)}) collective-permute-start(bf16[256,1536]{1,0:T(8,128)(2,1)S(1)} %collective-permute-done.19), channel_id=1, source_target_pairs={{0,8},{4,12},{8,16},{12,20},{16,24},{20,28},{24,0},{28,4},{1,9},{5... | collective-permute-start | bytes 2359304 | tf_op jit(solution)/shard_map/ppermute | solution.py:157
  309.6 14.7 %collective-permute-start.24 = (bf16[256,1536]{1,0:T(8,128)(2,1)S(1)}, bf16[256,1536]{1,0:T(8,128)(2,1)S(1)}, u32[]{:S(2)}, u32[]{:S(2)}) collective-permute-start(bf16[256,1536]{1,0:T(8,128)(2,1)S(1)} %dynamic-slice_convert_fusion.3), channel_id=1, source_target_pairs={{0,4},{4,0},{8,12},{12,8},{16,20},{20,16},{24,28},{28,24},{1,5},{5... | collective-permute-start | bytes 2359304 | tf_op jit(solution)/shard_map/ppermute | solution.py:157
  324.5 22.0 %collective-permute-start.25 = (bf16[256,1536]{1,0:T(8,128)(2,1)S(1)}, bf16[256,1536]{1,0:T(8,128)(2,1)S(1)}, u32[]{:S(2)}, u32[]{:S(2)}) collective-permute-start(bf16[256,1536]{1,0:T(8,128)(2,1)S(1)} %add_convert_fusion.3), channel_id=1, source_target_pairs={{0,8},{4,12},{8,16},{12,20},{16,24},{20,28},{24,0},{28,4},{1,9},{5... | collective-permute-start | bytes 2359304 | tf_op jit(solution)/shard_map/ppermute | solution.py:157
  357.3 21.8 %collective-permute-start.27 = (bf16[256,1536]{1,0:T(8,128)(2,1)S(1)}, bf16[256,1536]{1,0:T(8,128)(2,1)S(1)}, u32[]{:S(2)}, u32[]{:S(2)}) collective-permute-start(bf16[256,1536]{1,0:T(8,128)(2,1)S(1)} %add_convert_fusion.2), channel_id=1, source_target_pairs={{0,8},{4,12},{8,16},{12,20},{16,24},{20,28},{24,0},{28,4},{1,9},{5... | collective-permute-start | bytes 2359304 | tf_op jit(solution)/shard_map/ppermute | solution.py:157
  388.5 23.6 %collective-permute-start.23 = (bf16[4,256,1536]{2,1,0:T(8,128)(2,1)}, bf16[4,256,1536]{2,1,0:T(8,128)(2,1)}, u32[]{:S(2)}, u32[]{:S(2)}) collective-permute-start(bf16[4,256,1536]{2,1,0:T(8,128)(2,1)} %pad_maximum_fusion.3), channel_id=1, source_target_pairs={{0,4},{4,0},{8,12},{12,8},{16,20},{20,16},{24,28},{28,24},{1,5},{5... | collective-permute-start | bytes 9437192 | tf_op jit(solution)/shard_map/ppermute | solution.py:157
  393.0 22.5 %collective-permute-start.30 = (bf16[256,1536]{1,0:T(8,128)(2,1)}, bf16[256,1536]{1,0:T(8,128)(2,1)}, u32[]{:S(2)}, u32[]{:S(2)}) collective-permute-start(bf16[256,1536]{1,0:T(8,128)(2,1)} %dynamic-slice_convert_fusion), channel_id=1, source_target_pairs={{0,4},{4,0},{8,12},{12,8},{16,20},{20,16},{24,28},{28,24},{1,5},{5... | collective-permute-start | bytes 2359304 | tf_op jit(solution)/shard_map/ppermute | solution.py:157
  397.3 22.3 %collective-permute-start.29 = (bf16[256,1536]{1,0:T(8,128)(2,1)}, bf16[256,1536]{1,0:T(8,128)(2,1)}, u32[]{:S(2)}, u32[]{:S(2)}) collective-permute-start(bf16[256,1536]{1,0:T(8,128)(2,1)} %get-tuple-element.38), channel_id=1, source_target_pairs={{0,8},{4,12},{8,16},{12,20},{16,24},{20,28},{24,0},{28,4},{1,9},{5... | collective-permute-start | bytes 2359304 | tf_op jit(solution)/shard_map/ppermute | solution.py:157
  410.6 161.1 %reduce-scatter.8.cloned.1.call-start = ((), (), s32[]{:S(2)}) async-start(), calls=%async_computation.8 | async-start | bytes 4423680 | tf_op jit(solution)/shard_map/reduce_scatter | solution.py:420
  428.7 32.4 %collective-permute-start.31 = (bf16[256,1536]{1,0:T(8,128)(2,1)}, bf16[256,1536]{1,0:T(8,128)(2,1)}, u32[]{:S(2)}, u32[]{:S(2)}) collective-permute-start(bf16[256,1536]{1,0:T(8,128)(2,1)} %select_convert_fusion), channel_id=1, source_target_pairs={{0,8},{4,12},{8,16},{12,20},{16,24},{20,28},{24,0},{28,4},{1,9},{5... | collective-permute-start | bytes 2359304 | tf_op jit(solution)/shard_map/ppermute | solution.py:157
  461.1 103.9 %collective-permute-start.42 = (bf16[4,2,2,48,1536]{4,3,0,2,1:T(8,128)(2,1)}, bf16[4,2,2,48,1536]{4,3,0,2,1:T(8,128)(2,1)}, u32[]{:S(2)}, u32[]{:S(2)}) collective-permute-start(bf16[4,2,2,48,1536]{4,3,0,2,1:T(8,128)(2,1)} %bitcast.316), channel_id=1, source_target_pairs={{0,4},{4,0},{8,12},{12,8},{16,20},{20,16},{24,28},{28,24},{1,5},{5... | collective-permute-start | bytes 7077896 | tf_op jit(solution)/shard_map/ppermute | solution.py:157
  479.8 186.9 %reduce-scatter.10.cloned.1.call-start = ((), (), s32[]{:S(2)}) async-start(), calls=%async_computation.9 | async-start | bytes 4300800
  485.1 13.9 %collective-permute-start.33 = (bf16[2,256,256]{1,2,0:T(8,128)(2,1)}, bf16[2,256,256]{1,2,0:T(8,128)(2,1)}, u32[]{:S(2)}, u32[]{:S(2)}) collective-permute-start(bf16[2,256,256]{1,2,0:T(8,128)(2,1)} %bitcast.393), channel_id=1, source_target_pairs={{0,1},{1,2},{2,3},{3,0},{4,5},{5,6},{6,7},{7,4},{8,9},{9,10},{10,1... | collective-permute-start | bytes 786440 | tf_op jit(solution)/shard_map/ppermute | solution.py:186
  486.8 20.6 %collective-permute-start.34 = (bf16[2,256,256]{1,2,0:T(8,128)(2,1)}, bf16[2,256,256]{1,2,0:T(8,128)(2,1)}, u32[]{:S(2)}, u32[]{:S(2)}) collective-permute-start(bf16[2,256,256]{1,2,0:T(8,128)(2,1)} %bitcast.394), channel_id=1, source_target_pairs={{0,2},{1,3},{2,0},{3,1},{4,6},{5,7},{6,4},{7,5},{8,10},{9,11},{10,... | collective-permute-start | bytes 786440 | tf_op jit(solution)/shard_map/ppermute | solution.py:186
  491.9 21.6 %collective-permute-start.35 = (bf16[2,256,256]{1,2,0:T(8,128)(2,1)}, bf16[2,256,256]{1,2,0:T(8,128)(2,1)}, u32[]{:S(2)}, u32[]{:S(2)}) collective-permute-start(bf16[2,256,256]{1,2,0:T(8,128)(2,1)} %bitcast.395), channel_id=1, source_target_pairs={{0,3},{1,0},{2,1},{3,2},{4,7},{5,4},{6,5},{7,6},{8,11},{9,8},{10,9... | collective-permute-start | bytes 786440 | tf_op jit(solution)/shard_map/ppermute | solution.py:186
  499.0 24.9 %collective-permute-start.32 = (bf16[256,1536]{1,0:T(8,128)(2,1)}, bf16[256,1536]{1,0:T(8,128)(2,1)}, u32[]{:S(2)}, u32[]{:S(2)}) collective-permute-start(bf16[256,1536]{1,0:T(8,128)(2,1)} %fusion.107), channel_id=1, source_target_pairs={{0,8},{4,12},{8,16},{12,20},{16,24},{20,28},{24,0},{28,4},{1,9},{5... | collective-permute-start | bytes 2359304 | tf_op jit(solution)/shard_map/ppermute | solution.py:157
  546.3 54.1 %collective-permute-start.37 = (bf16[4,2,2,48,2176]{4,3,0,2,1:T(8,128)(2,1)}, bf16[4,2,2,48,2176]{4,3,0,2,1:T(8,128)(2,1)}, u32[]{:S(2)}, u32[]{:S(2)}) collective-permute-start(bf16[4,2,2,48,2176]{4,3,0,2,1:T(8,128)(2,1)} %bitcast.315), channel_id=1, source_target_pairs={{0,4},{4,0},{8,12},{12,8},{16,20},{20,16},{24,28},{28,24},{1,5},{5... | collective-permute-start | bytes 10027016 | tf_op jit(solution)/shard_map/ppermute | solution.py:157
  565.0 22.6 %collective-permute-start.36 = (bf16[256,1536]{1,0:T(8,128)(2,1)}, bf16[256,1536]{1,0:T(8,128)(2,1)}, u32[]{:S(2)}, u32[]{:S(2)}) collective-permute-start(bf16[256,1536]{1,0:T(8,128)(2,1)} %fusion.108), channel_id=1, source_target_pairs={{0,8},{4,12},{8,16},{12,20},{16,24},{20,28},{24,0},{28,4},{1,9},{5... | collective-permute-start | bytes 2359304 | tf_op jit(solution)/shard_map/ppermute | solution.py:157
  570.2 28.8 %collective-permute-start.43 = (bf16[4,2,48,768]{3,2,0,1:T(8,128)(2,1)S(1)}, bf16[4,2,48,768]{3,2,0,1:T(8,128)(2,1)}, u32[]{:S(2)}, u32[]{:S(2)}) collective-permute-start(bf16[4,2,48,768]{3,2,0,1:T(8,128)(2,1)S(1)} %dynamic-slice_bitcast_fusion.7), channel_id=1, source_target_pairs={{0,1},{1,0},{2,3},{3,2},{4,5},{5,4},{6,7},{7,6},{8,9},{9,8},{10,11... | collective-permute-start | bytes 1769480 | tf_op jit(solution)/shard_map/ppermute | solution.py:157
  574.7 50.5 %all-to-all-start.1 = ((bf16[8,2,48,1152]{3,2,1,0:T(8,128)(2,1)}), bf16[8,2,48,1152]{3,2,1,0:T(8,128)(2,1)}, u32[]{:S(2)}, u32[]{:S(2)}) async-start(bf16[8,2,48,1152]{3,2,1,0:T(8,128)(2,1)} %copy.182), calls=%async_computation.3 | async-start | bytes 3538944 | tf_op jit(solution)/shard_map/all_to_all | solution.py:460
  582.0 25.8 %collective-permute-start.45 = (bf16[4,2,48,768]{3,2,0,1:T(8,128)(2,1)S(1)}, bf16[4,2,48,768]{3,2,0,1:T(8,128)(2,1)S(1)}, u32[]{:S(2)}, u32[]{:S(2)}) collective-permute-start(bf16[4,2,48,768]{3,2,0,1:T(8,128)(2,1)S(1)} %dynamic-slice_bitcast_fusion.6), channel_id=1, source_target_pairs={{0,2},{1,3},{2,0},{3,1},{4,6},{5,7},{6,4},{7,5},{8,10},{9,11},{10,... | collective-permute-start | bytes 1769480 | tf_op jit(solution)/shard_map/ppermute | solution.py:157
  600.3 11.7 %collective-permute-start.44 = (bf16[4,48,768]{2,1,0:T(8,128)(2,1)S(1)}, bf16[4,48,768]{2,1,0:T(8,128)(2,1)S(1)}, u32[]{:S(2)}, u32[]{:S(2)}) collective-permute-start(bf16[4,48,768]{2,1,0:T(8,128)(2,1)S(1)} %dynamic-slice_bitcast_fusion.12), channel_id=1, source_target_pairs={{0,2},{1,3},{2,0},{3,1},{4,6},{5,7},{6,4},{7,5},{8,10},{9,11},{10,... | collective-permute-start | bytes 884744 | tf_op jit(solution)/shard_map/ppermute | solution.py:157
  604.8 29.2 %collective-permute-start.38 = (bf16[4,2,48,1024]{3,2,0,1:T(8,128)(2,1)}, bf16[4,2,48,1024]{3,2,0,1:T(8,128)(2,1)}, u32[]{:S(2)}, u32[]{:S(2)}) collective-permute-start(bf16[4,2,48,1024]{3,2,0,1:T(8,128)(2,1)} %dynamic-slice_bitcast_fusion.1), channel_id=1, source_target_pairs={{0,1},{1,0},{2,3},{3,2},{4,5},{5,4},{6,7},{7,6},{8,9},{9,8},{10,11... | collective-permute-start | bytes 2359304 | tf_op jit(solution)/shard_map/ppermute | solution.py:157
  605.9 31.7 %collective-permute-start.40 = (bf16[4,2,48,1152]{3,2,0,1:T(8,128)(2,1)}, bf16[4,2,48,1152]{3,2,0,1:T(8,128)(2,1)}, u32[]{:S(2)}, u32[]{:S(2)}) collective-permute-start(bf16[4,2,48,1152]{3,2,0,1:T(8,128)(2,1)} %dynamic-slice_bitcast_fusion), channel_id=1, source_target_pairs={{0,2},{1,3},{2,0},{3,1},{4,6},{5,7},{6,4},{7,5},{8,10},{9,11},{10,... | collective-permute-start | bytes 2654216 | tf_op jit(solution)/shard_map/ppermute | solution.py:157
  608.8 30.9 %collective-permute-start.46 = (bf16[4,48,768]{2,1,0:T(8,128)(2,1)}, bf16[4,48,768]{2,1,0:T(8,128)(2,1)}, u32[]{:S(2)}, u32[]{:S(2)}) collective-permute-start(bf16[4,48,768]{2,1,0:T(8,128)(2,1)} %dynamic-slice_bitcast_fusion.11), channel_id=1, source_target_pairs={{0,1},{1,0},{2,3},{3,2},{4,5},{5,4},{6,7},{7,6},{8,9},{9,8},{10,11... | collective-permute-start | bytes 884744 | tf_op jit(solution)/shard_map/ppermute | solution.py:157
  639.0 10.8 %collective-permute-start.41 = (bf16[4,48,1152]{2,1,0:T(8,128)(2,1)S(1)}, bf16[4,48,1152]{2,1,0:T(8,128)(2,1)S(1)}, u32[]{:S(2)}, u32[]{:S(2)}) collective-permute-start(bf16[4,48,1152]{2,1,0:T(8,128)(2,1)S(1)} %dynamic-slice_bitcast_fusion.8), channel_id=1, source_target_pairs={{0,1},{1,0},{2,3},{3,2},{4,5},{5,4},{6,7},{7,6},{8,9},{9,8},{10,11... | collective-permute-start | bytes 1327112 | tf_op jit(solution)/shard_map/ppermute | solution.py:157
  (130 other events, 1098.4 us)
Sparse Core Ops, SparseCore 0:
  72.5 63.0 all-gather.4
  176.2 84.0 all-gather.2
  410.7 49.6 reduce-scatter.5
  479.9 60.5 reduce-scatter.7
  559.8 67.7 reduce-scatter.9

commit v4 on v3

--- a/solution.py
+++ b/solution.py
@@ -364,7 +364,10 @@
         jnp.einsum("td,fd->tf", back, weight_d, preferred_element_type=F32).astype(LOW)
         for back in upstream
     ]
-    inputs_own = chip.ring(normed2)
+    inputs_own = [normed2, chip.shift(normed2)]
+    for step in range(2, n_dp // 2):
+        waits = grad_actives if step == 2 else ()
+        inputs_own.append(chip.shift(hold(inputs_own[-1], *waits)))
 
     def both_cores(part, *waits):
         part = hold(part, *waits)
@@ -389,15 +392,15 @@
             grad_active * upward * sigmoid_gate * (1.0 + gate * (1.0 - sigmoid_gate))
         ).astype(LOW)
         grad_upward = (grad_active * gate * sigmoid_gate).astype(LOW)
-        back_gate, back_upward = grad_gate, grad_upward
+        back_gate = grad_gate
         if step == 1:
             back_gate = hold(grad_gate, grads[0])
         if step > 1:
             arrived = chip.shift(grad_sums[-1].astype(LOW))
-            back_gate, back_upward = hold(grad_gate, arrived), hold(grad_upward, arrived)
+            back_gate = hold(grad_gate, arrived)
         grads.append(
             jnp.einsum("tf,df->td", back_gate, weight_g, preferred_element_type=F32)
-            + jnp.einsum("tf,df->td", back_upward, weight_u, preferred_element_type=F32)
+            + jnp.einsum("tf,df->td", grad_upward, weight_u, preferred_element_type=F32)
         )
         kept.append(core_sum(grads[-1]))
         if step > 0:

time: 704 us -> 699 us (level)
  waiting for transfers between devices: 211 us -> 199 us
    ppermute x44, waiting for transfers between devices: 169 us -> 147 us  [shift(): return lax.ppermute(value, self.axis, self.up)]
    all_gather x1, waiting for transfers between devices: 0.01 us -> 7.55 us  [per_device(): units_all = lax.all_gather(hold(units, both), 'ctx', axis=0, tiled=True)]
    dot_general x4, matrix products: 16.2 us -> 8.89 us  [per_device(): jnp.einsum('td,fd->tf', back, weight_d, preferred_element_type=F32)]
    unnamed x250 -> x266, local copies, waits for them, and re-layouts: 20.6 us -> 25.7 us
    slice x29 -> x33, local copies, waits for them, and re-layouts: 18.9 us -> 21 us  [hold(): first = other[(0,) * other.ndim]]
  transfers between devices with their start and end apart: 57 -> 57, of which waited for: 29 -> 29; matrix products, arithmetic and copies ran while one was open for 45% -> 44% of each run, Pallas kernels for 4% -> 4%
where the time goes in v4:
time: 699 us; the launch traced here: 688 us
  waiting for transfers between devices  199 us (28%)
  matrix products  127 us (18%)
  local copies, waits for them, and re-layouts  121 us (17%)
  other arithmetic  97.8 us (14%)
  between operations  61 us (9%)
  starting transfers between devices  51.9 us (7%)
  Pallas kernels  30.2 us (4%)
    ppermute x44, waiting for transfers between devices, shift(): return lax.ppermute(value, self.axis, self.up)  147 us
    ppermute x44, starting transfers between devices, shift(): return lax.ppermute(value, self.axis, self.up)  31.9 us
    unnamed x266, local copies, waits for them, and re-layouts  25.7 us
    another operation x21, other arithmetic, ordered(): jnp.stack([jnp.where(first, parts[0], parts[1]), jnp.where(first, parts[1...  24.3 us
    dot_general x2, matrix products, plane_sum(): jnp.einsum('td,tf->df', fed_all, hold(jnp.concatenate(parts, axis=0), wai...  24.2 us
    select_n x22, other arithmetic, hold(): value = jnp.where(first != first, jnp.zeros_like(value), value)  23.8 us
    slice x33, local copies, waits for them, and re-layouts, hold(): first = other[(0,) * other.ndim]  21 us
    pallas_call x1, Pallas kernels, attend_back(): pl.pallas_call(attend_back_kernel, grid=(HEADS,), in_specs=[pl.BlockSpec(...  20 us
  transfers between devices with their start and end apart: 57, of which 29 were waited for; matrix products, arithmetic and copies ran while one was open for 44% of the time, Pallas kernels for 4%

profile of v4, /device:TPU:0, one launch (start us, length us, event | category | flops | bytes accessed | tf_op | source)
XLA Modules:
  0.0 688.3 jit_solution(11021814466938745421)
XLA Ops:
  12.1 3.1 collective-permute-start.2
  20.5 5.1 collective-permute-done.2
  37.7 9.8 %collective-permute-done.4 = bf16[48,3712]{1,0:T(8,128)(2,1)S(1)} collective-permute-done((bf16[48,3712]{1,0:T(8,128)(2,1)S(1)}, bf16[48,3712]{1,0:T(8,128)(2,1)S(1)}, u32[]{:S(2)}, u32[]{:S(2)}) %collective-permute-start.4) | collective-permute-done | bytes 356384 | tf_op jit(solution)/shard_map/ppermute | solution.py:157
  52.3 10.3 %collective-permute-done.5 = bf16[4,48,1792]{2,1,0:T(8,128)(2,1)S(1)} collective-permute-done((bf16[4,48,1792]{2,1,0:T(8,128)(2,1)S(1)}, bf16[4,48,1792]{2,1,0:T(8,128)(2,1)S(1)}, u32[]{:S(2)}, u32[]{:S(2)}) %collective-permute-start.5) | collective-permute-done | bytes 688160 | tf_op jit(solution)/shard_map/ppermute | solution.py:157
  72.3 26.1 %collective-permute-done.8 = bf16[4,2,48,1792]{3,2,0,1:T(8,128)(2,1)} collective-permute-done((bf16[4,2,48,1792]{3,2,0,1:T(8,128)(2,1)}, bf16[4,2,48,1792]{3,2,0,1:T(8,128)(2,1)}, u32[]{:S(2)}, u32[]{:S(2)}) %collective-permute-start.8) | collective-permute-done | bytes 1376288 | tf_op jit(solution)/shard_map/ppermute | solution.py:157
  112.4 3.6 stack_reshape.20
  115.9 3.4 stack_reshape.21
  123.7 4.3 all-to-all-start
  141.9 3.1 pad_maximum_fusion.1
  148.2 4.2 fusion.180
  184.4 8.4 %collective-permute-done.13 = bf16[256,512]{0,1:T(8,128)(2,1)} collective-permute-done((bf16[256,512]{0,1:T(8,128)(2,1)}, bf16[256,512]{0,1:T(8,128)(2,1)}, u32[]{:S(2)}, u32[]{:S(2)}) %collective-permute-start.13) | collective-permute-done | bytes 262176 | tf_op jit(solution)/shard_map/ppermute | solution.py:342
  193.9 5.9 collective-permute-done.14
  206.4 10.3 %shard_map.254 = bf16[256,1536]{1,0:T(8,128)(2,1)S(1)} custom-call(bf16[256,1536]{1,0:T(8,128)(2,1)S(1)} %copy.166.q_ref, bf16[1024,512]{1,0:T(8,128)(2,1)S(1)} %bitcast.326, bf16[1024,512]{1,0:T(8,128)(2,1)S(1)} %bitcast.327, f32[256,1024]{1,0:T(8,128)S(1)} %fusion.106.bias_ref), custom_call_target="tpu_custom_call" | custom-call | flops 10000000000 | bytes 1000000 | tf_op jit(solution)/shard_map/pallas_call | solution.py:59
  216.7 4.4 multiply_reduce_fusion.2
  230.8 3.4 constant_dynamic-slice_fusion.11
  251.6 7.5 %all-gather.3.cloned.1.call-done = bf16[3072,1152]{1,0:T(8,128)(2,1)} async-done(((bf16[768,1152]{1,0:T(8,128)(2,1)}), bf16[3072,1152]{1,0:T(8,128)(2,1)}) %all-gather.3.cloned.1.call-update) | async-done | bytes 7077904 | tf_op jit(solution)/shard_map/all_gather | solution.py:348
  259.1 3.7 fusion.194
  285.5 3.0 fusion.59
  290.5 3.0 collective-permute-done.19
  304.9 2.9 fusion.64
  309.7 10.5 %collective-permute-done.21 = bf16[256,1536]{1,0:T(8,128)(2,1)S(1)} collective-permute-done((bf16[256,1536]{1,0:T(8,128)(2,1)S(1)}, bf16[256,1536]{1,0:T(8,128)(2,1)S(1)}, u32[]{:S(2)}, u32[]{:S(2)}) %collective-permute-start.21) | collective-permute-done | bytes 786464 | tf_op jit(solution)/shard_map/ppermute | solution.py:157
  326.7 15.8 %collective-permute-done.25 = bf16[256,1536]{1,0:T(8,128)(2,1)S(1)} collective-permute-done((bf16[256,1536]{1,0:T(8,128)(2,1)S(1)}, bf16[256,1536]{1,0:T(8,128)(2,1)S(1)}, u32[]{:S(2)}, u32[]{:S(2)}) %collective-permute-start.25) | collective-permute-done | bytes 786464 | tf_op jit(solution)/shard_map/ppermute | solution.py:157
  356.4 17.9 %collective-permute-done.27 = bf16[256,1536]{1,0:T(8,128)(2,1)S(1)} collective-permute-done((bf16[256,1536]{1,0:T(8,128)(2,1)S(1)}, bf16[256,1536]{1,0:T(8,128)(2,1)S(1)}, u32[]{:S(2)}, u32[]{:S(2)}) %collective-permute-start.27) | collective-permute-done | bytes 786464 | tf_op jit(solution)/shard_map/ppermute | solution.py:157
  393.8 11.2 %convolution_convert_fusion.3 = bf16[1536,1152]{1,0:T(8,128)(2,1)S(1)} fusion(bf16[512,1152]{1,0:T(8,128)(2,1)} %copy-done.122, bf16[512,1152]{1,0:T(8,128)(2,1)} %copy-done.121, bf16[512,1152]{1,0:T(8,128)(2,1)} %copy-done.120, bf16[512,1152]{1,0:T(8,128)(2,1)} %copy-done.123, pred[]{:T(512)} %bitcast.95, bf16[512,1536]{1,0:T(8,128)(2,1)} %bitcast.389, ...), kind=kOutput, calls=%fused_computation.8 | convolution fusion | flops 7295926272 | bytes 14548993 | tf_op jit(solution)/shard_map/td,tf->df/dot_general | solution.py:417
  411.8 4.1 collective-permute-done.29
  415.9 4.5 multiply_reduce_fusion
  425.1 4.1 fusion.49.g_ref
  429.2 20.0 %shard_map.255 = (f32[256,1536]{1,0:T(8,128)S(1)}, bf16[2,1024,256]{2,1,0:T(8,128)(2,1)S(1)}) custom-call(bf16[256,1536]{1,0:T(8,128)(2,1)S(1)} %copy-done.6, bf16[256,1536]{1,0:T(8,128)(2,1)S(1)} %fusion.49.g_ref, bf16[1024,512]{1,0:T(8,128)(2,1)S(1)} %bitcast.328, bf16[1024,512]{1,0:T(8,128)(2,1)S(1)} %bitcast.329, f32[1024,256]{1,0:T(8,128)S(1)} %copy-done.2), custom_call_target="tpu_custom_call" | custom-call | flops 20000000000 | bytes 1000000 | tf_op jit(solution)/shard_map/pallas_call | solution.py:106
  462.8 13.0 %convolution_convert_fusion.2 = bf16[1536,1152]{1,0:T(8,128)(2,1)} fusion(bf16[512,1152]{1,0:T(8,128)(2,1)} %copy-done.127, bf16[512,1152]{1,0:T(8,128)(2,1)} %copy-done.126, bf16[512,1152]{1,0:T(8,128)(2,1)} %copy-done.125, bf16[512,1152]{1,0:T(8,128)(2,1)} %copy-done.124, pred[]{:T(512)} %bitcast.100, bf16[512,1536]{1,0:T(8,128)(2,1)} %bitcast.390, ...), kind=kOutput, calls=%fused_computation.7 | convolution fusion | flops 7295926272 | bytes 14548993 | tf_op jit(solution)/shard_map/td,tf->df/dot_general | solution.py:417
  493.0 4.0 collective-permute-done.33
  497.0 6.1 collective-permute-done.34
  503.1 4.6 collective-permute-done.35
  521.0 4.9 fusion.112
  525.9 3.0 fusion.85
  530.4 3.2 convolution_convert_fusion
  533.6 2.9 fusion.5
  540.8 11.4 %fusion.7 = bf16[1152,1536]{1,0:T(8,128)(2,1)S(1)} fusion(bf16[512,1536]{1,0:T(8,128)(2,1)} %copy-done.64, bf16[512,1536]{1,0:T(8,128)(2,1)} %copy-done.67, bf16[512,1536]{1,0:T(8,128)(2,1)} %copy-done.66, bf16[512,1536]{1,0:T(8,128)(2,1)} %copy-done.65, bf16[512,1152]{1,0:T(8,128)(2,1)} %copy-done.128, bf16[512,1152]{1,0:T(8,128)(2,1)} %copy-done.111, ...), kind=kOutput, calls=%fused_computation.17 | convolution fusion | flops 7294156800 | bytes 14548993 | tf_op jit(solution)/shard_map/tf,td->fd/dot_general | solution.py:456
  569.4 6.2 all-to-all-start.1
  578.6 3.6 collective-permute-done.36
  582.1 3.1 add_convert_fusion
  587.1 5.9 collective-permute-done.43
  606.2 13.5 %all-to-all-done.1 = bf16[8,2,48,1152]{3,2,1,0:T(8,128)(2,1)} async-done(((bf16[8,2,48,1152]{3,2,1,0:T(8,128)(2,1)}), bf16[8,2,48,1152]{3,2,1,0:T(8,128)(2,1)}, u32[]{:S(2)}, u32[]{:S(2)}) %all-to-all-start.1) | async-done | bytes 1769504 | tf_op jit(solution)/shard_map/all_to_all | solution.py:463
  622.2 7.6 %collective-permute-done.38 = bf16[4,2,48,1024]{3,2,0,1:T(8,128)(2,1)} collective-permute-done((bf16[4,2,48,1024]{3,2,0,1:T(8,128)(2,1)}, bf16[4,2,48,1024]{3,2,0,1:T(8,128)(2,1)}, u32[]{:S(2)}, u32[]{:S(2)}) %collective-permute-start.38) | collective-permute-done | bytes 786464 | tf_op jit(solution)/shard_map/ppermute | solution.py:157
  636.2 4.3 collective-permute-done.39
  640.6 4.3 collective-permute-done.41
  648.3 7.5 %collective-permute-done.47 = bf16[48,3712]{1,0:T(8,128)(2,1)S(1)} collective-permute-done((bf16[48,3712]{1,0:T(8,128)(2,1)S(1)}, bf16[48,3712]{1,0:T(8,128)(2,1)S(1)}, u32[]{:S(2)}, u32[]{:S(2)}) %collective-permute-start.47) | collective-permute-done | bytes 356384 | tf_op jit(solution)/shard_map/ppermute | solution.py:157
  658.1 3.0 fusion.82
  674.2 3.2 collective-permute-done.49
  (605 shorter events, 298.3 us)
Async XLA Ops:
  7.2 223.6 %all-gather.5.cloned.1.call-start = ((), (), s32[]{:S(2)}) async-start(), calls=%async_computation.6 | async-start | bytes 7077888 | tf_op jit(solution)/shard_map/all_gather | solution.py:270
  12.1 13.5 %collective-permute-start.2 = (bf16[48,3712]{1,0:T(8,128)(2,1)S(1)}, bf16[48,3712]{1,0:T(8,128)(2,1)}, u32[]{:S(2)}, u32[]{:S(2)}) collective-permute-start(bf16[48,3712]{1,0:T(8,128)(2,1)S(1)} %pad_dynamic-update-slice_fusion), channel_id=1, source_target_pairs={{0,8},{4,12},{8,16},{12,20},{16,24},{20,28},{24,0},{28,4},{1,9},{5... | collective-permute-start | bytes 1069064 | tf_op jit(solution)/shard_map/ppermute | solution.py:157
  17.2 11.6 %collective-permute-start = (bf16[280,768]{1,0:T(8,128)(2,1)}, bf16[280,768]{1,0:T(8,128)(2,1)S(1)}, u32[]{:S(2)}, u32[]{:S(2)}) collective-permute-start(bf16[280,768]{1,0:T(8,128)(2,1)} %get-tuple-element.107), channel_id=1, source_target_pairs={{0,2},{1,3},{2,0},{3,1},{4,6},{5,7},{6,4},{7,5},{8,10},{9,11},{10,... | collective-permute-start | bytes 1290248 | tf_op jit(solution)/shard_map/ppermute | solution.py:157
  18.8 11.4 %collective-permute-start.1 = (bf16[280,768]{1,0:T(8,128)(2,1)}, bf16[280,768]{1,0:T(8,128)(2,1)}, u32[]{:S(2)}, u32[]{:S(2)}) collective-permute-start(bf16[280,768]{1,0:T(8,128)(2,1)} %get-tuple-element.108), channel_id=1, source_target_pairs={{0,1},{1,0},{2,3},{3,2},{4,5},{5,4},{6,7},{7,6},{8,9},{9,8},{10,11... | collective-permute-start | bytes 1290248 | tf_op jit(solution)/shard_map/ppermute | solution.py:157
  25.6 11.5 %collective-permute-start.3 = (bf16[48,3712]{1,0:T(8,128)(2,1)}, bf16[48,3712]{1,0:T(8,128)(2,1)S(1)}, u32[]{:S(2)}, u32[]{:S(2)}) collective-permute-start(bf16[48,3712]{1,0:T(8,128)(2,1)} %collective-permute-done.2), channel_id=1, source_target_pairs={{0,8},{4,12},{8,16},{12,20},{16,24},{20,28},{24,0},{28,4},{1,9},{5... | collective-permute-start | bytes 1069064 | tf_op jit(solution)/shard_map/ppermute | solution.py:157
  37.1 10.4 %collective-permute-start.4 = (bf16[48,3712]{1,0:T(8,128)(2,1)S(1)}, bf16[48,3712]{1,0:T(8,128)(2,1)S(1)}, u32[]{:S(2)}, u32[]{:S(2)}) collective-permute-start(bf16[48,3712]{1,0:T(8,128)(2,1)S(1)} %collective-permute-done.3), channel_id=1, source_target_pairs={{0,8},{4,12},{8,16},{12,20},{16,24},{20,28},{24,0},{28,4},{1,9},{5... | collective-permute-start | bytes 1069064 | tf_op jit(solution)/shard_map/ppermute | solution.py:157
  47.8 14.8 %collective-permute-start.5 = (bf16[4,48,1792]{2,1,0:T(8,128)(2,1)S(1)}, bf16[4,48,1792]{2,1,0:T(8,128)(2,1)S(1)}, u32[]{:S(2)}, u32[]{:S(2)}) collective-permute-start(bf16[4,48,1792]{2,1,0:T(8,128)(2,1)S(1)} %slice.380), channel_id=1, source_target_pairs={{0,1},{1,0},{2,3},{3,2},{4,5},{5,4},{6,7},{7,6},{8,9},{9,8},{10,11... | collective-permute-start | bytes 2064392 | tf_op jit(solution)/shard_map/ppermute | solution.py:157
  48.9 15.6 %collective-permute-start.6 = (bf16[4,48,1920]{2,1,0:T(8,128)(2,1)S(1)}, bf16[4,48,1920]{2,1,0:T(8,128)(2,1)S(1)}, u32[]{:S(2)}, u32[]{:S(2)}) collective-permute-start(bf16[4,48,1920]{2,1,0:T(8,128)(2,1)S(1)} %slice.382), channel_id=1, source_target_pairs={{0,2},{1,3},{2,0},{3,1},{4,6},{5,7},{6,4},{7,5},{8,10},{9,11},{10,... | collective-permute-start | bytes 2211848 | tf_op jit(solution)/shard_map/ppermute | solution.py:157
  66.0 35.9 %collective-permute-start.7 = (bf16[4,2,48,1920]{3,2,1,0:T(8,128)(2,1)}, bf16[4,2,48,1920]{3,2,1,0:T(8,128)(2,1)}, u32[]{:S(2)}, u32[]{:S(2)}) collective-permute-start(bf16[4,2,48,1920]{3,2,1,0:T(8,128)(2,1)} %maximum_select_fusion.9), channel_id=1, source_target_pairs={{0,1},{1,0},{2,3},{3,2},{4,5},{5,4},{6,7},{7,6},{8,9},{9,8},{10,11... | collective-permute-start | bytes 4423688 | tf_op jit(solution)/shard_map/ppermute | solution.py:157
  70.1 28.4 %collective-permute-start.8 = (bf16[4,2,48,1792]{3,2,0,1:T(8,128)(2,1)}, bf16[4,2,48,1792]{3,2,0,1:T(8,128)(2,1)}, u32[]{:S(2)}, u32[]{:S(2)}) collective-permute-start(bf16[4,2,48,1792]{3,2,0,1:T(8,128)(2,1)} %maximum_select_fusion.11), channel_id=1, source_target_pairs={{0,2},{1,3},{2,0},{3,1},{4,6},{5,7},{6,4},{7,5},{8,10},{9,11},{10,... | collective-permute-start | bytes 4128776 | tf_op jit(solution)/shard_map/ppermute | solution.py:157
  107.5 21.1 %collective-permute-start.10 = (bf16[4,2,2,48,1792]{4,3,0,2,1:T(8,128)(2,1)}, bf16[4,2,2,48,1792]{4,3,0,2,1:T(8,128)(2,1)}, u32[]{:S(2)}, u32[]{:S(2)}) collective-permute-start(bf16[4,2,2,48,1792]{4,3,0,2,1:T(8,128)(2,1)} %fusion.47), channel_id=1, source_target_pairs={{0,4},{4,0},{8,12},{12,8},{16,20},{20,16},{24,28},{28,24},{1,5},{5... | collective-permute-start | bytes 8257544 | tf_op jit(solution)/shard_map/ppermute | solution.py:157
  109.9 29.7 %collective-permute-start.9 = (bf16[4,2,2,48,1920]{4,3,2,1,0:T(8,128)(2,1)}, bf16[4,2,2,48,1920]{4,3,2,1,0:T(8,128)(2,1)}, u32[]{:S(2)}, u32[]{:S(2)}) collective-permute-start(bf16[4,2,2,48,1920]{4,3,2,1,0:T(8,128)(2,1)} %fusion.44), channel_id=1, source_target_pairs={{0,4},{4,0},{8,12},{12,8},{16,20},{20,16},{24,28},{28,24},{1,5},{5... | collective-permute-start | bytes 8847368 | tf_op jit(solution)/shard_map/ppermute | solution.py:157
  123.7 47.1 %all-to-all-start = ((bf16[8,2,48,1152]{3,2,1,0:T(8,128)(2,1)}), bf16[8,2,48,1152]{3,2,1,0:T(8,128)(2,1)}, u32[]{:S(2)}, u32[]{:S(2)}) async-start(bf16[8,2,48,1152]{3,2,1,0:T(8,128)(2,1)} %copy.167), calls=%async_computation | async-start | bytes 3538944 | tf_op jit(solution)/shard_map/all_to_all | solution.py:278
  128.1 131.0 %all-gather.3.cloned.1.call-start = ((), (), s32[]{:S(2)}) async-start(), calls=%async_computation.5 | async-start | bytes 8847360 | tf_op jit(solution)/shard_map/all_gather | solution.py:348
  136.7 21.6 %collective-permute-start.11 = (bf16[2,280,768]{2,1,0:T(8,128)(2,1)}, bf16[2,280,768]{2,1,0:T(8,128)(2,1)}, u32[]{:S(2)}, u32[]{:S(2)}) collective-permute-start(bf16[2,280,768]{2,1,0:T(8,128)(2,1)} %maximum_select_fusion.13), channel_id=1, source_target_pairs={{0,1},{1,0},{2,3},{3,2},{4,5},{5,4},{6,7},{7,6},{8,9},{9,8},{10,11... | collective-permute-start | bytes 2580488 | tf_op jit(solution)/shard_map/ppermute | solution.py:157
  138.9 23.7 %collective-permute-start.12 = (bf16[2,280,768]{2,1,0:T(8,128)(2,1)}, bf16[2,280,768]{2,1,0:T(8,128)(2,1)}, u32[]{:S(2)}, u32[]{:S(2)}) collective-permute-start(bf16[2,280,768]{2,1,0:T(8,128)(2,1)} %maximum_select_fusion.14), channel_id=1, source_target_pairs={{0,2},{1,3},{2,0},{3,1},{4,6},{5,7},{6,4},{7,5},{8,10},{9,11},{10,... | collective-permute-start | bytes 2580488 | tf_op jit(solution)/shard_map/ppermute | solution.py:157
  174.5 390.6 %reduce-scatter.6.cloned.1.call-start = ((), (), s32[]{:S(2)}) async-start(), calls=%async_computation.7 | async-start | bytes 4423680 | tf_op jit(solution)/shard_map/reduce_scatter | solution.py:423
  179.5 13.3 %collective-permute-start.13 = (bf16[256,512]{0,1:T(8,128)(2,1)}, bf16[256,512]{0,1:T(8,128)(2,1)}, u32[]{:S(2)}, u32[]{:S(2)}) collective-permute-start(bf16[256,512]{0,1:T(8,128)(2,1)} %fusion.149), channel_id=1, source_target_pairs={{0,1},{1,2},{2,3},{3,0},{4,5},{5,6},{6,7},{7,4},{8,9},{9,10},{10,1... | collective-permute-start | bytes 786440 | tf_op jit(solution)/shard_map/ppermute | solution.py:342
  180.8 19.0 %collective-permute-start.14 = (bf16[256,512]{0,1:T(8,128)(2,1)}, bf16[256,512]{0,1:T(8,128)(2,1)S(1)}, u32[]{:S(2)}, u32[]{:S(2)}) collective-permute-start(bf16[256,512]{0,1:T(8,128)(2,1)} %fusion.149), channel_id=1, source_target_pairs={{0,2},{1,3},{2,0},{3,1},{4,6},{5,7},{6,4},{7,5},{8,10},{9,11},{10,... | collective-permute-start | bytes 786440 | tf_op jit(solution)/shard_map/ppermute | solution.py:342
  182.2 21.3 %collective-permute-start.15 = (bf16[256,512]{0,1:T(8,128)(2,1)}, bf16[256,512]{0,1:T(8,128)(2,1)}, u32[]{:S(2)}, u32[]{:S(2)}) collective-permute-start(bf16[256,512]{0,1:T(8,128)(2,1)} %fusion.149), channel_id=1, source_target_pairs={{0,3},{1,0},{2,1},{3,2},{4,7},{5,4},{6,5},{7,6},{8,11},{9,8},{10,9... | collective-permute-start | bytes 786440 | tf_op jit(solution)/shard_map/ppermute | solution.py:342
  226.7 43.3 %collective-permute-start.17 = (bf16[256,1536]{1,0:T(8,128)(2,1)}, bf16[256,1536]{1,0:T(8,128)(2,1)}, u32[]{:S(2)}, u32[]{:S(2)}) collective-permute-start(bf16[256,1536]{1,0:T(8,128)(2,1)} %fusion.48), channel_id=1, source_target_pairs={{0,8},{4,12},{8,16},{12,20},{16,24},{20,28},{24,0},{28,4},{1,9},{5... | collective-permute-start | bytes 2359304 | tf_op jit(solution)/shard_map/ppermute | solution.py:157
  271.3 10.8 %collective-permute-start.18 = (bf16[256,1536]{1,0:T(8,128)(2,1)S(1)}, bf16[256,1536]{1,0:T(8,128)(2,1)S(1)}, u32[]{:S(2)}, u32[]{:S(2)}) collective-permute-start(bf16[256,1536]{1,0:T(8,128)(2,1)S(1)} %get-tuple-element.111), channel_id=1, source_target_pairs={{0,4},{4,0},{8,12},{12,8},{16,20},{20,16},{24,28},{28,24},{1,5},{5... | collective-permute-start | bytes 2359304 | tf_op jit(solution)/shard_map/ppermute | solution.py:157
  271.4 22.1 %collective-permute-start.19 = (bf16[256,1536]{1,0:T(8,128)(2,1)S(1)}, bf16[256,1536]{1,0:T(8,128)(2,1)S(1)}, u32[]{:S(2)}, u32[]{:S(2)}) collective-permute-start(bf16[256,1536]{1,0:T(8,128)(2,1)S(1)} %get-tuple-element.112), channel_id=1, source_target_pairs={{0,8},{4,12},{8,16},{12,20},{16,24},{20,28},{24,0},{28,4},{1,9},{5... | collective-permute-start | bytes 2359304 | tf_op jit(solution)/shard_map/ppermute | solution.py:157
  298.2 22.2 %collective-permute-start.24 = (bf16[256,1536]{1,0:T(8,128)(2,1)S(1)}, bf16[256,1536]{1,0:T(8,128)(2,1)S(1)}, u32[]{:S(2)}, u32[]{:S(2)}) collective-permute-start(bf16[256,1536]{1,0:T(8,128)(2,1)S(1)} %dynamic-slice_convert_fusion.3), channel_id=1, source_target_pairs={{0,4},{4,0},{8,12},{12,8},{16,20},{20,16},{24,28},{28,24},{1,5},{5... | collective-permute-start | bytes 2359304 | tf_op jit(solution)/shard_map/ppermute | solution.py:157
  298.8 21.5 %collective-permute-start.21 = (bf16[256,1536]{1,0:T(8,128)(2,1)S(1)}, bf16[256,1536]{1,0:T(8,128)(2,1)S(1)}, u32[]{:S(2)}, u32[]{:S(2)}) collective-permute-start(bf16[256,1536]{1,0:T(8,128)(2,1)S(1)} %collective-permute-done.19), channel_id=1, source_target_pairs={{0,8},{4,12},{8,16},{12,20},{16,24},{20,28},{24,0},{28,4},{1,9},{5... | collective-permute-start | bytes 2359304 | tf_op jit(solution)/shard_map/ppermute | solution.py:157
  320.7 21.8 %collective-permute-start.25 = (bf16[256,1536]{1,0:T(8,128)(2,1)S(1)}, bf16[256,1536]{1,0:T(8,128)(2,1)S(1)}, u32[]{:S(2)}, u32[]{:S(2)}) collective-permute-start(bf16[256,1536]{1,0:T(8,128)(2,1)S(1)} %add_convert_fusion.3), channel_id=1, source_target_pairs={{0,8},{4,12},{8,16},{12,20},{16,24},{20,28},{24,0},{28,4},{1,9},{5... | collective-permute-start | bytes 2359304 | tf_op jit(solution)/shard_map/ppermute | solution.py:157
  352.3 22.0 %collective-permute-start.27 = (bf16[256,1536]{1,0:T(8,128)(2,1)S(1)}, bf16[256,1536]{1,0:T(8,128)(2,1)S(1)}, u32[]{:S(2)}, u32[]{:S(2)}) collective-permute-start(bf16[256,1536]{1,0:T(8,128)(2,1)S(1)} %add_convert_fusion.2), channel_id=1, source_target_pairs={{0,8},{4,12},{8,16},{12,20},{16,24},{20,28},{24,0},{28,4},{1,9},{5... | collective-permute-start | bytes 2359304 | tf_op jit(solution)/shard_map/ppermute | solution.py:157
  384.5 23.9 %collective-permute-start.23 = (bf16[4,256,1536]{2,1,0:T(8,128)(2,1)}, bf16[4,256,1536]{2,1,0:T(8,128)(2,1)}, u32[]{:S(2)}, u32[]{:S(2)}) collective-permute-start(bf16[4,256,1536]{2,1,0:T(8,128)(2,1)} %pad_maximum_fusion.3), channel_id=1, source_target_pairs={{0,4},{4,0},{8,12},{12,8},{16,20},{20,16},{24,28},{28,24},{1,5},{5... | collective-permute-start | bytes 9437192 | tf_op jit(solution)/shard_map/ppermute | solution.py:157
  389.0 22.8 %collective-permute-start.30 = (bf16[256,1536]{1,0:T(8,128)(2,1)}, bf16[256,1536]{1,0:T(8,128)(2,1)}, u32[]{:S(2)}, u32[]{:S(2)}) collective-permute-start(bf16[256,1536]{1,0:T(8,128)(2,1)} %dynamic-slice_convert_fusion), channel_id=1, source_target_pairs={{0,4},{4,0},{8,12},{12,8},{16,20},{20,16},{24,28},{28,24},{1,5},{5... | collective-permute-start | bytes 2359304 | tf_op jit(solution)/shard_map/ppermute | solution.py:157
  393.3 22.6 %collective-permute-start.29 = (bf16[256,1536]{1,0:T(8,128)(2,1)}, bf16[256,1536]{1,0:T(8,128)(2,1)}, u32[]{:S(2)}, u32[]{:S(2)}) collective-permute-start(bf16[256,1536]{1,0:T(8,128)(2,1)} %get-tuple-element.38), channel_id=1, source_target_pairs={{0,8},{4,12},{8,16},{12,20},{16,24},{20,28},{24,0},{28,4},{1,9},{5... | collective-permute-start | bytes 2359304 | tf_op jit(solution)/shard_map/ppermute | solution.py:157
  406.9 159.5 %reduce-scatter.8.cloned.1.call-start = ((), (), s32[]{:S(2)}) async-start(), calls=%async_computation.8 | async-start | bytes 4423680 | tf_op jit(solution)/shard_map/reduce_scatter | solution.py:423
  424.9 32.3 %collective-permute-start.31 = (bf16[256,1536]{1,0:T(8,128)(2,1)}, bf16[256,1536]{1,0:T(8,128)(2,1)}, u32[]{:S(2)}, u32[]{:S(2)}) collective-permute-start(bf16[256,1536]{1,0:T(8,128)(2,1)} %select_convert_fusion), channel_id=1, source_target_pairs={{0,8},{4,12},{8,16},{12,20},{16,24},{20,28},{24,0},{28,4},{1,9},{5... | collective-permute-start | bytes 2359304 | tf_op jit(solution)/shard_map/ppermute | solution.py:157
  457.2 102.3 %collective-permute-start.42 = (bf16[4,2,2,48,1536]{4,3,0,2,1:T(8,128)(2,1)}, bf16[4,2,2,48,1536]{4,3,0,2,1:T(8,128)(2,1)}, u32[]{:S(2)}, u32[]{:S(2)}) collective-permute-start(bf16[4,2,2,48,1536]{4,3,0,2,1:T(8,128)(2,1)} %bitcast.322), channel_id=1, source_target_pairs={{0,4},{4,0},{8,12},{12,8},{16,20},{20,16},{24,28},{28,24},{1,5},{5... | collective-permute-start | bytes 7077896 | tf_op jit(solution)/shard_map/ppermute | solution.py:157
  475.8 185.3 %reduce-scatter.10.cloned.1.call-start = ((), (), s32[]{:S(2)}) async-start(), calls=%async_computation.9 | async-start | bytes 4300800
  481.1 16.0 %collective-permute-start.33 = (bf16[2,256,256]{1,2,0:T(8,128)(2,1)}, bf16[2,256,256]{1,2,0:T(8,128)(2,1)}, u32[]{:S(2)}, u32[]{:S(2)}) collective-permute-start(bf16[2,256,256]{1,2,0:T(8,128)(2,1)} %bitcast.399), channel_id=1, source_target_pairs={{0,1},{1,2},{2,3},{3,0},{4,5},{5,6},{6,7},{7,4},{8,9},{9,10},{10,1... | collective-permute-start | bytes 786440 | tf_op jit(solution)/shard_map/ppermute | solution.py:186
  484.4 18.7 %collective-permute-start.34 = (bf16[2,256,256]{1,2,0:T(8,128)(2,1)}, bf16[2,256,256]{1,2,0:T(8,128)(2,1)}, u32[]{:S(2)}, u32[]{:S(2)}) collective-permute-start(bf16[2,256,256]{1,2,0:T(8,128)(2,1)} %bitcast.400), channel_id=1, source_target_pairs={{0,2},{1,3},{2,0},{3,1},{4,6},{5,7},{6,4},{7,5},{8,10},{9,11},{10,... | collective-permute-start | bytes 786440 | tf_op jit(solution)/shard_map/ppermute | solution.py:186
  486.7 21.0 %collective-permute-start.35 = (bf16[2,256,256]{1,2,0:T(8,128)(2,1)}, bf16[2,256,256]{1,2,0:T(8,128)(2,1)}, u32[]{:S(2)}, u32[]{:S(2)}) collective-permute-start(bf16[2,256,256]{1,2,0:T(8,128)(2,1)} %bitcast.401), channel_id=1, source_target_pairs={{0,3},{1,0},{2,1},{3,2},{4,7},{5,4},{6,5},{7,6},{8,11},{9,8},{10,9... | collective-permute-start | bytes 786440 | tf_op jit(solution)/shard_map/ppermute | solution.py:186
  493.0 25.1 %collective-permute-start.32 = (bf16[256,1536]{1,0:T(8,128)(2,1)}, bf16[256,1536]{1,0:T(8,128)(2,1)}, u32[]{:S(2)}, u32[]{:S(2)}) collective-permute-start(bf16[256,1536]{1,0:T(8,128)(2,1)} %fusion.119), channel_id=1, source_target_pairs={{0,8},{4,12},{8,16},{12,20},{16,24},{20,28},{24,0},{28,4},{1,9},{5... | collective-permute-start | bytes 2359304 | tf_op jit(solution)/shard_map/ppermute | solution.py:157
  540.8 54.4 %collective-permute-start.37 = (bf16[4,2,2,48,2176]{4,3,0,2,1:T(8,128)(2,1)}, bf16[4,2,2,48,2176]{4,3,0,2,1:T(8,128)(2,1)}, u32[]{:S(2)}, u32[]{:S(2)}) collective-permute-start(bf16[4,2,2,48,2176]{4,3,0,2,1:T(8,128)(2,1)} %bitcast.321), channel_id=1, source_target_pairs={{0,4},{4,0},{8,12},{12,8},{16,20},{20,16},{24,28},{28,24},{1,5},{5... | collective-permute-start | bytes 10027016 | tf_op jit(solution)/shard_map/ppermute | solution.py:157
  559.5 22.6 %collective-permute-start.36 = (bf16[256,1536]{1,0:T(8,128)(2,1)}, bf16[256,1536]{1,0:T(8,128)(2,1)}, u32[]{:S(2)}, u32[]{:S(2)}) collective-permute-start(bf16[256,1536]{1,0:T(8,128)(2,1)} %fusion.120), channel_id=1, source_target_pairs={{0,8},{4,12},{8,16},{12,20},{16,24},{20,28},{24,0},{28,4},{1,9},{5... | collective-permute-start | bytes 2359304 | tf_op jit(solution)/shard_map/ppermute | solution.py:157
  564.1 28.8 %collective-permute-start.43 = (bf16[4,2,48,768]{3,2,0,1:T(8,128)(2,1)S(1)}, bf16[4,2,48,768]{3,2,0,1:T(8,128)(2,1)}, u32[]{:S(2)}, u32[]{:S(2)}) collective-permute-start(bf16[4,2,48,768]{3,2,0,1:T(8,128)(2,1)S(1)} %dynamic-slice_bitcast_fusion.7), channel_id=1, source_target_pairs={{0,1},{1,0},{2,3},{3,2},{4,5},{5,4},{6,7},{7,6},{8,9},{9,8},{10,11... | collective-permute-start | bytes 1769480 | tf_op jit(solution)/shard_map/ppermute | solution.py:157
  569.4 50.3 %all-to-all-start.1 = ((bf16[8,2,48,1152]{3,2,1,0:T(8,128)(2,1)}), bf16[8,2,48,1152]{3,2,1,0:T(8,128)(2,1)}, u32[]{:S(2)}, u32[]{:S(2)}) async-start(bf16[8,2,48,1152]{3,2,1,0:T(8,128)(2,1)} %copy.182), calls=%async_computation.3 | async-start | bytes 3538944 | tf_op jit(solution)/shard_map/all_to_all | solution.py:463
  576.8 26.5 %collective-permute-start.45 = (bf16[4,2,48,768]{3,2,0,1:T(8,128)(2,1)S(1)}, bf16[4,2,48,768]{3,2,0,1:T(8,128)(2,1)S(1)}, u32[]{:S(2)}, u32[]{:S(2)}) collective-permute-start(bf16[4,2,48,768]{3,2,0,1:T(8,128)(2,1)S(1)} %dynamic-slice_bitcast_fusion.6), channel_id=1, source_target_pairs={{0,2},{1,3},{2,0},{3,1},{4,6},{5,7},{6,4},{7,5},{8,10},{9,11},{10,... | collective-permute-start | bytes 1769480 | tf_op jit(solution)/shard_map/ppermute | solution.py:157
  594.2 11.2 %collective-permute-start.44 = (bf16[4,48,768]{2,1,0:T(8,128)(2,1)S(1)}, bf16[4,48,768]{2,1,0:T(8,128)(2,1)S(1)}, u32[]{:S(2)}, u32[]{:S(2)}) collective-permute-start(bf16[4,48,768]{2,1,0:T(8,128)(2,1)S(1)} %dynamic-slice_bitcast_fusion.12), channel_id=1, source_target_pairs={{0,2},{1,3},{2,0},{3,1},{4,6},{5,7},{6,4},{7,5},{8,10},{9,11},{10,... | collective-permute-start | bytes 884744 | tf_op jit(solution)/shard_map/ppermute | solution.py:157
  600.3 29.4 %collective-permute-start.38 = (bf16[4,2,48,1024]{3,2,0,1:T(8,128)(2,1)}, bf16[4,2,48,1024]{3,2,0,1:T(8,128)(2,1)}, u32[]{:S(2)}, u32[]{:S(2)}) collective-permute-start(bf16[4,2,48,1024]{3,2,0,1:T(8,128)(2,1)} %dynamic-slice_bitcast_fusion.1), channel_id=1, source_target_pairs={{0,1},{1,0},{2,3},{3,2},{4,5},{5,4},{6,7},{7,6},{8,9},{9,8},{10,11... | collective-permute-start | bytes 2359304 | tf_op jit(solution)/shard_map/ppermute | solution.py:157
  602.8 30.2 %collective-permute-start.40 = (bf16[4,2,48,1152]{3,2,0,1:T(8,128)(2,1)}, bf16[4,2,48,1152]{3,2,0,1:T(8,128)(2,1)}, u32[]{:S(2)}, u32[]{:S(2)}) collective-permute-start(bf16[4,2,48,1152]{3,2,0,1:T(8,128)(2,1)} %dynamic-slice_bitcast_fusion), channel_id=1, source_target_pairs={{0,2},{1,3},{2,0},{3,1},{4,6},{5,7},{6,4},{7,5},{8,10},{9,11},{10,... | collective-permute-start | bytes 2654216 | tf_op jit(solution)/shard_map/ppermute | solution.py:157
  604.2 30.9 %collective-permute-start.46 = (bf16[4,48,768]{2,1,0:T(8,128)(2,1)}, bf16[4,48,768]{2,1,0:T(8,128)(2,1)}, u32[]{:S(2)}, u32[]{:S(2)}) collective-permute-start(bf16[4,48,768]{2,1,0:T(8,128)(2,1)} %dynamic-slice_bitcast_fusion.11), channel_id=1, source_target_pairs={{0,1},{1,0},{2,3},{3,2},{4,5},{5,4},{6,7},{7,6},{8,9},{9,8},{10,11... | collective-permute-start | bytes 884744 | tf_op jit(solution)/shard_map/ppermute | solution.py:157
  634.5 10.3 %collective-permute-start.41 = (bf16[4,48,1152]{2,1,0:T(8,128)(2,1)S(1)}, bf16[4,48,1152]{2,1,0:T(8,128)(2,1)S(1)}, u32[]{:S(2)}, u32[]{:S(2)}) collective-permute-start(bf16[4,48,1152]{2,1,0:T(8,128)(2,1)S(1)} %dynamic-slice_bitcast_fusion.8), channel_id=1, source_target_pairs={{0,1},{1,0},{2,3},{3,2},{4,5},{5,4},{6,7},{7,6},{8,9},{9,8},{10,11... | collective-permute-start | bytes 1327112 | tf_op jit(solution)/shard_map/ppermute | solution.py:157
  (138 other events, 1154.5 us)
Sparse Core Ops, SparseCore 0:
  72.4 62.8 all-gather.4
  174.6 84.5 all-gather.2
  407.0 47.6 reduce-scatter.5
  475.9 58.7 reduce-scatter.7
  554.3 68.9 reduce-scatter.9
